TPU v7x, 32 devices: a whole 2x2x4 slice. The times are simulated.
32 devices in a mesh: groups: 2 (over y), ctx: 4 (over z), tm: 2 (over x), tp: 2 (over core).
Axes of the slice: x: 2, y: 2, z: 4, core: 2. Of those that a mesh axis runs over, the one named last changes fastest.
Arguments:
- tokens: bfloat16 [256, 8, 1024], P(('groups', 'tm'), 'ctx'), parts along dimension 0, may hold values from -6 to 6
- norm_gain: float32 [1024], replicated, may hold values from 0.1 to 1.9
- block_mask: int32 [4, 4, 4], P(('groups', 'tm'), 'ctx'), parts along dimension 0, may hold values from 0 to 1, as said below
- w_query: bfloat16 [1024, 1024], P('tm', 'tp'), may hold values from -1.25 to 1.25
- w_key: bfloat16 [1024, 1024], P('tm', 'tp'), may hold values from -1.25 to 1.25
- w_value: bfloat16 [1024, 1024], P('tm', 'tp'), may hold values from -0.1875 to 0.1875
- w_out: bfloat16 [1024, 1024], P('tp', 'tm'), may hold values from -0.1875 to 0.1875
- w_up: bfloat16 [1024, 2048], P('tm', 'tp'), may hold values from -0.1875 to 0.1875
- w_down: bfloat16 [2048, 1024], P('tp', 'tm'), may hold values from -0.125 to 0.125
- conv_weight: float32 [5, 1024], P(None, 'tp'), may hold values from -2.5 to 2.5
Outputs:
- denoised: bfloat16 [256, 8, 1024], P(('groups', 'tm'), 'ctx', 'tp'), parts along dimension 0
There are 2 independent parts, one for each index of `groups`. A program takes and returns all parts, laid end to end along the dimension named above; an argument that names none is the same for every part. Nothing has to cross between parts.
Inputs may be any that keep to these rules, and one draw needn't show every extreme that they name: block_mask[w, i, i] is 1 for every window w and block i.
All inputs are finite; a program needn't handle non-finite values.
Results may differ from a plain program's by a relative error of at most 0.0076.
Values may be sent and summed in bfloat16 or wider, within the bound.
No kernel may reach another device: no remote copies, remote signals or barrier semaphores. Data moves between devices by JAX's collectives and lax.ppermute only.
A program may use at most 64 MiB of HBM per device.

v0:
```python
import jax
import jax.numpy as jnp
from jax import lax
from jax.sharding import PartitionSpec as P

HEAD_DIM = 64
KERNEL = 5


def from_behind(value, axis, steps):
    count = lax.axis_size(axis)
    first, last = (max(0, -steps), min(count, count - steps))
    return lax.ppermute(value, axis, [(source, source + steps) for source in range(first, last)])


def rms_norm(tokens, norm_gain):
    values = tokens.astype(jnp.float32)
    square = jnp.mean(values * values, axis=-1, keepdims=True)
    return (values * lax.rsqrt(square + 1e-05) * norm_gain).astype(jnp.bfloat16)


def on_device(
    tokens, norm_gain, block_mask, w_query, w_key, w_value, w_out, w_up, w_down, conv_weight
):
    frames_here, dancers_here, width = tokens.shape
    rows_here = frames_here * dancers_here
    normed_grid = rms_norm(tokens, norm_gain)
    normed = normed_grid.reshape(rows_here, width)
    pieces = (
        lax.all_gather(w_query, "tm", axis=0, tiled=True),
        lax.all_gather(w_key, "tm", axis=0, tiled=True),
        lax.all_gather(w_value, "tm", axis=0, tiled=True),
        lax.all_gather(w_up, "tm", axis=0, tiled=True),
    )
    query_sum, key_sum, value_sum, hidden = tuple(
        (jnp.dot(normed, piece_one, preferred_element_type=jnp.float32) for piece_one in pieces)
    )
    local_heads = query_sum.shape[1] // HEAD_DIM
    queries = query_sum.astype(jnp.bfloat16).reshape(rows_here, local_heads, HEAD_DIM)
    key_grid = key_sum.astype(jnp.bfloat16).reshape(
        frames_here, dancers_here, local_heads * HEAD_DIM
    )
    value_grid = value_sum.astype(jnp.bfloat16).reshape(
        frames_here, dancers_here, local_heads * HEAD_DIM
    )
    mask_row = block_mask[0, 0].astype(jnp.float32)
    cycle_blocks = mask_row.shape[0]
    key_piece = lax.all_gather(key_grid, "ctx", axis=1, tiled=True)
    value_piece = lax.all_gather(value_grid, "ctx", axis=1, tiled=True)
    count = key_piece.shape[1]
    block_ids = jnp.arange(count) // dancers_here
    picker = (block_ids[:, None] == jnp.arange(cycle_blocks)[None, :]).astype(jnp.float32)
    allowed_dancers = jnp.dot(picker, mask_row)
    peak_old = jnp.full((local_heads, rows_here), -1e30, jnp.float32)
    key_rows = key_piece.reshape(frames_here * count, local_heads, HEAD_DIM)
    value_rows = value_piece.reshape(frames_here * count, local_heads, HEAD_DIM)
    allowed = jnp.tile(allowed_dancers, frames_here)
    scores = (
        jnp.einsum("qhd,khd->hqk", queries, key_rows, preferred_element_type=jnp.float32) * 0.125
    )
    scores = jnp.where(allowed[None, None, :] > 0, scores, -1e30)
    peak_new = jnp.maximum(peak_old, jnp.max(scores, axis=-1))
    expo = jnp.exp(scores - peak_new[:, :, None]) * allowed[None, None, :]
    total_new = jnp.sum(expo, axis=-1)
    probs = expo.astype(jnp.bfloat16)
    mixed_new = jnp.einsum("hqk,khd->hqd", probs, value_rows, preferred_element_type=jnp.float32)
    attended = (
        (mixed_new / total_new[:, :, None])
        .transpose(1, 0, 2)
        .reshape(rows_here, local_heads * HEAD_DIM)
        .astype(jnp.bfloat16)
    )
    activated = jax.nn.gelu(hidden, approximate=True).astype(jnp.bfloat16)
    out_full, down_full = (
        lax.all_gather(w_out, "tm", axis=1, tiled=True),
        lax.all_gather(w_down, "tm", axis=1, tiled=True),
    )
    branches = jnp.dot(attended, out_full, preferred_element_type=jnp.float32)
    branches = branches + jnp.dot(activated, down_full, preferred_element_type=jnp.float32)
    mine = lax.psum_scatter(
        branches.astype(jnp.bfloat16), "tp", scatter_dimension=1, tiled=True
    ).astype(jnp.float32)
    features_here = mine.shape[1]
    first_feature = lax.axis_index("tp") * features_here
    normed_cols = lax.dynamic_slice_in_dim(normed_grid, first_feature, features_here, 2)
    padded = jnp.pad(normed_cols.astype(jnp.float32), ((4, 4), (0, 0), (0, 0)))
    extended = jnp.zeros((frames_here + 4, dancers_here, features_here), jnp.float32)
    for offset in range(KERNEL):
        extended = extended + conv_weight[offset] * padded[offset : offset + frames_here + 4]
    convolved = extended[2 : frames_here + 2]
    from_before = from_behind(extended[frames_here + 2 :], "tm", 1)
    from_after = from_behind(extended[0:2], "tm", -1)
    convolved = convolved.at[0:2].add(from_before)
    convolved = convolved.at[frames_here - 2 :].add(from_after)
    token_cols = lax.dynamic_slice_in_dim(tokens, first_feature, features_here, 2).astype(
        jnp.float32
    )
    result = token_cols + mine.reshape(frames_here, dancers_here, features_here) + convolved
    return result.astype(jnp.bfloat16)


def solution(mesh):
    placed = (
        P(("groups", "tm"), "ctx", None),
        P(),
        P(("groups", "tm"), "ctx", None),
        P("tm", "tp"),
        P("tm", "tp"),
        P("tm", "tp"),
        P("tp", "tm"),
        P("tm", "tp"),
        P("tp", "tm"),
        P(None, "tp"),
    )
    return jax.shard_map(
        on_device,
        mesh=mesh,
        in_specs=placed,
        out_specs=P(("groups", "tm"), "ctx", "tp"),
        check_vma=False,
    )
```

profile of v0, /device:TPU:0, one launch (start us, length us, event | category | flops | bytes accessed | tf_op | source)
XLA Modules:
  0.0 189.5 jit_solution(12623946930418223822)
XLA Ops:
  6.5 0.7 all-gather.7.cloned.1.call-update
  7.3 0.7 all-gather.9.cloned.1.call-update
  8.1 0.7 all-gather.11.cloned.1.call-update
  12.0 1.0 fusion.26
  13.0 19.9 %all-gather.7.cloned.1.call-done = bf16[1024,512]{1,0:T(8,128)(2,1)} async-done(((bf16[512,512]{1,0:T(8,128)(2,1)}), bf16[1024,512]{1,0:T(8,128)(2,1)}) %all-gather.7.cloned.1.call-update) | async-done | bytes 1048592 | tf_op jit(solution)/shard_map/all_gather | solution.py:30
  32.9 1.5 convolution_convert_fusion.2
  34.6 21.2 %all-gather.9.cloned.1.call-done = bf16[1024,512]{1,0:T(8,128)(2,1)} async-done(((bf16[512,512]{1,0:T(8,128)(2,1)}), bf16[1024,512]{1,0:T(8,128)(2,1)}) %all-gather.9.cloned.1.call-update) | async-done | bytes 1048592 | tf_op jit(solution)/shard_map/all_gather | solution.py:31
  55.8 1.5 convolution_convert_fusion.1
  57.4 15.6 %all_gather.26 = bf16[64,8,512]{2,0,1:T(8,128)(2,1)S(1)} all-gather(bf16[64,2,512]{2,0,1:T(8,128)(2,1)S(1)} %copy.35), channel_id=1, replica_groups=mesh['groups'=2,'ctx'=4,'tm'=2,'tp'=2] {'ctx'}, dimensions={1}, use_global_device_ids=true | all-gather | bytes 655360 | tf_op jit(solution)/shard_map/all_gather | solution.py:48
  73.9 4.8 %all-gather.11.cloned.1.call-done = bf16[1024,512]{1,0:T(8,128)(2,1)} async-done(((bf16[512,512]{1,0:T(8,128)(2,1)}), bf16[1024,512]{1,0:T(8,128)(2,1)}) %all-gather.11.cloned.1.call-update) | async-done | bytes 1048592 | tf_op jit(solution)/shard_map/all_gather | solution.py:32
  78.7 1.5 convolution_convert_fusion
  81.0 15.6 %all_gather.28 = bf16[64,8,512]{2,0,1:T(8,128)(2,1)S(1)} all-gather(bf16[64,2,512]{2,0,1:T(8,128)(2,1)S(1)} %copy.38), channel_id=1, replica_groups=mesh['groups'=2,'ctx'=4,'tm'=2,'tp'=2] {'ctx'}, dimensions={1}, use_global_device_ids=true | all-gather | bytes 655360 | tf_op jit(solution)/shard_map/all_gather | solution.py:49
  96.9 1.5 reshape.132
  99.6 0.9 fusion.5
  100.5 12.8 %all-gather.17.cloned.1.call-done = bf16[1024,1024]{1,0:T(8,128)(2,1)} async-done(((bf16[1024,512]{1,0:T(8,128)(2,1)}), bf16[1024,1024]{1,0:T(8,128)(2,1)}) %all-gather.17.cloned.1.call-update) | async-done | bytes 2097168 | tf_op jit(solution)/shard_map/all_gather | solution.py:76
  113.3 34.5 %all-gather.15.cloned.1.call-done = bf16[1024,1024]{1,0:T(8,128)(2,1)} async-done(((bf16[512,1024]{1,0:T(8,128)(2,1)}), bf16[1024,1024]{1,0:T(8,128)(2,1)}) %all-gather.15.cloned.1.call-update) | async-done | bytes 2097168 | tf_op jit(solution)/shard_map/all_gather | solution.py:33
  147.8 3.1 %fusion.30 = f32[128,1024]{1,0:T(8,128)S(1)} fusion(bf16[1024,1024]{1,0:T(8,128)(2,1)} %all-gather.17.cloned.1.call-done, bf16[128,1024]{1,0:T(8,128)(2,1)S(1)} %reshape.127, bf16[1024,1024]{1,0:T(8,128)(2,1)} %all-gather.15.cloned.1.call-done), kind=kOutput, calls=%fused_computation.45 | convolution fusion | flops 538050560 | bytes 4980736 | tf_op jit(solution)/shard_map/dot_general | solution.py:79
  150.9 19.6 %all-gather.13.cloned.1.call-done = bf16[512,1024]{1,0:T(8,128)(2,1)} async-done(((bf16[512,512]{1,0:T(8,128)(2,1)}), bf16[512,1024]{1,0:T(8,128)(2,1)}) %all-gather.13.cloned.1.call-update) | async-done | bytes 1048592 | tf_op jit(solution)/shard_map/all_gather | solution.py:75
  170.6 2.3 %fusion.3 = bf16[128,1024]{1,0:T(8,128)(2,1)} fusion(f32[128,1024]{1,0:T(8,128)S(1)} %fusion.30, bf16[128,512]{0,1:T(8,128)(2,1)S(1)} %bitcast.34, bf16[512,1024]{1,0:T(8,128)(2,1)} %all-gather.13.cloned.1.call-done), kind=kOutput, calls=%fused_computation.6 | convolution fusion | flops 134479872 | bytes 1966080 | tf_op jit(solution)/shard_map/dot_general | solution.py:78
  172.9 2.2 %collective-permute-start = (f32[2,2,512]{2,1,0:T(2,128)S(1)}, f32[2,2,512]{2,1,0:T(2,128)S(1)}, u32[]{:S(2)}, u32[]{:S(2)}) collective-permute-start(f32[2,2,512]{2,1,0:T(2,128)S(1)} %get-tuple-element.30), channel_id=1, source_target_pairs={{0,2},{1,3},{4,6},{5,7},{8,10},{9,11},{12,14},{13,15},{16,18},{17,... | collective-permute-start | bytes 24584 | tf_op jit(solution)/shard_map/ppermute | solution.py:13
  175.1 1.3 collective-permute-start.1
  176.5 4.2 %collective-permute-done.1 = f32[2,2,512]{2,1,0:T(2,128)S(1)} collective-permute-done((f32[2,2,512]{2,1,0:T(2,128)S(1)}, f32[2,2,512]{2,1,0:T(2,128)S(1)}, u32[]{:S(2)}, u32[]{:S(2)}) %collective-permute-start.1) | collective-permute-done | bytes 8224 | tf_op jit(solution)/shard_map/ppermute | solution.py:13
  180.7 1.1 reshape.136
  181.8 0.8 add_convert_fusion
  (55 shorter events, 6.5 us)
Async XLA Ops:
  6.5 4.0 %copy-start = (bf16[64,2,1024]{2,1,0:T(2,128)(2,1)S(1)}, bf16[64,2,1024]{2,1,0:T(2,128)(2,1)}, u32[]{:S(2)}) copy-start(bf16[64,2,1024]{2,1,0:T(2,128)(2,1)} %param.14) | copy-start | bytes 786436
  6.5 26.4 %all-gather.7.cloned.1.call-start = ((), (), s32[]{:S(2)}) async-start(), calls=%async_computation.1 | async-start | bytes 1572864 | tf_op jit(solution)/shard_map/all_gather | solution.py:30
  7.3 3.7 %copy-start.5 = (f32[1024]{0:T(1024)S(1)}, f32[1024]{0:T(1024)}, u32[]{:S(2)}) copy-start(f32[1024]{0:T(1024)} %param.15) | copy-start | bytes 12292
  7.3 48.6 %all-gather.9.cloned.1.call-start = ((), (), s32[]{:S(2)}) async-start(), calls=%async_computation.2 | async-start | bytes 1572864 | tf_op jit(solution)/shard_map/all_gather | solution.py:31
  8.0 70.7 %all-gather.11.cloned.1.call-start = ((), (), s32[]{:S(2)}) async-start(), calls=%async_computation.3 | async-start | bytes 1572864 | tf_op jit(solution)/shard_map/all_gather | solution.py:32
  8.8 104.5 %all-gather.17.cloned.1.call-start = ((), (), s32[]{:S(2)}) async-start(), calls=%async_computation.6 | async-start | bytes 3145728 | tf_op jit(solution)/shard_map/all_gather | solution.py:76
  9.3 2.3 %copy-start.4 = (f32[5,512]{1,0:T(8,128)S(1)}, f32[5,512]{1,0:T(8,128)}, u32[]{:S(2)}) copy-start(f32[5,512]{1,0:T(8,128)} %param.23) | copy-start | bytes 30724
  9.3 2.3 %copy-start.6 = (s32[1,1,4]{2,1,0:T(1,128)S(1)}, s32[1,1,4]{2,1,0:T(1,128)}, u32[]{:S(2)}) copy-start(s32[1,1,4]{2,1,0:T(1,128)} %param.16) | copy-start | bytes 52
  9.3 138.5 %all-gather.15.cloned.1.call-start = ((), (), s32[]{:S(2)}) async-start(), calls=%async_computation.5 | async-start | bytes 3145728 | tf_op jit(solution)/shard_map/all_gather | solution.py:33
  9.9 160.6 %all-gather.13.cloned.1.call-start = ((), (), s32[]{:S(2)}) async-start(), calls=%async_computation.4 | async-start | bytes 1572864 | tf_op jit(solution)/shard_map/all_gather | solution.py:75
  10.5 170.2 %reduce-scatter.2.cloned.1.call-start = ((), (), s32[]{:S(2)}) async-start(), calls=%async_computation.7 | async-start | bytes 393216 | tf_op jit(solution)/shard_map/reduce_scatter | solution.py:80
  98.4 1.2 copy-start.3
  150.9 22.0 %copy-start.2 = (f32[68,2,512]{2,1,0:T(2,128)S(1)}, f32[68,2,512]{2,1,0:T(2,128)}, u32[]{:S(2)}) copy-start(f32[68,2,512]{2,1,0:T(2,128)} %fusion.26) | copy-start | bytes 835588
  150.9 25.5 %slice-start = ((f32[68,2,512]{2,1,0:T(2,128)}), f32[64,2,512]{2,1,0:T(2,128)S(1)}, s32[]{:S(2)}) async-start(f32[68,2,512]{2,1,0:T(2,128)} %fusion.26), calls=%async_computation.8 | async-start | bytes 524288 | tf_op jit(solution)/shard_map/slice | solution.py:90
  150.9 30.9 %copy-start.1 = (bf16[64,2,1024]{2,1,0:T(2,128)(2,1)S(1)}, bf16[64,2,1024]{2,1,0:T(2,128)(2,1)}, u32[]{:S(2)}) copy-start(bf16[64,2,1024]{2,1,0:T(2,128)(2,1)} %param.14) | copy-start | bytes 786436
  172.9 3.6 %collective-permute-start = (f32[2,2,512]{2,1,0:T(2,128)S(1)}, f32[2,2,512]{2,1,0:T(2,128)S(1)}, u32[]{:S(2)}, u32[]{:S(2)}) collective-permute-start(f32[2,2,512]{2,1,0:T(2,128)S(1)} %get-tuple-element.30), channel_id=1, source_target_pairs={{0,2},{1,3},{4,6},{5,7},{8,10},{9,11},{12,14},{13,15},{16,18},{17,... | collective-permute-start | bytes 24584 | tf_op jit(solution)/shard_map/ppermute | solution.py:13
  175.1 5.5 %collective-permute-start.1 = (f32[2,2,512]{2,1,0:T(2,128)S(1)}, f32[2,2,512]{2,1,0:T(2,128)S(1)}, u32[]{:S(2)}, u32[]{:S(2)}) collective-permute-start(f32[2,2,512]{2,1,0:T(2,128)S(1)} %get-tuple-element.29), channel_id=1, source_target_pairs={{2,0},{3,1},{6,4},{7,5},{10,8},{11,9},{14,12},{15,13},{18,16},{19,... | collective-permute-start | bytes 24584 | tf_op jit(solution)/shard_map/ppermute | solution.py:13
Sparse Core Ops, SparseCore 0:
  8.9 23.9 all-gather.6
  34.5 21.2 all-gather.8
  57.4 21.2 all-gather.10
  80.1 33.1 all-gather.16
  114.7 33.1 all-gather.14
  149.2 21.2 all-gather.12
  173.0 7.6 reduce-scatter.1
where the time goes:
time: 190 us; the launch traced here: 189 us
  waiting for transfers between devices  121 us (64%)
  blocking collectives  31.3 us (16%)
  between operations  13.8 us (7%)
  matrix products  11.6 us (6%)
  local copies, waits for them, and re-layouts  4.94 us (3%)
  starting transfers between devices  3.75 us (2%)
  other arithmetic  3.36 us (2%)
    all_gather x1, waiting for transfers between devices, on_device(): lax.all_gather(w_up, 'tm', axis=0, tiled=True)  34.5 us
    all_gather x1, waiting for transfers between devices, on_device(): lax.all_gather(w_key, 'tm', axis=0, tiled=True)  21.2 us
    all_gather x1, waiting for transfers between devices, on_device(): lax.all_gather(w_query, 'tm', axis=0, tiled=True)  19.9 us
    all_gather x1, waiting for transfers between devices, on_device(): lax.all_gather(w_out, 'tm', axis=1, tiled=True)  19.6 us
    all_gather x1, blocking collectives, on_device(): key_piece = lax.all_gather(key_grid, 'ctx', axis=1, tiled=True)  15.6 us
    all_gather x1, blocking collectives, on_device(): value_piece = lax.all_gather(value_grid, 'ctx', axis=1, tiled=True)  15.6 us
    all_gather x1, waiting for transfers between devices, on_device(): lax.all_gather(w_down, 'tm', axis=1, tiled=True)  12.8 us
    all_gather x1, waiting for transfers between devices, on_device(): lax.all_gather(w_value, 'tm', axis=0, tiled=True)  4.79 us
  transfers between devices with their start and end apart: 9, of which 7 were waited for; matrix products, arithmetic and copies ran while one was open for 8% of the time, Pallas kernels for 0%

commit v1 on v0

v1 whole, which is shorter than its diff:
```python
import functools

import jax
import jax.numpy as jnp
from jax import lax
from jax.experimental import pallas as pl
from jax.experimental.pallas import tpu as pltpu
from jax.sharding import PartitionSpec as P

HEAD_DIM = 64
KERNEL = 5
MASKED = -1e30
VMEM = pltpu.CompilerParams(vmem_limit_bytes=48 * 1024 * 1024)


def from_behind(value, axis, steps):
    count = lax.axis_size(axis)
    first, last = (max(0, -steps), min(count, count - steps))
    return lax.ppermute(value, axis, [(source, source + steps) for source in range(first, last)])


def rms_norm(tokens, norm_gain):
    values = tokens.astype(jnp.float32)
    square = jnp.mean(values * values, axis=-1, keepdims=True)
    return (values * lax.rsqrt(square + 1e-05) * norm_gain).astype(jnp.bfloat16)


def across(value, axis, step):
    count = lax.axis_size(axis)
    return lax.ppermute(value, axis, [(source, source ^ step) for source in range(count)])


def convolve(normed_cols, conv_weight):
    frames_here, dancers_here, features_here = normed_cols.shape
    wide = normed_cols.astype(jnp.float32)
    before = from_behind(normed_cols[frames_here - 2 :], "tm", 1).astype(jnp.float32)
    after = from_behind(normed_cols[0:2], "tm", -1).astype(jnp.float32)
    padded = jnp.concatenate([before, wide, after], axis=0)
    convolved = jnp.zeros((frames_here, dancers_here, features_here), jnp.float32)
    for offset in range(KERNEL):
        convolved = convolved + conv_weight[offset] * padded[offset : offset + frames_here]
    return convolved


def project_kernel(n_ctx, place, *refs):
    own, firsts, seconds = refs[0], refs[1:n_ctx], refs[n_ctx : 2 * n_ctx - 1]
    near_w, far_w, farther_w = refs[2 * n_ctx - 1 : 2 * n_ctx + 2]
    outs = refs[2 * n_ctx + 2 : 3 * n_ctx + 2]
    qkv_out = refs[3 * n_ctx + 2]
    held = refs[3 * n_ctx + 3]
    tm, groups, tp = place[0], place[1], place[2]
    rows, width = own.shape
    half, near, far = rows // 2, near_w.shape[0], far_w.shape[0]
    cuts = (
        (0, near, pl.multiple_of(tm * near, near)),
        (near, far, pl.multiple_of((1 - tm) * near + groups * far, far)),
        (near + far, far, pl.multiple_of((1 - tm) * near + (1 - groups) * far, far)),
    )
    for to, size, start in cuts:
        held[0:rows, to : to + size] = own[:, pl.ds(start, size)]
        for d in range(1, n_ctx):
            here = pl.multiple_of(d * rows + tp * half, half)
            there = pl.multiple_of(d * rows + (1 - tp) * half, half)
            held[pl.ds(here, half), to : to + size] = firsts[d - 1][:, pl.ds(start, size)]
            held[pl.ds(there, half), to : to + size] = seconds[d - 1][:, pl.ds(start, size)]
    total = jnp.dot(held[:, 0:near], near_w[...], preferred_element_type=jnp.float32)
    total += jnp.dot(held[:, near : near + far], far_w[...], preferred_element_type=jnp.float32)
    total += jnp.dot(held[:, near + far :], farther_w[...], preferred_element_type=jnp.float32)
    hidden = outs[0].shape[1]
    activated = jax.nn.gelu(total[:, :hidden], approximate=True).astype(jnp.bfloat16)
    for d in range(n_ctx):
        outs[d][...] = activated[d * rows : (d + 1) * rows]
    qkv_out[...] = total[:, hidden:].astype(jnp.bfloat16)


def attend_kernel(n_ctx, place, *refs):
    masks, qkv, outs = refs[:n_ctx], refs[n_ctx], refs[n_ctx + 1 :]
    ctx = place[0]
    rows, wide = outs[0].shape
    heads = wide // HEAD_DIM
    lane_head = lax.broadcasted_iota(jnp.int32, (1, wide), 1) // HEAD_DIM
    keys = qkv[:, wide : 2 * wide]
    values = qkv[:, 2 * wide :]
    for i in range(n_ctx):
        queries = qkv[i * rows : (i + 1) * rows, 0:wide]
        bias = jnp.concatenate(
            [
                jnp.full((1, rows), jnp.where(masks[i][0, ctx ^ j] > 0, 0.0, MASKED), jnp.float32)
                for j in range(n_ctx)
            ],
            axis=1,
        )
        result = jnp.zeros((rows, wide), jnp.float32)
        for head in range(heads):
            one = jnp.where(lane_head == head, queries, jnp.zeros_like(queries))
            scores = lax.dot_general(
                one, keys, (((1,), (1,)), ((), ())), preferred_element_type=jnp.float32
            )
            scores = scores * 0.125 + bias
            peak = jnp.max(scores, axis=-1, keepdims=True)
            expo = jnp.exp(scores - peak)
            total = jnp.sum(expo, axis=-1, keepdims=True)
            mixed = jnp.dot(expo.astype(jnp.bfloat16), values, preferred_element_type=jnp.float32)
            result = jnp.where(lane_head == head, mixed / total, result)
        outs[i][...] = result.astype(jnp.bfloat16)


def join_kernel(n_ctx, place, *refs):
    ctx, tm, groups, tp = place[0], place[1], place[2], place[3]
    acts, atts = refs[:n_ctx], refs[n_ctx : 2 * n_ctx]
    near_down, near_out, far_out, base = refs[2 * n_ctx : 2 * n_ctx + 4]
    pieces = refs[2 * n_ctx + 4 : 3 * n_ctx + 4]
    keep, send = refs[3 * n_ctx + 4 : 3 * n_ctx + 6]
    act_held, att_held = refs[3 * n_ctx + 6 :]
    hidden, wide = acts[0].shape[1], atts[0].shape[1]
    for d in range(n_ctx):
        act_held[ctx ^ d] = acts[d][...]
        att_held[ctx ^ d] = atts[d][...]

    def dot(left, right):
        return jnp.dot(left, right, preferred_element_type=jnp.float32)

    near_sum = None
    far_sum = None
    for e in range(n_ctx):
        term = dot(act_held[e], near_down[e * hidden : (e + 1) * hidden])
        term += dot(att_held[e], near_out[e * wide : (e + 1) * wide])
        near_sum = term if near_sum is None else near_sum + term
        term = dot(att_held[e], far_out[e * wide : (e + 1) * wide])
        far_sum = term if far_sum is None else far_sum + term
    for step in range(n_ctx // 2):
        far_sum += dot(act_held[2 * step + groups], pieces[2 * step][...])
        far_sum += dot(act_held[2 * step + 1 - groups], pieces[2 * step + 1][...])
    same = tm == tp
    keep[...] = jnp.where(same, near_sum, far_sum) + base[...]
    send[...] = jnp.where(same, far_sum, near_sum).astype(jnp.bfloat16)


def smem():
    return pl.BlockSpec(memory_space=pltpu.SMEM)


def vmem():
    return pl.BlockSpec(memory_space=pltpu.VMEM)


def split_over_ctx(
    tokens, norm_gain, block_mask, w_query, w_key, w_value, w_out, w_up, w_down, conv_weight
):
    n_ctx = lax.axis_size("ctx")
    groups, ctx = lax.axis_index("groups"), lax.axis_index("ctx")
    tm, tp = lax.axis_index("tm"), lax.axis_index("tp")
    frames_here, dancers_here, width = tokens.shape
    rows = frames_here * dancers_here
    depth = w_query.shape[0]
    wide = w_query.shape[1] // n_ctx
    hidden = w_up.shape[1] // n_ctx
    columns = w_out.shape[1]
    packed_width = hidden + 3 * wide

    def packed(first, count):
        return jnp.concatenate(
            [
                lax.dynamic_slice(w, (first, ctx * size), (count, size))
                for w, size in ((w_up, hidden), (w_query, wide), (w_key, wide), (w_value, wide))
            ],
            axis=1,
        )

    normed_grid = rms_norm(tokens, norm_gain)
    normed = normed_grid.reshape(rows, width)
    half = lax.dynamic_slice_in_dim(normed, tp * (rows // 2), rows // 2, 0)
    firsts = [across(half, "ctx", d) for d in range(1, n_ctx)]
    masks = [block_mask[0]] + [across(block_mask[0], "ctx", d) for d in range(1, n_ctx)]
    seconds = [across(piece, "tp", 1) for piece in firsts]

    far_w = across(packed(groups * (depth // 2), depth // 2), "tm", 1)
    farther_w = across(far_w, "groups", 1)
    near_w = packed(0, depth)
    pieces = []
    for step in range(n_ctx // 2):
        start = (2 * step + groups) * hidden
        got = across(lax.dynamic_slice_in_dim(w_down, start, hidden, 0), "tm", 1)
        pieces += [got, across(got, "groups", 1)]
    far_out = across(w_out, "tm", 1)

    first_feature = tp * columns
    normed_cols = lax.dynamic_slice_in_dim(normed_grid, first_feature, columns, 2)
    token_cols = lax.dynamic_slice_in_dim(tokens, first_feature, columns, 2)
    base = (token_cols.astype(jnp.float32) + convolve(normed_cols, conv_weight)).reshape(
        rows, columns
    )

    place = jnp.stack([tm, groups, tp]).astype(jnp.int32)
    *acts, qkv = pl.pallas_call(
        functools.partial(project_kernel, n_ctx),
        out_shape=[jax.ShapeDtypeStruct((rows, hidden), jnp.bfloat16)] * n_ctx
        + [jax.ShapeDtypeStruct((n_ctx * rows, 3 * wide), jnp.bfloat16)],
        in_specs=[smem()] + [vmem()] * (2 * n_ctx + 2),
        out_specs=[vmem()] * (n_ctx + 1),
        scratch_shapes=[pltpu.VMEM((n_ctx * rows, width), jnp.bfloat16)],
        compiler_params=VMEM,
        name="project",
        cost_estimate=pl.CostEstimate(
            flops=2 * n_ctx * rows * width * packed_width,
            bytes_accessed=4 * 1024 * 1024,
            transcendentals=n_ctx * rows * hidden,
        ),
    )(place, normed, *firsts, *seconds, near_w, far_w, farther_w)
    acts = [acts[0]] + [across(acts[d], "ctx", d) for d in range(1, n_ctx)]

    place = ctx.astype(jnp.int32).reshape(1)
    atts = pl.pallas_call(
        functools.partial(attend_kernel, n_ctx),
        out_shape=[jax.ShapeDtypeStruct((rows, wide), jnp.bfloat16)] * n_ctx,
        in_specs=[smem()] * (n_ctx + 1) + [vmem()],
        out_specs=[vmem()] * n_ctx,
        compiler_params=VMEM,
        name="attend",
        cost_estimate=pl.CostEstimate(
            flops=4 * wide * (n_ctx * rows) ** 2,
            bytes_accessed=1024 * 1024,
            transcendentals=(wide // HEAD_DIM) * (n_ctx * rows) ** 2,
        ),
    )(place, *masks, qkv)
    atts = [atts[0]] + [across(atts[d], "ctx", d) for d in range(1, n_ctx)]

    place = jnp.stack([ctx, tm, groups, tp]).astype(jnp.int32)
    keep, send = pl.pallas_call(
        functools.partial(join_kernel, n_ctx),
        out_shape=[
            jax.ShapeDtypeStruct((rows, columns), jnp.float32),
            jax.ShapeDtypeStruct((rows, columns), jnp.bfloat16),
        ],
        in_specs=[smem()] + [vmem()] * (3 * n_ctx + 4),
        out_specs=[vmem()] * 2,
        scratch_shapes=[
            pltpu.VMEM((n_ctx, rows, hidden), jnp.bfloat16),
            pltpu.VMEM((n_ctx, rows, wide), jnp.bfloat16),
        ],
        compiler_params=VMEM,
        name="join",
        cost_estimate=pl.CostEstimate(
            flops=4 * rows * columns * n_ctx * (hidden + wide),
            bytes_accessed=5 * 1024 * 1024,
            transcendentals=0,
        ),
    )(place, *acts, *atts, w_down, w_out, far_out, base, *pieces)
    other = across(send, "tp", 1).astype(jnp.float32)
    return (keep + other).astype(jnp.bfloat16).reshape(frames_here, dancers_here, columns)


def gather_all(
    tokens, norm_gain, block_mask, w_query, w_key, w_value, w_out, w_up, w_down, conv_weight
):
    frames_here, dancers_here, width = tokens.shape
    rows_here = frames_here * dancers_here
    normed_grid = rms_norm(tokens, norm_gain)
    normed = normed_grid.reshape(rows_here, width)
    query_sum, key_sum, value_sum, hidden = tuple(
        jnp.dot(
            normed,
            lax.all_gather(piece, "tm", axis=0, tiled=True),
            preferred_element_type=jnp.float32,
        )
        for piece in (w_query, w_key, w_value, w_up)
    )
    local_heads = query_sum.shape[1] // HEAD_DIM
    queries = query_sum.astype(jnp.bfloat16).reshape(rows_here, local_heads, HEAD_DIM)
    grid = (frames_here, dancers_here, local_heads * HEAD_DIM)
    key_piece = lax.all_gather(
        key_sum.astype(jnp.bfloat16).reshape(grid), "ctx", axis=1, tiled=True
    )
    value_piece = lax.all_gather(
        value_sum.astype(jnp.bfloat16).reshape(grid), "ctx", axis=1, tiled=True
    )
    count = key_piece.shape[1]
    allowed = jnp.tile(jnp.repeat(block_mask[0, 0].astype(jnp.float32), dancers_here), frames_here)
    key_rows = key_piece.reshape(frames_here * count, local_heads, HEAD_DIM)
    value_rows = value_piece.reshape(frames_here * count, local_heads, HEAD_DIM)
    scores = (
        jnp.einsum("qhd,khd->hqk", queries, key_rows, preferred_element_type=jnp.float32) * 0.125
    )
    scores = jnp.where(allowed[None, None, :] > 0, scores, MASKED)
    expo = jnp.exp(scores - jnp.max(scores, axis=-1, keepdims=True)) * allowed[None, None, :]
    total = jnp.sum(expo, axis=-1)
    mixed = jnp.einsum(
        "hqk,khd->hqd", expo.astype(jnp.bfloat16), value_rows, preferred_element_type=jnp.float32
    )
    attended = (
        (mixed / total[:, :, None])
        .transpose(1, 0, 2)
        .reshape(rows_here, local_heads * HEAD_DIM)
        .astype(jnp.bfloat16)
    )
    activated = jax.nn.gelu(hidden, approximate=True).astype(jnp.bfloat16)
    out_full = lax.all_gather(w_out, "tm", axis=1, tiled=True)
    down_full = lax.all_gather(w_down, "tm", axis=1, tiled=True)
    branches = jnp.dot(attended, out_full, preferred_element_type=jnp.float32)
    branches = branches + jnp.dot(activated, down_full, preferred_element_type=jnp.float32)
    mine = lax.psum_scatter(
        branches.astype(jnp.bfloat16), "tp", scatter_dimension=1, tiled=True
    ).astype(jnp.float32)
    features_here = mine.shape[1]
    first_feature = lax.axis_index("tp") * features_here
    normed_cols = lax.dynamic_slice_in_dim(normed_grid, first_feature, features_here, 2)
    token_cols = lax.dynamic_slice_in_dim(tokens, first_feature, features_here, 2)
    result = (
        token_cols.astype(jnp.float32)
        + mine.reshape(frames_here, dancers_here, features_here)
        + convolve(normed_cols, conv_weight)
    )
    return result.astype(jnp.bfloat16)


def solution(mesh):
    n_ctx, n_tm = mesh.shape["ctx"], mesh.shape["tm"]

    def on_device(*arrays):
        local_heads = arrays[3].shape[1] // HEAD_DIM
        pairs = n_tm == 2 and mesh.shape["groups"] == 2 and mesh.shape["tp"] == 2
        even = n_ctx & (n_ctx - 1) == 0 and n_ctx > 1 and local_heads % (2 * n_ctx) == 0
        chosen = split_over_ctx if pairs and even else gather_all
        return chosen(*arrays)

    placed = (
        P(("groups", "tm"), "ctx", None),
        P(),
        P(("groups", "tm"), "ctx", None),
        P("tm", "tp"),
        P("tm", "tp"),
        P("tm", "tp"),
        P("tp", "tm"),
        P("tm", "tp"),
        P("tp", "tm"),
        P(None, "tp"),
    )
    return jax.shard_map(
        on_device,
        mesh=mesh,
        in_specs=placed,
        out_specs=P(("groups", "tm"), "ctx", "tp"),
        check_vma=False,
    )
```

time: 190 us -> 79.2 us (0.42)
  waiting for transfers between devices: 121 us -> 9.56 us
  blocking collectives: 31.3 us -> 0 us
  starting transfers between devices: 3.75 us -> 33.2 us
  local copies, waits for them, and re-layouts: 4.94 us -> 20.5 us
  between operations: 13.8 us -> 0.28 us
  matrix products: 11.6 us -> 0 us
  Pallas kernels: 0 us -> 7.9 us
  other arithmetic: 3.36 us -> 6.46 us
    all_gather x6 -> x0, waiting for transfers between devices: 113 us -> none  [the longest x1 34.5 us: on_device(): lax.all_gather(w_up, 'tm', axis=0, tiled=True)]
    all_gather x2 -> x0, blocking collectives: 31.3 us -> none  [the longest x1 15.6 us: on_device(): key_piece = lax.all_gather(key_grid, 'ctx', axis=1, tiled=True)]
    ppermute x0 -> x23, starting transfers between devices: none -> 28.6 us  [across(): lax.ppermute(value, axis, [(source, source ^ step) for source in range(co...]
    dot_general x8 -> x0, matrix products: 11.6 us -> none  [the longest x3 4.59 us: on_device(): jnp.dot(normed, piece_one, preferred_element_type=jnp.float32)]
    ppermute x0 -> x23, waiting for transfers between devices: none -> 9.5 us  [across(): lax.ppermute(value, axis, [(source, source ^ step) for source in range(co...]
    unnamed x14 -> x54, local copies, waits for them, and re-layouts: 0.63 us -> 8.77 us
    pallas_call x0 -> x3, Pallas kernels: none -> 7.9 us  [the longest x1 3.44 us: split_over_ctx(): pl.pallas_call(functools.partial(attend_kernel, n_ctx), out_shape=[jax.Sh...]
    dynamic_slice x1 -> x9, local copies, waits for them, and re-layouts: 0.1 us -> 7.9 us  [the longest x7 6.4 us: packed(): lax.dynamic_slice(w, (first, ctx * size), (count, size))]
  transfers between devices with their start and end apart: 9 -> 25, of which waited for: 7 -> 7; matrix products, arithmetic and copies ran while one was open for 8% -> 18% of each run, Pallas kernels for 0% -> 8%
where the time goes in v1:
time: 79.2 us; the launch traced here: 77.9 us
  starting transfers between devices  33.2 us (42%)
  local copies, waits for them, and re-layouts  20.5 us (26%)
  waiting for transfers between devices  9.56 us (12%)
  Pallas kernels  7.9 us (10%)
  other arithmetic  6.46 us (8%)
    ppermute x23, starting transfers between devices, across(): lax.ppermute(value, axis, [(source, source ^ step) for source in range(co...  28.6 us
    ppermute x23, waiting for transfers between devices, across(): lax.ppermute(value, axis, [(source, source ^ step) for source in range(co...  9.5 us
    unnamed x54, local copies, waits for them, and re-layouts  8.77 us
    dynamic_slice x7, local copies, waits for them, and re-layouts, packed(): lax.dynamic_slice(w, (first, ctx * size), (count, size))  6.4 us
    ppermute x2, starting transfers between devices, from_behind(): lax.ppermute(value, axis, [(source, source + steps) for source in range(f...  4.67 us
    pallas_call x1, Pallas kernels, split_over_ctx(): pl.pallas_call(functools.partial(attend_kernel, n_ctx), out_shape=[jax.Sh...  3.44 us
    pallas_call x1, Pallas kernels, split_over_ctx(): pl.pallas_call(functools.partial(project_kernel, n_ctx), out_shape=[jax.S...  2.89 us
    convert_element_type x1, other arithmetic, convolve(): wide = normed_cols.astype(jnp.float32)  1.7 us
  transfers between devices with their start and end apart: 25, of which 7 were waited for; matrix products, arithmetic and copies ran while one was open for 18% of the time, Pallas kernels for 8%

profile of v1, /device:TPU:0, one launch (start us, length us, event | category | flops | bytes accessed | tf_op | source)
XLA Modules:
  0.0 77.9 jit_solution(9182623349833020369)
XLA Ops:
  0.0 1.3 %fusion = f32[64,2]{1,0:T(8,128)S(1)} fusion(bf16[64,2,1024]{2,1,0:T(2,128)(2,1)} %param.10), kind=kLoop, calls=%fused_computation.3 | loop fusion | flops 393088 | bytes 262656 | tf_op jit(solution)/shard_map/reduce_sum | solution.py:24
  1.3 1.3 %fusion.2 = bf16[64,2,1024]{2,1,0:T(2,128)(2,1)S(1)} fusion(bf16[64,2,1024]{2,1,0:T(2,128)(2,1)} %param.10, f32[1024]{0:T(1024)} %param.11, f32[64,2]{1,0:T(8,128)S(1)} %add_rsqrt_fusion), kind=kLoop, calls=%fused_computation.5 | loop fusion | flops 524288 | bytes 528896 | tf_op jit(solution)/shard_map/convert_element_type | solution.py:25
  3.4 3.0 %collective-permute-start = (bf16[64,1024]{1,0:T(8,128)(2,1)}, bf16[64,1024]{1,0:T(8,128)(2,1)S(1)}, u32[]{:S(2)}, u32[]{:S(2)}) collective-permute-start(bf16[64,1024]{1,0:T(8,128)(2,1)} %constant_dynamic-slice_fusion.8), channel_id=1, source_target_pairs={{0,4},{4,0},{8,12},{12,8},{1,5},{5,1},{9,13},{13,9},{2,6},{6,2},{1... | collective-permute-start | bytes 393224 | tf_op jit(solution)/shard_map/ppermute | solution.py:30
  6.4 2.6 %collective-permute-start.1 = (bf16[64,1024]{1,0:T(8,128)(2,1)}, bf16[64,1024]{1,0:T(8,128)(2,1)}, u32[]{:S(2)}, u32[]{:S(2)}) collective-permute-start(bf16[64,1024]{1,0:T(8,128)(2,1)} %constant_dynamic-slice_fusion.8), channel_id=1, source_target_pairs={{0,8},{4,12},{8,0},{12,4},{1,9},{5,13},{9,1},{13,5},{2,10},{6,14},... | collective-permute-start | bytes 393224 | tf_op jit(solution)/shard_map/ppermute | solution.py:30
  13.3 1.7 %collective-permute-start.6 = (bf16[256,640]{1,0:T(8,128)(2,1)}, bf16[256,640]{1,0:T(8,128)(2,1)}, u32[]{:S(2)}, u32[]{:S(2)}) collective-permute-start(bf16[256,640]{1,0:T(8,128)(2,1)} %pad_maximum_fusion.1), channel_id=1, source_target_pairs={{0,2},{2,0},{1,3},{3,1},{4,6},{6,4},{5,7},{7,5},{8,10},{10,8},{9,1... | collective-permute-start | bytes 983048 | tf_op jit(solution)/shard_map/ppermute | solution.py:30
  19.8 1.8 %collective-permute-start.22 = (bf16[256,512]{1,0:T(8,128)(2,1)}, bf16[256,512]{1,0:T(8,128)(2,1)S(1)}, u32[]{:S(2)}, u32[]{:S(2)}) collective-permute-start(bf16[256,512]{1,0:T(8,128)(2,1)} %get-tuple-element.27), channel_id=1, source_target_pairs={{0,2},{2,0},{1,3},{3,1},{4,6},{6,4},{5,7},{7,5},{8,10},{10,8},{9,1... | collective-permute-start | bytes 786440 | tf_op jit(solution)/shard_map/ppermute | solution.py:30
  24.2 1.7 %collective-permute-start.7 = (bf16[256,640]{1,0:T(8,128)(2,1)}, bf16[256,640]{1,0:T(8,128)(2,1)}, u32[]{:S(2)}, u32[]{:S(2)}) collective-permute-start(bf16[256,640]{1,0:T(8,128)(2,1)} %collective-permute-done.6.refs_8_), channel_id=1, source_target_pairs={{0,16},{16,0},{1,17},{17,1},{2,18},{18,2},{3,19},{19,3},{4,20},{20... | collective-permute-start | bytes 983048 | tf_op jit(solution)/shard_map/ppermute | solution.py:30
  26.0 1.7 %dynamic-slice_convert_fusion = f32[64,2,512]{2,1,0:T(2,128)} fusion(bf16[64,2,1024]{2,1,0:T(2,128)(2,1)} %copy-done.19, s32[]{:T(128)S(6)} %select_n.35), kind=kLoop, calls=%fused_computation.25 | loop fusion | flops 65536 | bytes 393220 | tf_op jit(solution)/shard_map/convert_element_type | solution.py:35
  27.7 1.3 %constant_dynamic-slice_fusion.1 = (bf16[2,2,512]{2,1,0:T(2,128)(2,1)}, bf16[2,2,512]{2,1,0:T(2,128)(2,1)}) fusion(bf16[64,2,1024]{2,1,0:T(2,128)(2,1)} %copy-done.19, s32[]{:T(128)S(6)} %add.80, s32[]{:T(128)S(6)} %select_n.35), kind=kLoop, calls=%fused_computation.28 | loop fusion | bytes 16392 | tf_op jit(solution)/shard_map/slice | solution.py:36
  29.8 1.7 %collective-permute-start.21 = (bf16[256,512]{1,0:T(8,128)(2,1)S(1)}, bf16[256,512]{1,0:T(8,128)(2,1)S(1)}, u32[]{:S(2)}, u32[]{:S(2)}) collective-permute-start(bf16[256,512]{1,0:T(8,128)(2,1)S(1)} %collective-permute-done.20.refs_12_), channel_id=1, source_target_pairs={{0,16},{16,0},{1,17},{17,1},{2,18},{18,2},{3,19},{19,3},{4,20},{20... | collective-permute-start | bytes 786440 | tf_op jit(solution)/shard_map/ppermute | solution.py:30
  31.5 3.9 %collective-permute-done.22.refs_14_ = bf16[256,512]{1,0:T(8,128)(2,1)S(1)} collective-permute-done((bf16[256,512]{1,0:T(8,128)(2,1)}, bf16[256,512]{1,0:T(8,128)(2,1)S(1)}, u32[]{:S(2)}, u32[]{:S(2)}) %collective-permute-start.22) | collective-permute-done | bytes 262176 | tf_op jit(solution)/shard_map/ppermute | solution.py:30
  35.4 1.7 %collective-permute-start.23 = (bf16[256,512]{1,0:T(8,128)(2,1)S(1)}, bf16[256,512]{1,0:T(8,128)(2,1)S(1)}, u32[]{:S(2)}, u32[]{:S(2)}) collective-permute-start(bf16[256,512]{1,0:T(8,128)(2,1)S(1)} %collective-permute-done.22.refs_14_), channel_id=1, source_target_pairs={{0,16},{16,0},{1,17},{17,1},{2,18},{18,2},{3,19},{19,3},{4,20},{20... | collective-permute-start | bytes 786440 | tf_op jit(solution)/shard_map/ppermute | solution.py:30
  37.9 3.5 %collective-permute-start.12 = (s32[1,4]{1,0:T(1,128)S(1)}, s32[1,4]{1,0:T(1,128)S(1)}, u32[]{:S(2)}, u32[]{:S(2)}) collective-permute-start(s32[1,4]{1,0:T(1,128)S(1)} %bitcast.11), channel_id=1, source_target_pairs={{0,8},{4,12},{8,0},{12,4},{1,9},{5,13},{9,1},{13,5},{2,10},{6,14},... | collective-permute-start | bytes 56 | tf_op jit(solution)/shard_map/ppermute | solution.py:30
  44.1 2.9 %project.1 = (bf16[128,256]{1,0:T(8,128)(2,1)S(1)}, bf16[128,256]{1,0:T(8,128)(2,1)}, bf16[128,256]{1,0:T(8,128)(2,1)}, bf16[128,256]{1,0:T(8,128)(2,1)}, bf16[512,384]{1,0:T(8,128)(2,1)S(1)}) custom-call(s32[3]{0:T(128)S(1)} %pad_add_fusion.1.place, bf16[128,1024]{1,0:T(8,128)(2,1)S(1)} %reshape.24.refs_0_, bf16[64,1024]{1,0:T(8,128)(2,1)S(1)} %copy-done.13, ...), custom_call_target="tpu_custom_call" | custom-call | flops 671088640 | bytes 4194304 | tf_op jit(solution)/shard_map/project/pallas_call | solution.py:195
  47.3 3.4 %collective-permute-start.18 = (bf16[2,2,512]{2,1,0:T(2,128)(2,1)S(1)}, bf16[2,2,512]{2,1,0:T(2,128)(2,1)S(1)}, u32[]{:S(2)}, u32[]{:S(2)}) collective-permute-start(bf16[2,2,512]{2,1,0:T(2,128)(2,1)S(1)} %copy-done.26), channel_id=1, source_target_pairs={{0,2},{1,3},{4,6},{5,7},{8,10},{9,11},{12,14},{13,15},{16,18},{17,... | collective-permute-start | bytes 12296 | tf_op jit(solution)/shard_map/ppermute | solution.py:19
  50.7 1.7 %collective-permute-done.13.refs_3_ = s32[1,4]{1,0:T(1,128)S(1)} collective-permute-done((s32[1,4]{1,0:T(1,128)S(1)}, s32[1,4]{1,0:T(1,128)S(1)}, u32[]{:S(2)}, u32[]{:S(2)}) %collective-permute-start.13) | collective-permute-done | bytes 48 | tf_op jit(solution)/shard_map/ppermute | solution.py:30
  52.5 1.3 %collective-permute-start.19 = (bf16[2,2,512]{2,1,0:T(2,128)(2,1)S(1)}, bf16[2,2,512]{2,1,0:T(2,128)(2,1)S(1)}, u32[]{:S(2)}, u32[]{:S(2)}) collective-permute-start(bf16[2,2,512]{2,1,0:T(2,128)(2,1)S(1)} %copy-done.25), channel_id=1, source_target_pairs={{2,0},{3,1},{6,4},{7,5},{10,8},{11,9},{14,12},{15,13},{18,16},{19,... | collective-permute-start | bytes 12296 | tf_op jit(solution)/shard_map/ppermute | solution.py:19
  53.8 3.4 %attend.1 = (bf16[128,128]{1,0:T(8,128)(2,1)S(1)}, bf16[128,128]{1,0:T(8,128)(2,1)S(1)}, bf16[128,128]{1,0:T(8,128)(2,1)}, bf16[128,128]{1,0:T(8,128)(2,1)}) custom-call(s32[1]{0:T(128)} %bitcast.place, s32[1,4]{1,0:T(1,128)S(1)} %bitcast.13, s32[1,4]{1,0:T(1,128)S(1)} %collective-permute-done.11.refs_1_, s32[1,4]{1,0:T(1,128)S(1)} %collective-permute-done.12.refs_2_, ...), custom_call_target="tpu_custom_call" | custom-call | flops 134217728 | bytes 1048576 | tf_op jit(solution)/shard_map/attend/pallas_call | solution.py:213
  58.0 2.5 %collective-permute-start.15 = (bf16[128,128]{1,0:T(8,128)(2,1)}, bf16[128,128]{1,0:T(8,128)(2,1)}, u32[]{:S(2)}, u32[]{:S(2)}) collective-permute-start(bf16[128,128]{1,0:T(8,128)(2,1)} %get-tuple-element.23), channel_id=1, source_target_pairs={{0,8},{4,12},{8,0},{12,4},{1,9},{5,13},{9,1},{13,5},{2,10},{6,14},... | collective-permute-start | bytes 98312 | tf_op jit(solution)/shard_map/ppermute | solution.py:30
  61.2 1.9 %collective-permute-start.16 = (bf16[128,128]{1,0:T(8,128)(2,1)}, bf16[128,128]{1,0:T(8,128)(2,1)}, u32[]{:S(2)}, u32[]{:S(2)}) collective-permute-start(bf16[128,128]{1,0:T(8,128)(2,1)} %get-tuple-element.24), channel_id=1, source_target_pairs={{0,12},{4,8},{8,4},{12,0},{1,13},{5,9},{9,5},{13,1},{2,14},{6,10},... | collective-permute-start | bytes 98312 | tf_op jit(solution)/shard_map/ppermute | solution.py:30
  63.8 1.9 %collective-permute-start.10 = (bf16[128,256]{1,0:T(8,128)(2,1)}, bf16[128,256]{1,0:T(8,128)(2,1)S(1)}, u32[]{:S(2)}, u32[]{:S(2)}) collective-permute-start(bf16[128,256]{1,0:T(8,128)(2,1)} %get-tuple-element.19), channel_id=1, source_target_pairs={{0,12},{4,8},{8,4},{12,0},{1,13},{5,9},{9,5},{13,1},{2,14},{6,10},... | collective-permute-start | bytes 196616 | tf_op jit(solution)/shard_map/ppermute | solution.py:30
  66.3 2.5 %collective-permute-start.9 = (bf16[128,256]{1,0:T(8,128)(2,1)}, bf16[128,256]{1,0:T(8,128)(2,1)}, u32[]{:S(2)}, u32[]{:S(2)}) collective-permute-start(bf16[128,256]{1,0:T(8,128)(2,1)} %get-tuple-element.18), channel_id=1, source_target_pairs={{0,8},{4,12},{8,0},{12,4},{1,9},{5,13},{9,1},{13,5},{2,10},{6,14},... | collective-permute-start | bytes 196616 | tf_op jit(solution)/shard_map/ppermute | solution.py:30
  74.2 1.6 %join.1 = (f32[128,512]{1,0:T(8,128)S(1)}, bf16[128,512]{1,0:T(8,128)(2,1)S(1)}) custom-call(s32[4]{0:T(128)S(1)} %pad_add_fusion.place, bf16[128,256]{1,0:T(8,128)(2,1)S(1)} %copy-done.7, bf16[128,256]{1,0:T(8,128)(2,1)S(1)} %collective-permute-done.8.refs_1_, bf16[128,256]{1,0:T(8,128)(2,1)} %collective-permute-done.9.refs_2_, ...), custom_call_target="tpu_custom_call" | custom-call | flops 402653184 | bytes 5242880 | tf_op jit(solution)/shard_map/join/pallas_call | solution.py:229
  75.8 1.3 %collective-permute-done.24 = bf16[128,512]{1,0:T(8,128)(2,1)S(1)} collective-permute-done((bf16[128,512]{1,0:T(8,128)(2,1)S(1)}, bf16[128,512]{1,0:T(8,128)(2,1)S(1)}, u32[]{:S(2)}, u32[]{:S(2)}) %collective-permute-start.24) | collective-permute-done | bytes 131104 | tf_op jit(solution)/shard_map/ppermute | solution.py:30
  (109 shorter events, 26.0 us)
Async XLA Ops:
  3.4 15.4 %collective-permute-start = (bf16[64,1024]{1,0:T(8,128)(2,1)}, bf16[64,1024]{1,0:T(8,128)(2,1)S(1)}, u32[]{:S(2)}, u32[]{:S(2)}) collective-permute-start(bf16[64,1024]{1,0:T(8,128)(2,1)} %constant_dynamic-slice_fusion.8), channel_id=1, source_target_pairs={{0,4},{4,0},{8,12},{12,8},{1,5},{5,1},{9,13},{13,9},{2,6},{6,2},{1... | collective-permute-start | bytes 393224 | tf_op jit(solution)/shard_map/ppermute | solution.py:30
  6.4 13.4 %collective-permute-start.1 = (bf16[64,1024]{1,0:T(8,128)(2,1)}, bf16[64,1024]{1,0:T(8,128)(2,1)}, u32[]{:S(2)}, u32[]{:S(2)}) collective-permute-start(bf16[64,1024]{1,0:T(8,128)(2,1)} %constant_dynamic-slice_fusion.8), channel_id=1, source_target_pairs={{0,8},{4,12},{8,0},{12,4},{1,9},{5,13},{9,1},{13,5},{2,10},{6,14},... | collective-permute-start | bytes 393224 | tf_op jit(solution)/shard_map/ppermute | solution.py:30
  9.0 12.6 %collective-permute-start.2 = (bf16[64,1024]{1,0:T(8,128)(2,1)}, bf16[64,1024]{1,0:T(8,128)(2,1)S(1)}, u32[]{:S(2)}, u32[]{:S(2)}) collective-permute-start(bf16[64,1024]{1,0:T(8,128)(2,1)} %constant_dynamic-slice_fusion.8), channel_id=1, source_target_pairs={{0,12},{4,8},{8,4},{12,0},{1,13},{5,9},{9,5},{13,1},{2,14},{6,10},... | collective-permute-start | bytes 393224 | tf_op jit(solution)/shard_map/ppermute | solution.py:30
  13.3 11.0 %collective-permute-start.6 = (bf16[256,640]{1,0:T(8,128)(2,1)}, bf16[256,640]{1,0:T(8,128)(2,1)}, u32[]{:S(2)}, u32[]{:S(2)}) collective-permute-start(bf16[256,640]{1,0:T(8,128)(2,1)} %pad_maximum_fusion.1), channel_id=1, source_target_pairs={{0,2},{2,0},{1,3},{3,1},{4,6},{6,4},{5,7},{7,5},{8,10},{10,8},{9,1... | collective-permute-start | bytes 983048 | tf_op jit(solution)/shard_map/ppermute | solution.py:30
  15.8 13.9 %collective-permute-start.20 = (bf16[256,512]{1,0:T(8,128)(2,1)}, bf16[256,512]{1,0:T(8,128)(2,1)S(1)}, u32[]{:S(2)}, u32[]{:S(2)}) collective-permute-start(bf16[256,512]{1,0:T(8,128)(2,1)} %get-tuple-element.28), channel_id=1, source_target_pairs={{0,2},{2,0},{1,3},{3,1},{4,6},{6,4},{5,7},{7,5},{8,10},{10,8},{9,1... | collective-permute-start | bytes 786440 | tf_op jit(solution)/shard_map/ppermute | solution.py:30
  18.8 3.5 %collective-permute-start.3 = (bf16[64,1024]{1,0:T(8,128)(2,1)S(1)}, bf16[64,1024]{1,0:T(8,128)(2,1)S(1)}, u32[]{:S(2)}, u32[]{:S(2)}) collective-permute-start(bf16[64,1024]{1,0:T(8,128)(2,1)S(1)} %collective-permute-done.refs_1_), channel_id=1, source_target_pairs={{0,1},{1,0},{2,3},{3,2},{4,5},{5,4},{6,7},{7,6},{8,9},{9,8},{10,11... | collective-permute-start | bytes 393224 | tf_op jit(solution)/shard_map/ppermute | solution.py:30
  19.8 15.6 %collective-permute-start.22 = (bf16[256,512]{1,0:T(8,128)(2,1)}, bf16[256,512]{1,0:T(8,128)(2,1)S(1)}, u32[]{:S(2)}, u32[]{:S(2)}) collective-permute-start(bf16[256,512]{1,0:T(8,128)(2,1)} %get-tuple-element.27), channel_id=1, source_target_pairs={{0,2},{2,0},{1,3},{3,1},{4,6},{6,4},{5,7},{7,5},{8,10},{10,8},{9,1... | collective-permute-start | bytes 786440 | tf_op jit(solution)/shard_map/ppermute | solution.py:30
  21.6 6.1 %collective-permute-start.4 = (bf16[64,1024]{1,0:T(8,128)(2,1)}, bf16[64,1024]{1,0:T(8,128)(2,1)}, u32[]{:S(2)}, u32[]{:S(2)}) collective-permute-start(bf16[64,1024]{1,0:T(8,128)(2,1)} %collective-permute-done.1.refs_2_), channel_id=1, source_target_pairs={{0,1},{1,0},{2,3},{3,2},{4,5},{5,4},{6,7},{7,6},{8,9},{9,8},{10,11... | collective-permute-start | bytes 393224 | tf_op jit(solution)/shard_map/ppermute | solution.py:30
  22.9 42.8 %collective-permute-start.17 = (bf16[512,512]{1,0:T(8,128)(2,1)S(1)}, bf16[512,512]{1,0:T(8,128)(2,1)S(1)}, u32[]{:S(2)}, u32[]{:S(2)}) collective-permute-start(bf16[512,512]{1,0:T(8,128)(2,1)S(1)} %copy-done.1), channel_id=1, source_target_pairs={{0,2},{2,0},{1,3},{3,1},{4,6},{6,4},{5,7},{7,5},{8,10},{10,8},{9,1... | collective-permute-start | bytes 1572872 | tf_op jit(solution)/shard_map/ppermute | solution.py:30
  24.2 13.7 %collective-permute-start.7 = (bf16[256,640]{1,0:T(8,128)(2,1)}, bf16[256,640]{1,0:T(8,128)(2,1)}, u32[]{:S(2)}, u32[]{:S(2)}) collective-permute-start(bf16[256,640]{1,0:T(8,128)(2,1)} %collective-permute-done.6.refs_8_), channel_id=1, source_target_pairs={{0,16},{16,0},{1,17},{17,1},{2,18},{18,2},{3,19},{19,3},{4,20},{20... | collective-permute-start | bytes 983048 | tf_op jit(solution)/shard_map/ppermute | solution.py:30
  27.7 9.5 %collective-permute-start.5 = (bf16[64,1024]{1,0:T(8,128)(2,1)}, bf16[64,1024]{1,0:T(8,128)(2,1)}, u32[]{:S(2)}, u32[]{:S(2)}) collective-permute-start(bf16[64,1024]{1,0:T(8,128)(2,1)} %copy-done.14), channel_id=1, source_target_pairs={{0,1},{1,0},{2,3},{3,2},{4,5},{5,4},{6,7},{7,6},{8,9},{9,8},{10,11... | collective-permute-start | bytes 393224 | tf_op jit(solution)/shard_map/ppermute | solution.py:30
  29.8 30.7 %collective-permute-start.21 = (bf16[256,512]{1,0:T(8,128)(2,1)S(1)}, bf16[256,512]{1,0:T(8,128)(2,1)S(1)}, u32[]{:S(2)}, u32[]{:S(2)}) collective-permute-start(bf16[256,512]{1,0:T(8,128)(2,1)S(1)} %collective-permute-done.20.refs_12_), channel_id=1, source_target_pairs={{0,16},{16,0},{1,17},{17,1},{2,18},{18,2},{3,19},{19,3},{4,20},{20... | collective-permute-start | bytes 786440 | tf_op jit(solution)/shard_map/ppermute | solution.py:30
  35.4 27.7 %collective-permute-start.23 = (bf16[256,512]{1,0:T(8,128)(2,1)S(1)}, bf16[256,512]{1,0:T(8,128)(2,1)S(1)}, u32[]{:S(2)}, u32[]{:S(2)}) collective-permute-start(bf16[256,512]{1,0:T(8,128)(2,1)S(1)} %collective-permute-done.22.refs_14_), channel_id=1, source_target_pairs={{0,16},{16,0},{1,17},{17,1},{2,18},{18,2},{3,19},{19,3},{4,20},{20... | collective-permute-start | bytes 786440 | tf_op jit(solution)/shard_map/ppermute | solution.py:30
  37.2 9.9 %collective-permute-start.11 = (s32[1,4]{1,0:T(1,128)S(1)}, s32[1,4]{1,0:T(1,128)S(1)}, u32[]{:S(2)}, u32[]{:S(2)}) collective-permute-start(s32[1,4]{1,0:T(1,128)S(1)} %bitcast.10), channel_id=1, source_target_pairs={{0,4},{4,0},{8,12},{12,8},{1,5},{5,1},{9,13},{13,9},{2,6},{6,2},{1... | collective-permute-start | bytes 56 | tf_op jit(solution)/shard_map/ppermute | solution.py:30
  37.9 9.4 %collective-permute-start.12 = (s32[1,4]{1,0:T(1,128)S(1)}, s32[1,4]{1,0:T(1,128)S(1)}, u32[]{:S(2)}, u32[]{:S(2)}) collective-permute-start(s32[1,4]{1,0:T(1,128)S(1)} %bitcast.11), channel_id=1, source_target_pairs={{0,8},{4,12},{8,0},{12,4},{1,9},{5,13},{9,1},{13,5},{2,10},{6,14},... | collective-permute-start | bytes 56 | tf_op jit(solution)/shard_map/ppermute | solution.py:30
  47.1 5.4 %collective-permute-start.13 = (s32[1,4]{1,0:T(1,128)S(1)}, s32[1,4]{1,0:T(1,128)S(1)}, u32[]{:S(2)}, u32[]{:S(2)}) collective-permute-start(s32[1,4]{1,0:T(1,128)S(1)} %bitcast.12), channel_id=1, source_target_pairs={{0,12},{4,8},{8,4},{12,0},{1,13},{5,9},{9,5},{13,1},{2,14},{6,10},... | collective-permute-start | bytes 56 | tf_op jit(solution)/shard_map/ppermute | solution.py:30
  47.3 10.5 %collective-permute-start.18 = (bf16[2,2,512]{2,1,0:T(2,128)(2,1)S(1)}, bf16[2,2,512]{2,1,0:T(2,128)(2,1)S(1)}, u32[]{:S(2)}, u32[]{:S(2)}) collective-permute-start(bf16[2,2,512]{2,1,0:T(2,128)(2,1)S(1)} %copy-done.26), channel_id=1, source_target_pairs={{0,2},{1,3},{4,6},{5,7},{8,10},{9,11},{12,14},{13,15},{16,18},{17,... | collective-permute-start | bytes 12296 | tf_op jit(solution)/shard_map/ppermute | solution.py:19
  52.5 5.5 %collective-permute-start.19 = (bf16[2,2,512]{2,1,0:T(2,128)(2,1)S(1)}, bf16[2,2,512]{2,1,0:T(2,128)(2,1)S(1)}, u32[]{:S(2)}, u32[]{:S(2)}) collective-permute-start(bf16[2,2,512]{2,1,0:T(2,128)(2,1)S(1)} %copy-done.25), channel_id=1, source_target_pairs={{2,0},{3,1},{6,4},{7,5},{10,8},{11,9},{14,12},{15,13},{18,16},{19,... | collective-permute-start | bytes 12296 | tf_op jit(solution)/shard_map/ppermute | solution.py:19
  57.8 7.9 %collective-permute-start.14 = (bf16[128,128]{1,0:T(8,128)(2,1)S(1)}, bf16[128,128]{1,0:T(8,128)(2,1)S(1)}, u32[]{:S(2)}, u32[]{:S(2)}) collective-permute-start(bf16[128,128]{1,0:T(8,128)(2,1)S(1)} %get-tuple-element.22), channel_id=1, source_target_pairs={{0,4},{4,0},{8,12},{12,8},{1,5},{5,1},{9,13},{13,9},{2,6},{6,2},{1... | collective-permute-start | bytes 98312 | tf_op jit(solution)/shard_map/ppermute | solution.py:30
  58.0 13.1 %collective-permute-start.15 = (bf16[128,128]{1,0:T(8,128)(2,1)}, bf16[128,128]{1,0:T(8,128)(2,1)}, u32[]{:S(2)}, u32[]{:S(2)}) collective-permute-start(bf16[128,128]{1,0:T(8,128)(2,1)} %get-tuple-element.23), channel_id=1, source_target_pairs={{0,8},{4,12},{8,0},{12,4},{1,9},{5,13},{9,1},{13,5},{2,10},{6,14},... | collective-permute-start | bytes 98312 | tf_op jit(solution)/shard_map/ppermute | solution.py:30
  61.2 9.9 %collective-permute-start.16 = (bf16[128,128]{1,0:T(8,128)(2,1)}, bf16[128,128]{1,0:T(8,128)(2,1)}, u32[]{:S(2)}, u32[]{:S(2)}) collective-permute-start(bf16[128,128]{1,0:T(8,128)(2,1)} %get-tuple-element.24), channel_id=1, source_target_pairs={{0,12},{4,8},{8,4},{12,0},{1,13},{5,9},{9,5},{13,1},{2,14},{6,10},... | collective-permute-start | bytes 98312 | tf_op jit(solution)/shard_map/ppermute | solution.py:30
  63.8 7.3 %collective-permute-start.10 = (bf16[128,256]{1,0:T(8,128)(2,1)}, bf16[128,256]{1,0:T(8,128)(2,1)S(1)}, u32[]{:S(2)}, u32[]{:S(2)}) collective-permute-start(bf16[128,256]{1,0:T(8,128)(2,1)} %get-tuple-element.19), channel_id=1, source_target_pairs={{0,12},{4,8},{8,4},{12,0},{1,13},{5,9},{9,5},{13,1},{2,14},{6,10},... | collective-permute-start | bytes 196616 | tf_op jit(solution)/shard_map/ppermute | solution.py:30
  65.7 5.4 %collective-permute-start.8 = (bf16[128,256]{1,0:T(8,128)(2,1)}, bf16[128,256]{1,0:T(8,128)(2,1)S(1)}, u32[]{:S(2)}, u32[]{:S(2)}) collective-permute-start(bf16[128,256]{1,0:T(8,128)(2,1)} %get-tuple-element.17), channel_id=1, source_target_pairs={{0,4},{4,0},{8,12},{12,8},{1,5},{5,1},{9,13},{13,9},{2,6},{6,2},{1... | collective-permute-start | bytes 196616 | tf_op jit(solution)/shard_map/ppermute | solution.py:30
  66.3 5.5 %collective-permute-start.9 = (bf16[128,256]{1,0:T(8,128)(2,1)}, bf16[128,256]{1,0:T(8,128)(2,1)}, u32[]{:S(2)}, u32[]{:S(2)}) collective-permute-start(bf16[128,256]{1,0:T(8,128)(2,1)} %get-tuple-element.18), channel_id=1, source_target_pairs={{0,8},{4,12},{8,0},{12,4},{1,9},{5,13},{9,1},{13,5},{2,10},{6,14},... | collective-permute-start | bytes 196616 | tf_op jit(solution)/shard_map/ppermute | solution.py:30
  (28 other events, 213.3 us)

commit v2 on v0

v2 whole, which is shorter than its diff:
```python
import functools

import jax
import jax.numpy as jnp
from jax import lax
from jax.experimental import pallas as pl
from jax.experimental.pallas import tpu as pltpu
from jax.sharding import PartitionSpec as P

HEAD_DIM = 64
KERNEL = 5
MASKED = -1e30


def from_behind(value, axis, steps):
    count = lax.axis_size(axis)
    first, last = (max(0, -steps), min(count, count - steps))
    return lax.ppermute(value, axis, [(source, source + steps) for source in range(first, last)])


def rms_norm(tokens, norm_gain):
    values = tokens.astype(jnp.float32)
    square = jnp.mean(values * values, axis=-1, keepdims=True)
    return (values * lax.rsqrt(square + 1e-05) * norm_gain).astype(jnp.bfloat16)


def across(value, axis, step):
    count = lax.axis_size(axis)
    return lax.ppermute(value, axis, [(source, source ^ step) for source in range(count)])


def two_ways(value):
    pairs = [
        (2 * source + core, 2 * (source ^ (1 + core)) + core)
        for source in range(lax.axis_size("ctx"))
        for core in range(2)
    ]
    return lax.ppermute(value, ("ctx", "tp"), pairs)


def convolve(normed_cols, conv_weight):
    frames_here, dancers_here, features_here = normed_cols.shape
    wide = normed_cols.astype(jnp.float32)
    before = from_behind(normed_cols[frames_here - 2 :], "tm", 1).astype(jnp.float32)
    after = from_behind(normed_cols[0:2], "tm", -1).astype(jnp.float32)
    padded = jnp.concatenate([before, wide, after], axis=0)
    convolved = jnp.zeros((frames_here, dancers_here, features_here), jnp.float32)
    for offset in range(KERNEL):
        convolved = convolved + conv_weight[offset] * padded[offset : offset + frames_here]
    return convolved


def begin(sems, pairs):
    copies = [
        pltpu.make_async_copy(source, target, sems.at[n]) for n, (source, target) in enumerate(pairs)
    ]
    for copy in copies:
        copy.start()
    return copies


def end(copies):
    for copy in copies:
        copy.wait()


def slot(index, size):
    return pl.ds(pl.multiple_of(index * size, size), size)


def prepare_kernel(
    n_ctx, place, tokens, gain, w_up, w_query, w_key, w_value, full, half, first, second, sems
):
    ctx, tm, groups, tp = place[0], place[1], place[2], place[3]
    rows = tokens.shape[0]
    count = first.shape[0]
    edge = second.shape[0] - count
    pairs, column = [], 0
    for w in (w_up, w_query, w_key, w_value):
        size = w.shape[1] // n_ctx
        for step, out in enumerate((first, second)):
            source = w.at[slot(2 * groups + step, count), slot(ctx, size)]
            pairs.append((source, out.at[0:count, column : column + size]))
        column += size
    copies = begin(sems, pairs)
    values = tokens[...].astype(jnp.float32)
    square = jnp.mean(values * values, axis=-1, keepdims=True)
    full[...] = (values * lax.rsqrt(square + 1e-05) * gain[...]).astype(jnp.bfloat16)
    half[...] = full[slot(tp, rows // 2), :]
    columns = full.shape[1] // 2
    last_edge = full[rows - edge :, slot(tp, columns)]
    first_edge = full[0:edge, slot(tp, columns)]
    second[count:, 0:columns] = jnp.where(tm == 0, last_edge, first_edge)
    second[count:, columns:] = jnp.zeros((edge, second.shape[1] - columns), jnp.bfloat16)
    end(copies)


def convolve_kernel(per_frame, place, tokens, full, halo, taps, base, held):
    tm, tp = place[1], place[3]
    rows, columns = base.shape
    edge = 16
    margin = 2 * per_frame
    near = halo[halo.shape[0] - edge :, 0:columns].astype(jnp.float32)
    zeros = jnp.zeros((edge, columns), jnp.float32)
    held[0:edge, :] = jnp.where(tm == 1, near, zeros)
    held[edge : edge + rows, :] = full[:, slot(tp, columns)].astype(jnp.float32)
    held[edge + rows :, :] = jnp.where(tm == 0, near, zeros)
    total = tokens[:, slot(tp, columns)].astype(jnp.float32)
    for offset in range(KERNEL):
        start = edge - margin + offset * per_frame
        total += taps[offset : offset + 1, :] * held[start : start + rows, :]
    base[...] = total


def project_kernel(n_ctx, place, *refs):
    own, block, other_block, piece, other_piece = refs[:5]
    w_up, w_query, w_key, w_value, first, second, far_first, far_second = refs[5:13]
    acts, qkv = refs[13 : 13 + n_ctx], refs[13 + n_ctx]
    held, weights, sems = refs[14 + n_ctx :]
    ctx, tm, groups, tp = place[0], place[1], place[2], place[3]
    rows, count = own.shape[0], first.shape[0]
    pairs, column = [], 0
    for w in (w_up, w_query, w_key, w_value):
        size = w.shape[1] // n_ctx
        target = weights.at[slot(tm, w.shape[0]), column : column + size]
        pairs.append((w.at[:, slot(ctx, size)], target))
        column += size
    quarters = 4 * (1 - tm) + 2 * groups, 4 * (1 - tm) + 2 * (1 - groups)
    pairs += [
        (first, weights.at[slot(quarters[0], count)]),
        (second.at[0:count], weights.at[slot(quarters[0] + 1, count)]),
        (far_first, weights.at[slot(quarters[1], count)]),
        (far_second.at[0:count], weights.at[slot(quarters[1] + 1, count)]),
        (own, held.at[0:rows]),
        (block, held.at[slot(1 + tp, rows)]),
        (other_block, held.at[slot(2 - tp, rows)]),
        (piece, held.at[slot(6 + tp, rows // 2)]),
        (other_piece, held.at[slot(7 - tp, rows // 2)]),
    ]
    end(begin(sems, pairs))
    total = jnp.dot(held[...], weights[...], preferred_element_type=jnp.float32)
    hidden = acts[0].shape[1]
    activated = jax.nn.gelu(total[:, :hidden], approximate=True).astype(jnp.bfloat16)
    for d in range(n_ctx):
        acts[d][...] = activated[d * rows : (d + 1) * rows]
    qkv[...] = total[:, hidden:].astype(jnp.bfloat16)


def attend_kernel(n_ctx, i, place, mask, activated, qkv, out):
    ctx = place[0]
    rows, hidden = activated.shape
    wide = out.shape[1] - hidden
    lane_head = lax.broadcasted_iota(jnp.int32, (1, wide), 1) // HEAD_DIM
    queries = qkv[i * rows : (i + 1) * rows, 0:wide]
    keys = qkv[:, wide : 2 * wide]
    values = qkv[:, 2 * wide :]
    bias = jnp.concatenate(
        [
            jnp.full((1, rows), jnp.where(mask[0, ctx ^ j] > 0, 0.0, MASKED), jnp.float32)
            for j in range(n_ctx)
        ],
        axis=1,
    )
    result = jnp.zeros((rows, wide), jnp.float32)
    for head in range(wide // HEAD_DIM):
        one = jnp.where(lane_head == head, queries, jnp.zeros_like(queries))
        scores = lax.dot_general(
            one, keys, (((1,), (1,)), ((), ())), preferred_element_type=jnp.float32
        )
        scores = scores * 0.125 + bias
        peak = jnp.max(scores, axis=-1, keepdims=True)
        expo = jnp.exp(scores - peak)
        total = jnp.sum(expo, axis=-1, keepdims=True)
        mixed = jnp.dot(expo.astype(jnp.bfloat16), values, preferred_element_type=jnp.float32)
        result = jnp.where(lane_head == head, mixed / total, result)
    out[:, 0:hidden] = activated[...]
    out[:, hidden:] = result.astype(jnp.bfloat16)


def join_kernel(n_ctx, place, *refs):
    near_down, near_out, base = refs[:3]
    far_down, farther_down, far_out = refs[3:6]
    parts = refs[6 : 6 + n_ctx]
    keep, send, down, out, acts, atts, sems = refs[6 + n_ctx :]
    ctx, tm, groups, tp = place[0], place[1], place[2], place[3]
    hidden, wide = acts.shape[1] // n_ctx, atts.shape[1] // n_ctx
    count = far_down.shape[0]
    pairs = []
    for d in range(n_ctx):
        pairs.append((parts[d].at[:, 0:hidden], acts.at[:, slot(ctx ^ d, hidden)]))
        pairs.append((parts[d].at[:, hidden:], atts.at[:, slot(ctx ^ d, wide)]))
    pairs.append((far_out, out))
    pairs.append((far_down, down.at[slot(groups, count)]))
    pairs.append((farther_down, down.at[slot(1 - groups, count)]))
    copies = begin(sems, pairs)

    def dot(left, right):
        return jnp.dot(left[...], right[...], preferred_element_type=jnp.float32)

    end(copies[: 2 * n_ctx])
    near_sum = dot(acts, near_down) + dot(atts, near_out)
    end(copies[2 * n_ctx :])
    far_sum = dot(acts, down) + dot(atts, out)
    same = tm == tp
    keep[...] = jnp.where(same, near_sum, far_sum) + base[...]
    send[...] = jnp.where(same, far_sum, near_sum).astype(jnp.bfloat16)


SMEM = pl.BlockSpec(memory_space=pltpu.SMEM)
VMEM = pl.BlockSpec(memory_space=pltpu.VMEM)
ANY = pl.BlockSpec(memory_space=pl.ANY)


def call(kernel, name, outs, ins, scratch=(), flops=0, moved=1 << 20, transcendentals=0):
    specs, values = zip(*ins)
    return pl.pallas_call(
        kernel,
        out_shape=[jax.ShapeDtypeStruct(shape, dtype) for shape, dtype in outs],
        in_specs=list(specs),
        out_specs=[VMEM] * len(outs),
        scratch_shapes=list(scratch),
        compiler_params=pltpu.CompilerParams(vmem_limit_bytes=32 * 1024 * 1024),
        name=name,
        cost_estimate=pl.CostEstimate(
            flops=flops, bytes_accessed=moved, transcendentals=transcendentals
        ),
    )(*values)


def split_over_ctx(
    tokens, norm_gain, block_mask, w_query, w_key, w_value, w_out, w_up, w_down, conv_weight
):
    n_ctx = lax.axis_size("ctx")
    groups, ctx = lax.axis_index("groups"), lax.axis_index("ctx")
    tm, tp = lax.axis_index("tm"), lax.axis_index("tp")
    frames_here, dancers_here, width = tokens.shape
    rows = frames_here * dancers_here
    depth = w_query.shape[0]
    wide = w_query.shape[1] // n_ctx
    hidden = w_up.shape[1] // n_ctx
    columns = w_out.shape[1]
    packed = hidden + 3 * wide
    bf16, f32 = jnp.bfloat16, jnp.float32
    place = jnp.stack([ctx, tm, groups, tp]).astype(jnp.int32)
    token_rows = tokens.reshape(rows, width)
    quarter = depth // 4

    full, half, first, second = call(
        functools.partial(prepare_kernel, n_ctx),
        "prepare",
        [
            ((rows, width), bf16),
            ((rows // 2, width), bf16),
            ((quarter, packed), bf16),
            ((quarter + 16, packed), bf16),
        ],
        [(SMEM, place), (VMEM, token_rows), (VMEM, norm_gain.reshape(1, width))]
        + [(ANY, w) for w in (w_up, w_query, w_key, w_value)],
        [pltpu.SemaphoreType.DMA((8,))],
    )
    block = two_ways(full)
    piece = across(half, "ctx", 3)
    x_first = across(first, "tm", 1)
    x_second = across(second, "tm", 1)
    y_first = across(x_first, "groups", 1)
    y_second = across(x_second, "groups", 1)
    masks = [block_mask[0]] + [across(block_mask[0], "ctx", d) for d in range(1, n_ctx)]
    other_block = across(block, "tp", 1)
    other_piece = across(piece, "tp", 1)
    half_down = w_down.shape[0] // 2
    x_down = across(lax.dynamic_slice_in_dim(w_down, groups * half_down, half_down, 0), "tm", 1)
    y_down = across(x_down, "groups", 1)
    x_out = across(w_out, "tm", 1)

    (base,) = call(
        functools.partial(convolve_kernel, dancers_here),
        "convolve",
        [((rows, columns), f32)],
        [
            (SMEM, place),
            (VMEM, token_rows),
            (VMEM, full),
            (VMEM, x_second),
            (VMEM, conv_weight),
        ],
        [pltpu.VMEM((rows + 32, columns), f32)],
    )
    *acts, qkv = call(
        functools.partial(project_kernel, n_ctx),
        "project",
        [((rows, hidden), bf16)] * n_ctx + [((n_ctx * rows, 3 * wide), bf16)],
        [(SMEM, place)]
        + [(ANY, value) for value in (full, block, other_block, piece, other_piece)]
        + [(ANY, value) for value in (w_up, w_query, w_key, w_value)]
        + [(ANY, value) for value in (x_first, x_second, y_first, y_second)],
        [
            pltpu.VMEM((n_ctx * rows, width), bf16),
            pltpu.VMEM((width, packed), bf16),
            pltpu.SemaphoreType.DMA((13,)),
        ],
        flops=2 * n_ctx * rows * width * packed,
        moved=4 << 20,
        transcendentals=n_ctx * rows * hidden,
    )
    parts = [None] * n_ctx
    for i in (2, 3, 1, 0):
        (part,) = call(
            functools.partial(attend_kernel, n_ctx, i),
            "attend",
            [((rows, hidden + wide), bf16)],
            [(SMEM, place), (SMEM, masks[i]), (VMEM, acts[i]), (VMEM, qkv)],
            flops=4 * wide * n_ctx * rows * rows,
            transcendentals=(wide // HEAD_DIM) * n_ctx * rows * rows,
        )
        parts[i] = across(part, "ctx", i) if i else part
    keep, send = call(
        functools.partial(join_kernel, n_ctx),
        "join",
        [((rows, columns), f32), ((rows, columns), bf16)],
        [(SMEM, place), (VMEM, w_down), (VMEM, w_out), (VMEM, base)]
        + [(ANY, value) for value in (x_down, y_down, x_out)]
        + [(ANY, value) for value in parts],
        [
            pltpu.VMEM(w_down.shape, bf16),
            pltpu.VMEM(w_out.shape, bf16),
            pltpu.VMEM((rows, w_down.shape[0]), bf16),
            pltpu.VMEM((rows, w_out.shape[0]), bf16),
            pltpu.SemaphoreType.DMA((2 * n_ctx + 3,)),
        ],
        flops=4 * rows * columns * n_ctx * (hidden + wide),
        moved=4 << 20,
    )
    other = across(send, "tp", 1).astype(f32)
    return (keep + other).astype(bf16).reshape(frames_here, dancers_here, columns)


def gather_all(
    tokens, norm_gain, block_mask, w_query, w_key, w_value, w_out, w_up, w_down, conv_weight
):
    frames_here, dancers_here, width = tokens.shape
    rows_here = frames_here * dancers_here
    normed_grid = rms_norm(tokens, norm_gain)
    normed = normed_grid.reshape(rows_here, width)
    query_sum, key_sum, value_sum, hidden = tuple(
        jnp.dot(
            normed,
            lax.all_gather(piece, "tm", axis=0, tiled=True),
            preferred_element_type=jnp.float32,
        )
        for piece in (w_query, w_key, w_value, w_up)
    )
    local_heads = query_sum.shape[1] // HEAD_DIM
    queries = query_sum.astype(jnp.bfloat16).reshape(rows_here, local_heads, HEAD_DIM)
    grid = (frames_here, dancers_here, local_heads * HEAD_DIM)
    key_piece = lax.all_gather(
        key_sum.astype(jnp.bfloat16).reshape(grid), "ctx", axis=1, tiled=True
    )
    value_piece = lax.all_gather(
        value_sum.astype(jnp.bfloat16).reshape(grid), "ctx", axis=1, tiled=True
    )
    count = key_piece.shape[1]
    allowed = jnp.tile(jnp.repeat(block_mask[0, 0].astype(jnp.float32), dancers_here), frames_here)
    key_rows = key_piece.reshape(frames_here * count, local_heads, HEAD_DIM)
    value_rows = value_piece.reshape(frames_here * count, local_heads, HEAD_DIM)
    scores = (
        jnp.einsum("qhd,khd->hqk", queries, key_rows, preferred_element_type=jnp.float32) * 0.125
    )
    scores = jnp.where(allowed[None, None, :] > 0, scores, MASKED)
    expo = jnp.exp(scores - jnp.max(scores, axis=-1, keepdims=True)) * allowed[None, None, :]
    total = jnp.sum(expo, axis=-1)
    mixed = jnp.einsum(
        "hqk,khd->hqd", expo.astype(jnp.bfloat16), value_rows, preferred_element_type=jnp.float32
    )
    attended = (
        (mixed / total[:, :, None])
        .transpose(1, 0, 2)
        .reshape(rows_here, local_heads * HEAD_DIM)
        .astype(jnp.bfloat16)
    )
    activated = jax.nn.gelu(hidden, approximate=True).astype(jnp.bfloat16)
    out_full = lax.all_gather(w_out, "tm", axis=1, tiled=True)
    down_full = lax.all_gather(w_down, "tm", axis=1, tiled=True)
    branches = jnp.dot(attended, out_full, preferred_element_type=jnp.float32)
    branches = branches + jnp.dot(activated, down_full, preferred_element_type=jnp.float32)
    mine = lax.psum_scatter(
        branches.astype(jnp.bfloat16), "tp", scatter_dimension=1, tiled=True
    ).astype(jnp.float32)
    features_here = mine.shape[1]
    first_feature = lax.axis_index("tp") * features_here
    normed_cols = lax.dynamic_slice_in_dim(normed_grid, first_feature, features_here, 2)
    token_cols = lax.dynamic_slice_in_dim(tokens, first_feature, features_here, 2)
    result = (
        token_cols.astype(jnp.float32)
        + mine.reshape(frames_here, dancers_here, features_here)
        + convolve(normed_cols, conv_weight)
    )
    return result.astype(jnp.bfloat16)


def solution(mesh):
    n_ctx, n_tm = mesh.shape["ctx"], mesh.shape["tm"]

    def on_device(*arrays):
        local_heads = arrays[3].shape[1] // HEAD_DIM
        pairs = n_tm == 2 and mesh.shape["groups"] == 2 and mesh.shape["tp"] == 2
        even = n_ctx == 4 and local_heads % (2 * n_ctx) == 0
        chosen = split_over_ctx if pairs and even else gather_all
        return chosen(*arrays)

    placed = (
        P(("groups", "tm"), "ctx", None),
        P(),
        P(("groups", "tm"), "ctx", None),
        P("tm", "tp"),
        P("tm", "tp"),
        P("tm", "tp"),
        P("tp", "tm"),
        P("tm", "tp"),
        P("tp", "tm"),
        P(None, "tp"),
    )
    return jax.shard_map(
        on_device,
        mesh=mesh,
        in_specs=placed,
        out_specs=P(("groups", "tm"), "ctx", "tp"),
        check_vma=False,
    )
```

time: 190 us -> 67.1 us (0.35)
  waiting for transfers between devices: 121 us -> 25.8 us
  blocking collectives: 31.3 us -> 0 us
  starting transfers between devices: 3.75 us -> 23.9 us
  between operations: 13.8 us -> 0.17 us
  matrix products: 11.6 us -> 0 us
  Pallas kernels: 0 us -> 11.3 us
  other arithmetic: 3.36 us -> 0.11 us
    all_gather x6 -> x0, waiting for transfers between devices: 113 us -> none  [the longest x1 34.5 us: on_device(): lax.all_gather(w_up, 'tm', axis=0, tiled=True)]
    all_gather x2 -> x0, blocking collectives: 31.3 us -> none  [the longest x1 15.6 us: on_device(): key_piece = lax.all_gather(key_grid, 'ctx', axis=1, tiled=True)]
    ppermute x2 -> x18, waiting for transfers between devices: 4.23 us -> 25.8 us  [the longest x17 25.8 us: across(): lax.ppermute(value, axis, [(source, source ^ step) for source in range(co...]
    ppermute x2 -> x18, starting transfers between devices: 3.52 us -> 23.9 us  [the longest x17 22.2 us: across(): lax.ppermute(value, axis, [(source, source ^ step) for source in range(co...]
    dot_general x8 -> x0, matrix products: 11.6 us -> none  [the longest x3 4.59 us: on_device(): jnp.dot(normed, piece_one, preferred_element_type=jnp.float32)]
    pallas_call x0 -> x8, Pallas kernels: none -> 11.3 us  [call(): pl.pallas_call(kernel, out_shape=[jax.ShapeDtypeStruct(shape, dtype) for...]
    unnamed x7 -> x0, waiting for transfers between devices: 3.68 us -> none
    unnamed x14 -> x18, local copies, waits for them, and re-layouts: 0.63 us -> 2.7 us
  transfers between devices with their start and end apart: 9 -> 18, of which waited for: 7 -> 5; matrix products, arithmetic and copies ran while one was open for 8% -> 2% of each run, Pallas kernels for 0% -> 14%
where the time goes in v2:
time: 67.1 us; the launch traced here: 66.8 us
  waiting for transfers between devices  25.8 us (38%)
  starting transfers between devices  23.9 us (36%)
  Pallas kernels  11.3 us (17%)
  local copies, waits for them, and re-layouts  5.63 us (8%)
    ppermute x17, waiting for transfers between devices, across(): lax.ppermute(value, axis, [(source, source ^ step) for source in range(co...  25.8 us
    ppermute x17, starting transfers between devices, across(): lax.ppermute(value, axis, [(source, source ^ step) for source in range(co...  22.2 us
    pallas_call x8, Pallas kernels, call(): pl.pallas_call(kernel, out_shape=[jax.ShapeDtypeStruct(shape, dtype) for...  11.3 us
    unnamed x18, local copies, waits for them, and re-layouts  2.7 us
    ppermute x1, starting transfers between devices, two_ways(): return lax.ppermute(value, ('ctx', 'tp'), pairs)  1.64 us
  transfers between devices with their start and end apart: 18, of which 5 were waited for; matrix products, arithmetic and copies ran while one was open for 2% of the time, Pallas kernels for 14%

profile of v2, /device:TPU:0, one launch (start us, length us, event | category | flops | bytes accessed | tf_op | source)
XLA Modules:
  0.0 66.8 jit_solution(4669141395722322071)
XLA Ops:
  0.0 1.2 %constant_dynamic-slice_fusion = bf16[512,512]{1,0:T(8,128)(2,1)S(1)} fusion(bf16[1024,512]{1,0:T(8,128)(2,1)} %refs_0_.1, s32[]{:T(128)S(6)} %select_n.3), kind=kLoop, calls=%fused_computation.2 | loop fusion | bytes 1048580 | tf_op jit(solution)/shard_map/dynamic_slice | solution.py:271
  1.2 3.0 %collective-permute-start.1 = (bf16[512,512]{1,0:T(8,128)(2,1)S(1)}, bf16[512,512]{1,0:T(8,128)(2,1)S(1)}, u32[]{:S(2)}, u32[]{:S(2)}) collective-permute-start(bf16[512,512]{1,0:T(8,128)(2,1)S(1)} %constant_dynamic-slice_fusion), channel_id=1, source_target_pairs={{0,2},{2,0},{1,3},{3,1},{4,6},{6,4},{5,7},{7,5},{8,10},{10,8},{9,1... | collective-permute-start | bytes 1572872 | tf_op jit(solution)/shard_map/ppermute | solution.py:29
  4.2 1.0 %reshape.9.tokens = bf16[128,1024]{1,0:T(8,128)(2,1)S(1)} reshape(bf16[64,2,1024]{2,1,0:T(2,128)(2,1)} %param.10) | data formatting | bytes 524288 | tf_op jit(solution)/shard_map/reshape | solution.py:245
  5.9 1.0 %copy-done.3 = bf16[512,512]{1,0:T(8,128)(2,1)S(1)} copy-done((bf16[512,512]{1,0:T(8,128)(2,1)S(1)}, bf16[512,512]{1,0:T(8,128)(2,1)}, u32[]{:S(2)}) %copy-start.3) | copy-done | bytes 524312
  7.0 1.0 %copy-done.4 = bf16[512,512]{1,0:T(8,128)(2,1)S(1)} copy-done((bf16[512,512]{1,0:T(8,128)(2,1)S(1)}, bf16[512,512]{1,0:T(8,128)(2,1)}, u32[]{:S(2)}) %copy-start.4) | copy-done | bytes 524312
  8.9 1.6 %collective-permute-start.4 = (bf16[128,1024]{1,0:T(8,128)(2,1)S(1)}, bf16[128,1024]{1,0:T(8,128)(2,1)S(1)}, u32[]{:S(2)}, u32[]{:S(2)}) collective-permute-start(bf16[128,1024]{1,0:T(8,128)(2,1)S(1)} %get-tuple-element.16.full.refs_0_), channel_id=1, source_target_pairs={{0,4},{1,9},{4,0},{5,13},{8,12},{9,1},{12,8},{13,5},{2,6},{3,11},{... | collective-permute-start | bytes 786440 | tf_op jit(solution)/shard_map/ppermute | solution.py:38
  10.5 2.5 %collective-permute-start.6 = (bf16[64,1024]{1,0:T(8,128)(2,1)S(1)}, bf16[64,1024]{1,0:T(8,128)(2,1)S(1)}, u32[]{:S(2)}, u32[]{:S(2)}) collective-permute-start(bf16[64,1024]{1,0:T(8,128)(2,1)S(1)} %get-tuple-element.18), channel_id=1, source_target_pairs={{0,12},{4,8},{8,4},{12,0},{1,13},{5,9},{9,5},{13,1},{2,14},{6,10},... | collective-permute-start | bytes 393224 | tf_op jit(solution)/shard_map/ppermute | solution.py:29
  13.5 1.5 %collective-permute-start = (bf16[144,640]{1,0:T(8,128)(2,1)S(1)}, bf16[144,640]{1,0:T(8,128)(2,1)S(1)}, u32[]{:S(2)}, u32[]{:S(2)}) collective-permute-start(bf16[144,640]{1,0:T(8,128)(2,1)S(1)} %get-tuple-element.17), channel_id=1, source_target_pairs={{0,2},{2,0},{1,3},{3,1},{4,6},{6,4},{5,7},{7,5},{8,10},{10,8},{9,1... | collective-permute-start | bytes 552968 | tf_op jit(solution)/shard_map/ppermute | solution.py:29
  15.0 6.5 %collective-permute-done.6.refs_3_ = bf16[64,1024]{1,0:T(8,128)(2,1)S(1)} collective-permute-done((bf16[64,1024]{1,0:T(8,128)(2,1)S(1)}, bf16[64,1024]{1,0:T(8,128)(2,1)S(1)}, u32[]{:S(2)}, u32[]{:S(2)}) %collective-permute-start.6) | collective-permute-done | bytes 131104 | tf_op jit(solution)/shard_map/ppermute | solution.py:29
  22.0 1.5 %collective-permute-start.2 = (bf16[512,512]{1,0:T(8,128)(2,1)S(1)}, bf16[512,512]{1,0:T(8,128)(2,1)S(1)}, u32[]{:S(2)}, u32[]{:S(2)}) collective-permute-start(bf16[512,512]{1,0:T(8,128)(2,1)S(1)} %collective-permute-done.1.refs_3_), channel_id=1, source_target_pairs={{0,16},{16,0},{1,17},{17,1},{2,18},{18,2},{3,19},{19,3},{4,20},{20... | collective-permute-start | bytes 1572872 | tf_op jit(solution)/shard_map/ppermute | solution.py:29
  24.4 2.1 %collective-permute-start.10 = (bf16[144,640]{1,0:T(8,128)(2,1)S(1)}, bf16[144,640]{1,0:T(8,128)(2,1)S(1)}, u32[]{:S(2)}, u32[]{:S(2)}) collective-permute-start(bf16[144,640]{1,0:T(8,128)(2,1)S(1)} %collective-permute-done.halo.refs_10_), channel_id=1, source_target_pairs={{0,16},{16,0},{1,17},{17,1},{2,18},{18,2},{3,19},{19,3},{4,20},{20... | collective-permute-start | bytes 552968 | tf_op jit(solution)/shard_map/ppermute | solution.py:29
  26.5 14.8 %collective-permute-done.9.refs_11_ = bf16[128,640]{1,0:T(8,128)(2,1)S(1)} collective-permute-done((bf16[128,640]{1,0:T(8,128)(2,1)S(1)}, bf16[128,640]{1,0:T(8,128)(2,1)S(1)}, u32[]{:S(2)}, u32[]{:S(2)}) %collective-permute-start.9) | collective-permute-done | bytes 163872 | tf_op jit(solution)/shard_map/ppermute | solution.py:29
  41.3 4.0 %collective-permute-start.15 = (s32[1,4]{1,0:T(1,128)S(1)}, s32[1,4]{1,0:T(1,128)S(1)}, u32[]{:S(2)}, u32[]{:S(2)}) collective-permute-start(s32[1,4]{1,0:T(1,128)S(1)} %bitcast.7), channel_id=1, source_target_pairs={{0,12},{4,8},{8,4},{12,0},{1,13},{5,9},{9,5},{13,1},{2,14},{6,10},... | collective-permute-start | bytes 56 | tf_op jit(solution)/shard_map/ppermute | solution.py:29
  45.3 0.9 %collective-permute-start.13 = (s32[1,4]{1,0:T(1,128)S(1)}, s32[1,4]{1,0:T(1,128)S(1)}, u32[]{:S(2)}, u32[]{:S(2)}) collective-permute-start(s32[1,4]{1,0:T(1,128)S(1)} %bitcast.8), channel_id=1, source_target_pairs={{0,8},{4,12},{8,0},{12,4},{1,9},{5,13},{9,1},{13,5},{2,10},{6,14},... | collective-permute-start | bytes 56 | tf_op jit(solution)/shard_map/ppermute | solution.py:29
  46.7 3.1 %project.1 = (bf16[128,256]{1,0:T(8,128)(2,1)S(1)}, bf16[128,256]{1,0:T(8,128)(2,1)S(1)}, bf16[128,256]{1,0:T(8,128)(2,1)S(1)}, bf16[128,256]{1,0:T(8,128)(2,1)S(1)}, bf16[512,384]{1,0:T(8,128)(2,1)S(1)}) custom-call(s32[4]{0:T(128)S(1)} %pad_add_fusion.place, bf16[128,1024]{1,0:T(8,128)(2,1)S(1)} %get-tuple-element.16.full.refs_0_, ...), custom_call_target="tpu_custom_call" | custom-call | flops 671088640 | bytes 4194304 | tf_op jit(solution)/shard_map/project/pallas_call | solution.py:216
  49.8 1.2 %attend.7 = bf16[128,384]{1,0:T(8,128)(2,1)S(1)} custom-call(s32[4]{0:T(128)S(1)} %pad_add_fusion.place, s32[1,4]{1,0:T(1,128)S(1)} %collective-permute-done.15.mask, bf16[128,256]{1,0:T(8,128)(2,1)S(1)} %get-tuple-element.24.activated, bf16[512,384]{1,0:T(8,128)(2,1)S(1)} %get-tuple-element.21.qkv), custom_call_target="tpu_custom_call" | custom-call | flops 33554432 | bytes 1048576 | tf_op jit(solution)/shard_map/attend/pallas_call | solution.py:216
  51.1 3.0 %collective-permute-start.16 = (bf16[128,384]{1,0:T(8,128)(2,1)S(1)}, bf16[128,384]{1,0:T(8,128)(2,1)S(1)}, u32[]{:S(2)}, u32[]{:S(2)}) collective-permute-start(bf16[128,384]{1,0:T(8,128)(2,1)S(1)} %attend.7), channel_id=1, source_target_pairs={{0,12},{4,8},{8,4},{12,0},{1,13},{5,9},{9,5},{13,1},{2,14},{6,10},... | collective-permute-start | bytes 294920 | tf_op jit(solution)/shard_map/ppermute | solution.py:29
  54.1 1.2 %attend.6 = bf16[128,384]{1,0:T(8,128)(2,1)S(1)} custom-call(s32[4]{0:T(128)S(1)} %pad_add_fusion.place, s32[1,4]{1,0:T(1,128)S(1)} %collective-permute-done.13.mask, bf16[128,256]{1,0:T(8,128)(2,1)S(1)} %get-tuple-element.23.activated, bf16[512,384]{1,0:T(8,128)(2,1)S(1)} %get-tuple-element.21.qkv), custom_call_target="tpu_custom_call" | custom-call | flops 33554432 | bytes 1048576 | tf_op jit(solution)/shard_map/attend/pallas_call | solution.py:216
  55.4 1.2 %attend.5 = bf16[128,384]{1,0:T(8,128)(2,1)S(1)} custom-call(s32[4]{0:T(128)S(1)} %pad_add_fusion.place, s32[1,4]{1,0:T(1,128)S(1)} %collective-permute-done.11.mask, bf16[128,256]{1,0:T(8,128)(2,1)S(1)} %get-tuple-element.22.activated, bf16[512,384]{1,0:T(8,128)(2,1)S(1)} %get-tuple-element.21.qkv), custom_call_target="tpu_custom_call" | custom-call | flops 33554432 | bytes 1048576 | tf_op jit(solution)/shard_map/attend/pallas_call | solution.py:216
  56.6 1.5 %collective-permute-start.12 = (bf16[128,384]{1,0:T(8,128)(2,1)S(1)}, bf16[128,384]{1,0:T(8,128)(2,1)S(1)}, u32[]{:S(2)}, u32[]{:S(2)}) collective-permute-start(bf16[128,384]{1,0:T(8,128)(2,1)S(1)} %attend.5), channel_id=1, source_target_pairs={{0,4},{4,0},{8,12},{12,8},{1,5},{5,1},{9,13},{13,9},{2,6},{6,2},{1... | collective-permute-start | bytes 294920 | tf_op jit(solution)/shard_map/ppermute | solution.py:29
  58.9 1.2 %attend.4.refs_6_ = bf16[128,384]{1,0:T(8,128)(2,1)S(1)} custom-call(s32[4]{0:T(128)S(1)} %pad_add_fusion.place, s32[1,4]{1,0:T(1,128)S(1)} %bitcast.10, bf16[128,256]{1,0:T(8,128)(2,1)S(1)} %get-tuple-element.20.activated, bf16[512,384]{1,0:T(8,128)(2,1)S(1)} %get-tuple-element.21.qkv), custom_call_target="tpu_custom_call" | custom-call | flops 33554432 | bytes 1048576 | tf_op jit(solution)/shard_map/attend/pallas_call | solution.py:216
  60.2 2.8 %collective-permute-done.14.refs_8_ = bf16[128,384]{1,0:T(8,128)(2,1)S(1)} collective-permute-done((bf16[128,384]{1,0:T(8,128)(2,1)S(1)}, bf16[128,384]{1,0:T(8,128)(2,1)S(1)}, u32[]{:S(2)}, u32[]{:S(2)}) %collective-permute-start.14) | collective-permute-done | bytes 98336 | tf_op jit(solution)/shard_map/ppermute | solution.py:29
  63.0 1.6 %join.1 = (f32[128,512]{1,0:T(8,128)S(1)}, bf16[128,512]{1,0:T(8,128)(2,1)S(1)}) custom-call(s32[4]{0:T(128)S(1)} %pad_add_fusion.place, bf16[1024,512]{1,0:T(8,128)(2,1)S(1)} %copy-done.1, bf16[512,512]{1,0:T(8,128)(2,1)S(1)} %copy-done.5, f32[128,512]{1,0:T(8,128)S(1)} %convolve.1.refs_2_, bf16[512,512]{1,0:T(8,128)(2,1)S(1)} %collective-permute-done.1.refs_3_, ...), custom_call_target="tpu_custom_call" | custom-call | flops 402653184 | bytes 4194304 | tf_op jit(solution)/shard_map/join/pallas_call | solution.py:216
  64.7 1.3 %collective-permute-done.17 = bf16[128,512]{1,0:T(8,128)(2,1)S(1)} collective-permute-done((bf16[128,512]{1,0:T(8,128)(2,1)S(1)}, bf16[128,512]{1,0:T(8,128)(2,1)S(1)}, u32[]{:S(2)}, u32[]{:S(2)}) %collective-permute-start.17) | collective-permute-done | bytes 131104 | tf_op jit(solution)/shard_map/ppermute | solution.py:29
  (43 shorter events, 5.8 us)
Async XLA Ops:
  0.0 5.3 %copy-start = (bf16[512,1024]{1,0:T(8,128)(2,1)S(1)}, bf16[512,1024]{1,0:T(8,128)(2,1)}, u32[]{:S(2)}) copy-start(bf16[512,1024]{1,0:T(8,128)(2,1)} %refs_5_.1) | copy-start | bytes 3145732
  1.2 4.2 %copy-start.2 = (bf16[512,512]{1,0:T(8,128)(2,1)S(1)}, bf16[512,512]{1,0:T(8,128)(2,1)}, u32[]{:S(2)}) copy-start(bf16[512,512]{1,0:T(8,128)(2,1)} %refs_6_.1) | copy-start | bytes 1572868
  1.2 20.8 %collective-permute-start.1 = (bf16[512,512]{1,0:T(8,128)(2,1)S(1)}, bf16[512,512]{1,0:T(8,128)(2,1)S(1)}, u32[]{:S(2)}, u32[]{:S(2)}) collective-permute-start(bf16[512,512]{1,0:T(8,128)(2,1)S(1)} %constant_dynamic-slice_fusion), channel_id=1, source_target_pairs={{0,2},{2,0},{1,3},{3,1},{4,6},{6,4},{5,7},{7,5},{8,10},{10,8},{9,1... | collective-permute-start | bytes 1572872 | tf_op jit(solution)/shard_map/ppermute | solution.py:29
  8.0 13.5 %copy-start.5 = (bf16[512,512]{1,0:T(8,128)(2,1)S(1)}, bf16[512,512]{1,0:T(8,128)(2,1)}, u32[]{:S(2)}) copy-start(bf16[512,512]{1,0:T(8,128)(2,1)} %refs_1_.1) | copy-start | bytes 1572868
  8.9 14.7 %collective-permute-start.4 = (bf16[128,1024]{1,0:T(8,128)(2,1)S(1)}, bf16[128,1024]{1,0:T(8,128)(2,1)S(1)}, u32[]{:S(2)}, u32[]{:S(2)}) collective-permute-start(bf16[128,1024]{1,0:T(8,128)(2,1)S(1)} %get-tuple-element.16.full.refs_0_), channel_id=1, source_target_pairs={{0,4},{1,9},{4,0},{5,13},{8,12},{9,1},{12,8},{13,5},{2,6},{3,11},{... | collective-permute-start | bytes 786440 | tf_op jit(solution)/shard_map/ppermute | solution.py:38
  10.5 11.0 %collective-permute-start.6 = (bf16[64,1024]{1,0:T(8,128)(2,1)S(1)}, bf16[64,1024]{1,0:T(8,128)(2,1)S(1)}, u32[]{:S(2)}, u32[]{:S(2)}) collective-permute-start(bf16[64,1024]{1,0:T(8,128)(2,1)S(1)} %get-tuple-element.18), channel_id=1, source_target_pairs={{0,12},{4,8},{8,4},{12,0},{1,13},{5,9},{9,5},{13,1},{2,14},{6,10},... | collective-permute-start | bytes 393224 | tf_op jit(solution)/shard_map/ppermute | solution.py:29
  13.0 10.5 %collective-permute-start.8 = (bf16[128,640]{1,0:T(8,128)(2,1)S(1)}, bf16[128,640]{1,0:T(8,128)(2,1)S(1)}, u32[]{:S(2)}, u32[]{:S(2)}) collective-permute-start(bf16[128,640]{1,0:T(8,128)(2,1)S(1)} %get-tuple-element.19), channel_id=1, source_target_pairs={{0,2},{2,0},{1,3},{3,1},{4,6},{6,4},{5,7},{7,5},{8,10},{10,8},{9,1... | collective-permute-start | bytes 491528 | tf_op jit(solution)/shard_map/ppermute | solution.py:29
  13.5 27.8 %copy-start.8 = (s32[1,1,4]{2,1,0:T(1,128)S(1)}, s32[1,1,4]{2,1,0:T(1,128)}, u32[]{:S(2)}) copy-start(s32[1,1,4]{2,1,0:T(1,128)} %param.12) | copy-start | bytes 52
  13.5 10.9 %collective-permute-start = (bf16[144,640]{1,0:T(8,128)(2,1)S(1)}, bf16[144,640]{1,0:T(8,128)(2,1)S(1)}, u32[]{:S(2)}, u32[]{:S(2)}) collective-permute-start(bf16[144,640]{1,0:T(8,128)(2,1)S(1)} %get-tuple-element.17), channel_id=1, source_target_pairs={{0,2},{2,0},{1,3},{3,1},{4,6},{6,4},{5,7},{7,5},{8,10},{10,8},{9,1... | collective-permute-start | bytes 552968 | tf_op jit(solution)/shard_map/ppermute | solution.py:29
  21.5 38.7 %collective-permute-start.3 = (bf16[512,512]{1,0:T(8,128)(2,1)S(1)}, bf16[512,512]{1,0:T(8,128)(2,1)S(1)}, u32[]{:S(2)}, u32[]{:S(2)}) collective-permute-start(bf16[512,512]{1,0:T(8,128)(2,1)S(1)} %copy-done.5), channel_id=1, source_target_pairs={{0,2},{2,0},{1,3},{3,1},{4,6},{6,4},{5,7},{7,5},{8,10},{10,8},{9,1... | collective-permute-start | bytes 1572872 | tf_op jit(solution)/shard_map/ppermute | solution.py:29
  22.0 41.0 %collective-permute-start.2 = (bf16[512,512]{1,0:T(8,128)(2,1)S(1)}, bf16[512,512]{1,0:T(8,128)(2,1)S(1)}, u32[]{:S(2)}, u32[]{:S(2)}) collective-permute-start(bf16[512,512]{1,0:T(8,128)(2,1)S(1)} %collective-permute-done.1.refs_3_), channel_id=1, source_target_pairs={{0,16},{16,0},{1,17},{17,1},{2,18},{18,2},{3,19},{19,3},{4,20},{20... | collective-permute-start | bytes 1572872 | tf_op jit(solution)/shard_map/ppermute | solution.py:29
  23.5 2.9 %collective-permute-start.7 = (bf16[64,1024]{1,0:T(8,128)(2,1)S(1)}, bf16[64,1024]{1,0:T(8,128)(2,1)S(1)}, u32[]{:S(2)}, u32[]{:S(2)}) collective-permute-start(bf16[64,1024]{1,0:T(8,128)(2,1)S(1)} %collective-permute-done.6.refs_3_), channel_id=1, source_target_pairs={{0,1},{1,0},{2,3},{3,2},{4,5},{5,4},{6,7},{7,6},{8,9},{9,8},{10,11... | collective-permute-start | bytes 393224 | tf_op jit(solution)/shard_map/ppermute | solution.py:29
  23.6 22.6 %collective-permute-start.5 = (bf16[128,1024]{1,0:T(8,128)(2,1)S(1)}, bf16[128,1024]{1,0:T(8,128)(2,1)S(1)}, u32[]{:S(2)}, u32[]{:S(2)}) collective-permute-start(bf16[128,1024]{1,0:T(8,128)(2,1)S(1)} %collective-permute-done.4.refs_1_), channel_id=1, source_target_pairs={{0,1},{1,0},{2,3},{3,2},{4,5},{5,4},{6,7},{7,6},{8,9},{9,8},{10,11... | collective-permute-start | bytes 786440 | tf_op jit(solution)/shard_map/ppermute | solution.py:29
  24.4 20.9 %collective-permute-start.10 = (bf16[144,640]{1,0:T(8,128)(2,1)S(1)}, bf16[144,640]{1,0:T(8,128)(2,1)S(1)}, u32[]{:S(2)}, u32[]{:S(2)}) collective-permute-start(bf16[144,640]{1,0:T(8,128)(2,1)S(1)} %collective-permute-done.halo.refs_10_), channel_id=1, source_target_pairs={{0,16},{16,0},{1,17},{17,1},{2,18},{18,2},{3,19},{19,3},{4,20},{20... | collective-permute-start | bytes 552968 | tf_op jit(solution)/shard_map/ppermute | solution.py:29
  26.5 14.8 %collective-permute-start.9 = (bf16[128,640]{1,0:T(8,128)(2,1)S(1)}, bf16[128,640]{1,0:T(8,128)(2,1)S(1)}, u32[]{:S(2)}, u32[]{:S(2)}) collective-permute-start(bf16[128,640]{1,0:T(8,128)(2,1)S(1)} %collective-permute-done.8.refs_9_), channel_id=1, source_target_pairs={{0,16},{16,0},{1,17},{17,1},{2,18},{18,2},{3,19},{19,3},{4,20},{20... | collective-permute-start | bytes 491528 | tf_op jit(solution)/shard_map/ppermute | solution.py:29
  41.3 8.5 %collective-permute-start.15 = (s32[1,4]{1,0:T(1,128)S(1)}, s32[1,4]{1,0:T(1,128)S(1)}, u32[]{:S(2)}, u32[]{:S(2)}) collective-permute-start(s32[1,4]{1,0:T(1,128)S(1)} %bitcast.7), channel_id=1, source_target_pairs={{0,12},{4,8},{8,4},{12,0},{1,13},{5,9},{9,5},{13,1},{2,14},{6,10},... | collective-permute-start | bytes 56 | tf_op jit(solution)/shard_map/ppermute | solution.py:29
  45.3 8.8 %collective-permute-start.13 = (s32[1,4]{1,0:T(1,128)S(1)}, s32[1,4]{1,0:T(1,128)S(1)}, u32[]{:S(2)}, u32[]{:S(2)}) collective-permute-start(s32[1,4]{1,0:T(1,128)S(1)} %bitcast.8), channel_id=1, source_target_pairs={{0,8},{4,12},{8,0},{12,4},{1,9},{5,13},{9,1},{13,5},{2,10},{6,14},... | collective-permute-start | bytes 56 | tf_op jit(solution)/shard_map/ppermute | solution.py:29
  46.1 9.2 %collective-permute-start.11 = (s32[1,4]{1,0:T(1,128)S(1)}, s32[1,4]{1,0:T(1,128)S(1)}, u32[]{:S(2)}, u32[]{:S(2)}) collective-permute-start(s32[1,4]{1,0:T(1,128)S(1)} %bitcast.9), channel_id=1, source_target_pairs={{0,4},{4,0},{8,12},{12,8},{1,5},{5,1},{9,13},{13,9},{2,6},{6,2},{1... | collective-permute-start | bytes 56 | tf_op jit(solution)/shard_map/ppermute | solution.py:29
  51.1 9.1 %collective-permute-start.16 = (bf16[128,384]{1,0:T(8,128)(2,1)S(1)}, bf16[128,384]{1,0:T(8,128)(2,1)S(1)}, u32[]{:S(2)}, u32[]{:S(2)}) collective-permute-start(bf16[128,384]{1,0:T(8,128)(2,1)S(1)} %attend.7), channel_id=1, source_target_pairs={{0,12},{4,8},{8,4},{12,0},{1,13},{5,9},{9,5},{13,1},{2,14},{6,10},... | collective-permute-start | bytes 294920 | tf_op jit(solution)/shard_map/ppermute | solution.py:29
  54.1 4.0 %copy-start.6 = (f32[5,512]{1,0:T(8,128)S(1)}, f32[5,512]{1,0:T(8,128)}, u32[]{:S(2)}) copy-start(f32[5,512]{1,0:T(8,128)} %taps.1) | copy-start | bytes 30724
  55.3 7.7 %collective-permute-start.14 = (bf16[128,384]{1,0:T(8,128)(2,1)S(1)}, bf16[128,384]{1,0:T(8,128)(2,1)S(1)}, u32[]{:S(2)}, u32[]{:S(2)}) collective-permute-start(bf16[128,384]{1,0:T(8,128)(2,1)S(1)} %attend.6), channel_id=1, source_target_pairs={{0,8},{4,12},{8,0},{12,4},{1,9},{5,13},{9,1},{13,5},{2,10},{6,14},... | collective-permute-start | bytes 294920 | tf_op jit(solution)/shard_map/ppermute | solution.py:29
  55.4 7.6 %copy-start.1 = (bf16[1024,512]{1,0:T(8,128)(2,1)S(1)}, bf16[1024,512]{1,0:T(8,128)(2,1)}, u32[]{:S(2)}) copy-start(bf16[1024,512]{1,0:T(8,128)(2,1)} %refs_0_.1) | copy-start | bytes 3145732
  56.6 6.4 %collective-permute-start.12 = (bf16[128,384]{1,0:T(8,128)(2,1)S(1)}, bf16[128,384]{1,0:T(8,128)(2,1)S(1)}, u32[]{:S(2)}, u32[]{:S(2)}) collective-permute-start(bf16[128,384]{1,0:T(8,128)(2,1)S(1)} %attend.5), channel_id=1, source_target_pairs={{0,4},{4,0},{8,12},{12,8},{1,5},{5,1},{9,13},{13,9},{2,6},{6,2},{1... | collective-permute-start | bytes 294920 | tf_op jit(solution)/shard_map/ppermute | solution.py:29
  64.6 1.4 %collective-permute-start.17 = (bf16[128,512]{1,0:T(8,128)(2,1)S(1)}, bf16[128,512]{1,0:T(8,128)(2,1)S(1)}, u32[]{:S(2)}, u32[]{:S(2)}) collective-permute-start(bf16[128,512]{1,0:T(8,128)(2,1)S(1)} %get-tuple-element.26), channel_id=1, source_target_pairs={{0,1},{1,0},{2,3},{3,2},{4,5},{5,4},{6,7},{7,6},{8,9},{9,8},{10,11... | collective-permute-start | bytes 393224 | tf_op jit(solution)/shard_map/ppermute | solution.py:29
  (3 other events, 2.8 us)

commit v3 on v2

--- a/solution.py
+++ b/solution.py
@@ -10,6 +10,8 @@
 HEAD_DIM = 64
 KERNEL = 5
 MASKED = -1e30
+LANES = 128
+AXES = ("ctx", "tm", "groups", "tp")
 
 
 def from_behind(value, axis, steps):
@@ -29,9 +31,9 @@
     return lax.ppermute(value, axis, [(source, source ^ step) for source in range(count)])
 
 
-def two_ways(value):
+def two_ways(value, steps):
     pairs = [
-        (2 * source + core, 2 * (source ^ (1 + core)) + core)
+        (2 * source + core, 2 * (source ^ steps[core]) + core)
         for source in range(lax.axis_size("ctx"))
         for core in range(2)
     ]
@@ -69,41 +71,56 @@
 
 
 def prepare_kernel(
-    n_ctx, place, tokens, gain, w_up, w_query, w_key, w_value, full, half, first, second, sems
+    n_ctx, mask, tokens, gain, w_up, w_query, w_key, w_value, full, first, second, sems
 ):
-    ctx, tm, groups, tp = place[0], place[1], place[2], place[3]
-    rows = tokens.shape[0]
+    ctx, tm, groups, tp = (lax.axis_index(name) for name in AXES)
     count = first.shape[0]
-    edge = second.shape[0] - count
-    pairs, column = [], 0
-    for w in (w_up, w_query, w_key, w_value):
-        size = w.shape[1] // n_ctx
-        for step, out in enumerate((first, second)):
+    pairs = []
+    for step, out in enumerate((first, second)):
+        column = 0
+        for w in (w_up, w_query, w_key, w_value):
+            size = w.shape[1] // n_ctx
             source = w.at[slot(2 * groups + step, count), slot(ctx, size)]
             pairs.append((source, out.at[0:count, column : column + size]))
-        column += size
+            column += size
     copies = begin(sems, pairs)
+    rows, width = tokens.shape
     values = tokens[...].astype(jnp.float32)
     square = jnp.mean(values * values, axis=-1, keepdims=True)
-    full[...] = (values * lax.rsqrt(square + 1e-05) * gain[...]).astype(jnp.bfloat16)
-    half[...] = full[slot(tp, rows // 2), :]
-    columns = full.shape[1] // 2
-    last_edge = full[rows - edge :, slot(tp, columns)]
+    full[0:rows, :] = (values * lax.rsqrt(square + 1e-05) * gain[...]).astype(jnp.bfloat16)
+    entries = [
+        jnp.full((8, LANES), mask[0, e].astype(jnp.float32), jnp.float32) for e in range(n_ctx)
+    ]
+    entries.append(jnp.zeros((8, width - n_ctx * LANES), jnp.float32))
+    full[rows:, :] = jnp.concatenate(entries, axis=1).astype(jnp.bfloat16)
+    edge = second.shape[0] - count
+    columns = width // 2
+    last_edge = full[rows - edge : rows, slot(tp, columns)]
     first_edge = full[0:edge, slot(tp, columns)]
     second[count:, 0:columns] = jnp.where(tm == 0, last_edge, first_edge)
     second[count:, columns:] = jnp.zeros((edge, second.shape[1] - columns), jnp.bfloat16)
     end(copies)
 
 
-def convolve_kernel(per_frame, place, tokens, full, halo, taps, base, held):
-    tm, tp = place[1], place[3]
+def pack_near_kernel(n_ctx, after, w_up, w_query, w_key, w_value, near, sems):
+    ctx = lax.axis_index("ctx")
+    pairs, column = [], 0
+    for w in (w_up, w_query, w_key, w_value):
+        size = w.shape[1] // n_ctx
+        pairs.append((w.at[:, slot(ctx, size)], near.at[:, column : column + size]))
+        column += size
+    end(begin(sems, pairs))
+
+
+def convolve_kernel(per_frame, tokens, full, halo, taps, base, held):
+    tm, tp = lax.axis_index("tm"), lax.axis_index("tp")
     rows, columns = base.shape
     edge = 16
     margin = 2 * per_frame
     near = halo[halo.shape[0] - edge :, 0:columns].astype(jnp.float32)
     zeros = jnp.zeros((edge, columns), jnp.float32)
     held[0:edge, :] = jnp.where(tm == 1, near, zeros)
-    held[edge : edge + rows, :] = full[:, slot(tp, columns)].astype(jnp.float32)
+    held[edge : edge + rows, :] = full[0:rows, slot(tp, columns)].astype(jnp.float32)
     held[edge + rows :, :] = jnp.where(tm == 0, near, zeros)
     total = tokens[:, slot(tp, columns)].astype(jnp.float32)
     for offset in range(KERNEL):
@@ -112,77 +129,94 @@
     base[...] = total
 
 
-def project_kernel(n_ctx, place, *refs):
+def project_kernel(n_ctx, *refs):
     own, block, other_block, piece, other_piece = refs[:5]
-    w_up, w_query, w_key, w_value, first, second, far_first, far_second = refs[5:13]
-    acts, qkv = refs[13 : 13 + n_ctx], refs[13 + n_ctx]
-    held, weights, sems = refs[14 + n_ctx :]
-    ctx, tm, groups, tp = place[0], place[1], place[2], place[3]
-    rows, count = own.shape[0], first.shape[0]
-    pairs, column = [], 0
-    for w in (w_up, w_query, w_key, w_value):
-        size = w.shape[1] // n_ctx
-        target = weights.at[slot(tm, w.shape[0]), column : column + size]
-        pairs.append((w.at[:, slot(ctx, size)], target))
-        column += size
-    quarters = 4 * (1 - tm) + 2 * groups, 4 * (1 - tm) + 2 * (1 - groups)
-    pairs += [
-        (first, weights.at[slot(quarters[0], count)]),
-        (second.at[0:count], weights.at[slot(quarters[0] + 1, count)]),
-        (far_first, weights.at[slot(quarters[1], count)]),
-        (far_second.at[0:count], weights.at[slot(quarters[1] + 1, count)]),
-        (own, held.at[0:rows]),
-        (block, held.at[slot(1 + tp, rows)]),
-        (other_block, held.at[slot(2 - tp, rows)]),
-        (piece, held.at[slot(6 + tp, rows // 2)]),
-        (other_piece, held.at[slot(7 - tp, rows // 2)]),
-    ]
-    end(begin(sems, pairs))
-    total = jnp.dot(held[...], weights[...], preferred_element_type=jnp.float32)
-    hidden = acts[0].shape[1]
+    near, first, second, far_first, far_second = refs[5:10]
+    acts = refs[10 : 10 + n_ctx]
+    queries, keys, values, bias, held, far = refs[10 + n_ctx :]
+    ctx, tm, groups, tp = (lax.axis_index(name) for name in AXES)
+    rows, count, depth = own.shape[0] - 8, first.shape[0], near.shape[0]
+    sources = (
+        (own, slot(0, rows), rows),
+        (block, slot(1 + tp, rows), rows),
+        (other_block, slot(2 - tp, rows), rows),
+        (piece, slot(6 + tp, rows // 2), rows // 2),
+        (other_piece, slot(7 - tp, rows // 2), rows // 2),
+    )
+    half = depth // 2
+    cuts = ((0, slot(tm, depth), depth), (depth, slot(2 * (1 - tm) + groups, half), half))
+    cuts += ((depth + half, slot(2 * (1 - tm) + 1 - groups, half), half),)
+    for source, target, size in sources:
+        for to, lanes, wide in cuts:
+            held[target, to : to + wide] = source[0:size, lanes]
+    far[0:count, :] = first[...]
+    far[count : 2 * count, :] = second[0:count, :]
+    far[2 * count : 3 * count, :] = far_first[...]
+    far[3 * count :, :] = far_second[0:count, :]
+    total = jnp.dot(held[:, 0:depth], near[...], preferred_element_type=jnp.float32)
+    total += jnp.dot(held[:, depth:], far[...], preferred_element_type=jnp.float32)
+    hidden, wide = acts[0].shape[1], queries.shape[1]
     activated = jax.nn.gelu(total[:, :hidden], approximate=True).astype(jnp.bfloat16)
     for d in range(n_ctx):
         acts[d][...] = activated[d * rows : (d + 1) * rows]
-    qkv[...] = total[:, hidden:].astype(jnp.bfloat16)
-
-
-def attend_kernel(n_ctx, i, place, mask, activated, qkv, out):
-    ctx = place[0]
+    projected = total[:, hidden:].astype(jnp.bfloat16)
+    queries[...] = projected[:, 0:wide]
+    keys[...] = projected[:, wide : 2 * wide]
+    values[...] = projected[:, 2 * wide :].T
+    for j in range(n_ctx):
+        lanes = slot(ctx ^ j, LANES)
+        one, other = block[rows:, lanes], other_block[rows:, lanes]
+        last, other_last = piece[rows // 2 :, lanes], other_piece[rows // 2 :, lanes]
+        entries = (
+            own[rows:, lanes],
+            jnp.where(tp == 0, one, other),
+            jnp.where(tp == 0, other, one),
+            jnp.where(tp == 0, other_last, last),
+        )
+        for i, entry in enumerate(entries):
+            flag = entry.astype(jnp.float32)
+            target = slice(j * LANES, (j + 1) * LANES)
+            bias[8 * i : 8 * (i + 1), target] = jnp.where(flag > 0, 0.0, MASKED)
+
+
+def attend_kernel(n_ctx, i, activated, queries, keys, values, bias, out):
     rows, hidden = activated.shape
     wide = out.shape[1] - hidden
+    block = queries[i * rows : (i + 1) * rows, :]
     lane_head = lax.broadcasted_iota(jnp.int32, (1, wide), 1) // HEAD_DIM
-    queries = qkv[i * rows : (i + 1) * rows, 0:wide]
-    keys = qkv[:, wide : 2 * wide]
-    values = qkv[:, 2 * wide :]
-    bias = jnp.concatenate(
-        [
-            jnp.full((1, rows), jnp.where(mask[0, ctx ^ j] > 0, 0.0, MASKED), jnp.float32)
+    allowed = jnp.concatenate(
+        [
+            jnp.broadcast_to(bias[8 * i : 8 * i + 1, j * LANES : (j + 1) * LANES], (rows, rows))
             for j in range(n_ctx)
         ],
-        axis=1,
-    )
-    result = jnp.zeros((rows, wide), jnp.float32)
+        axis=0,
+    )
+    results = []
     for head in range(wide // HEAD_DIM):
-        one = jnp.where(lane_head == head, queries, jnp.zeros_like(queries))
+        one = jnp.where(lane_head == head, block, jnp.zeros_like(block))
         scores = lax.dot_general(
-            one, keys, (((1,), (1,)), ((), ())), preferred_element_type=jnp.float32
+            keys[...], one, (((1,), (1,)), ((), ())), preferred_element_type=jnp.float32
         )
-        scores = scores * 0.125 + bias
-        peak = jnp.max(scores, axis=-1, keepdims=True)
+        scores = scores * 0.125 + allowed
+        peak = jnp.max(scores, axis=0, keepdims=True)
         expo = jnp.exp(scores - peak)
-        total = jnp.sum(expo, axis=-1, keepdims=True)
-        mixed = jnp.dot(expo.astype(jnp.bfloat16), values, preferred_element_type=jnp.float32)
-        result = jnp.where(lane_head == head, mixed / total, result)
+        total = jnp.sum(expo, axis=0, keepdims=True)
+        mixed = jnp.dot(
+            values[head * HEAD_DIM : (head + 1) * HEAD_DIM, :],
+            expo.astype(jnp.bfloat16),
+            preferred_element_type=jnp.float32,
+        )
+        results.append(mixed / total)
     out[:, 0:hidden] = activated[...]
-    out[:, hidden:] = result.astype(jnp.bfloat16)
-
-
-def join_kernel(n_ctx, place, *refs):
+    out[:, hidden:] = jnp.concatenate(results, axis=0).T.astype(jnp.bfloat16)
+
+
+def join_kernel(n_ctx, *refs):
     near_down, near_out, base = refs[:3]
     far_down, farther_down, far_out = refs[3:6]
     parts = refs[6 : 6 + n_ctx]
     keep, send, down, out, acts, atts, sems = refs[6 + n_ctx :]
-    ctx, tm, groups, tp = place[0], place[1], place[2], place[3]
+    ctx, tm, groups, tp = (lax.axis_index(name) for name in AXES)
     hidden, wide = acts.shape[1] // n_ctx, atts.shape[1] // n_ctx
     count = far_down.shape[0]
     pairs = []
@@ -211,7 +245,9 @@
 ANY = pl.BlockSpec(memory_space=pl.ANY)
 
 
-def call(kernel, name, outs, ins, scratch=(), flops=0, moved=1 << 20, transcendentals=0):
+def call(
+    kernel, name, outs, ins, scratch=(), flops=0, moved=1 << 20, transcendentals=0, limit=16 << 20
+):
     specs, values = zip(*ins)
     return pl.pallas_call(
         kernel,
@@ -219,7 +255,7 @@
         in_specs=list(specs),
         out_specs=[VMEM] * len(outs),
         scratch_shapes=list(scratch),
-        compiler_params=pltpu.CompilerParams(vmem_limit_bytes=32 * 1024 * 1024),
+        compiler_params=pltpu.CompilerParams(vmem_limit_bytes=limit),
         name=name,
         cost_estimate=pl.CostEstimate(
             flops=flops, bytes_accessed=moved, transcendentals=transcendentals
@@ -241,43 +277,55 @@
     columns = w_out.shape[1]
     packed = hidden + 3 * wide
     bf16, f32 = jnp.bfloat16, jnp.float32
-    place = jnp.stack([ctx, tm, groups, tp]).astype(jnp.int32)
     token_rows = tokens.reshape(rows, width)
     quarter = depth // 4
 
-    full, half, first, second = call(
+    full, first, second = call(
         functools.partial(prepare_kernel, n_ctx),
         "prepare",
         [
-            ((rows, width), bf16),
-            ((rows // 2, width), bf16),
+            ((rows + 8, width), bf16),
             ((quarter, packed), bf16),
             ((quarter + 16, packed), bf16),
         ],
-        [(SMEM, place), (VMEM, token_rows), (VMEM, norm_gain.reshape(1, width))]
+        [
+            (SMEM, block_mask[0]),
+            (VMEM, token_rows),
+            (VMEM, norm_gain.reshape(1, width)),
+        ]
         + [(ANY, w) for w in (w_up, w_query, w_key, w_value)],
         [pltpu.SemaphoreType.DMA((8,))],
-    )
-    block = two_ways(full)
-    piece = across(half, "ctx", 3)
+        limit=None,
+    )
+    (near,) = call(
+        functools.partial(pack_near_kernel, n_ctx),
+        "pack_near",
+        [((depth, packed), bf16)],
+        [(ANY, w) for w in (second, w_up, w_query, w_key, w_value)],
+        [pltpu.SemaphoreType.DMA((4,))],
+    )
+    block = two_ways(full, (1, 2))
+    piece = lax.dynamic_slice_in_dim(block, tp * (rows // 2), rows // 2 + 8, 0)
+    piece = two_ways(piece, (2, 1))
     x_first = across(first, "tm", 1)
     x_second = across(second, "tm", 1)
     y_first = across(x_first, "groups", 1)
     y_second = across(x_second, "groups", 1)
-    masks = [block_mask[0]] + [across(block_mask[0], "ctx", d) for d in range(1, n_ctx)]
     other_block = across(block, "tp", 1)
     other_piece = across(piece, "tp", 1)
     half_down = w_down.shape[0] // 2
-    x_down = across(lax.dynamic_slice_in_dim(w_down, groups * half_down, half_down, 0), "tm", 1)
-    y_down = across(x_down, "groups", 1)
-    x_out = across(w_out, "tm", 1)
+    sent_down = lax.dynamic_slice_in_dim(w_down, groups * half_down, half_down, 0)
+    sent_down, sent_out, _ = lax.optimization_barrier(
+        (sent_down, w_out, (second,))
+    )
+    x_down = across(sent_down, "tm", 1)
+    x_out = across(sent_out, "tm", 1)
 
     (base,) = call(
         functools.partial(convolve_kernel, dancers_here),
         "convolve",
         [((rows, columns), f32)],
         [
-            (SMEM, place),
             (VMEM, token_rows),
             (VMEM, full),
             (VMEM, x_second),
@@ -285,21 +333,20 @@
         ],
         [pltpu.VMEM((rows + 32, columns), f32)],
     )
-    *acts, qkv = call(
+    *acts, queries, keys, values, bias = call(
         functools.partial(project_kernel, n_ctx),
         "project",
-        [((rows, hidden), bf16)] * n_ctx + [((n_ctx * rows, 3 * wide), bf16)],
-        [(SMEM, place)]
-        + [(ANY, value) for value in (full, block, other_block, piece, other_piece)]
-        + [(ANY, value) for value in (w_up, w_query, w_key, w_value)]
-        + [(ANY, value) for value in (x_first, x_second, y_first, y_second)],
+        [((rows, hidden), bf16)] * n_ctx
+        + [((n_ctx * rows, wide), bf16)] * 2
+        + [((wide, n_ctx * rows), bf16), ((8 * n_ctx, n_ctx * LANES), f32)],
+        [(VMEM, value) for value in (full, block, other_block, piece, other_piece)]
+        + [(VMEM, value) for value in (near, x_first, x_second, y_first, y_second)],
         [
             pltpu.VMEM((n_ctx * rows, width), bf16),
-            pltpu.VMEM((width, packed), bf16),
-            pltpu.SemaphoreType.DMA((13,)),
+            pltpu.VMEM((depth, packed), bf16),
         ],
-        flops=2 * n_ctx * rows * width * packed,
-        moved=4 << 20,
+        flops=8 * n_ctx * rows * width * packed,
+        moved=64 << 20,
         transcendentals=n_ctx * rows * hidden,
     )
     parts = [None] * n_ctx
@@ -308,16 +355,19 @@
             functools.partial(attend_kernel, n_ctx, i),
             "attend",
             [((rows, hidden + wide), bf16)],
-            [(SMEM, place), (SMEM, masks[i]), (VMEM, acts[i]), (VMEM, qkv)],
+            [(VMEM, value) for value in (acts[i], queries, keys, values, bias)],
             flops=4 * wide * n_ctx * rows * rows,
             transcendentals=(wide // HEAD_DIM) * n_ctx * rows * rows,
         )
+        if i == 1:
+            x_down, part = lax.optimization_barrier((x_down, part))
         parts[i] = across(part, "ctx", i) if i else part
+    y_down = across(x_down, "groups", 1)
     keep, send = call(
         functools.partial(join_kernel, n_ctx),
         "join",
         [((rows, columns), f32), ((rows, columns), bf16)],
-        [(SMEM, place), (VMEM, w_down), (VMEM, w_out), (VMEM, base)]
+        [(VMEM, w_down), (VMEM, w_out), (VMEM, base)]
         + [(ANY, value) for value in (x_down, y_down, x_out)]
         + [(ANY, value) for value in parts],
         [
@@ -403,7 +453,7 @@
     def on_device(*arrays):
         local_heads = arrays[3].shape[1] // HEAD_DIM
         pairs = n_tm == 2 and mesh.shape["groups"] == 2 and mesh.shape["tp"] == 2
-        even = n_ctx == 4 and local_heads % (2 * n_ctx) == 0
+        even = n_ctx == 4 and local_heads == 2 * n_ctx
         chosen = split_over_ctx if pairs and even else gather_all
         return chosen(*arrays)
 

time: 67.1 us -> 51.5 us (0.77)
  waiting for transfers between devices: 25.8 us -> 18.1 us
  starting transfers between devices: 23.9 us -> 17.9 us
  Pallas kernels: 11.3 us -> 9.59 us
    ppermute x17 -> x13, waiting for transfers between devices: 25.8 us -> 12.5 us  [across(): lax.ppermute(value, axis, [(source, source ^ step) for source in range(co...]
    ppermute x17 -> x13, starting transfers between devices: 22.2 us -> 12.4 us  [across(): lax.ppermute(value, axis, [(source, source ^ step) for source in range(co...]
    ppermute x1 -> x2, waiting for transfers between devices: 0.01 us -> 5.62 us  [two_ways(): return lax.ppermute(value, ('ctx', 'tp'), pairs)]
    ppermute x1 -> x2, starting transfers between devices: 1.64 us -> 5.46 us  [two_ways(): return lax.ppermute(value, ('ctx', 'tp'), pairs)]
    pallas_call x8 -> x9, Pallas kernels: 11.3 us -> 9.59 us  [call(): pl.pallas_call(kernel, out_shape=[jax.ShapeDtypeStruct(shape, dtype) for...]
    dynamic_slice x1, local copies, waits for them, and re-layouts: 1.16 us -> 0.04 us  [split_over_ctx(): lax.dynamic_slice_in_dim(w_down, groups * half_down, half_down, 0)]
    dynamic_slice x0 -> x1, local copies, waits for them, and re-layouts: none -> 0.92 us  [split_over_ctx(): piece = lax.dynamic_slice_in_dim(block, tp * (rows // 2), rows // 2 + 8, 0)]
    unnamed x18 -> x20, local copies, waits for them, and re-layouts: 2.7 us -> 1.99 us
  transfers between devices with their start and end apart: 18 -> 15, of which waited for: 5 -> 6; matrix products, arithmetic and copies ran while one was open for 2% -> 2% of each run, Pallas kernels for 14% -> 11%
where the time goes in v3:
time: 51.5 us; the launch traced here: 51.2 us
  waiting for transfers between devices  18.1 us (35%)
  starting transfers between devices  17.9 us (35%)
  Pallas kernels  9.59 us (19%)
  local copies, waits for them, and re-layouts  5.42 us (11%)
    ppermute x13, waiting for transfers between devices, across(): lax.ppermute(value, axis, [(source, source ^ step) for source in range(co...  12.5 us
    ppermute x13, starting transfers between devices, across(): lax.ppermute(value, axis, [(source, source ^ step) for source in range(co...  12.4 us
    pallas_call x9, Pallas kernels, call(): pl.pallas_call(kernel, out_shape=[jax.ShapeDtypeStruct(shape, dtype) for...  9.59 us
    ppermute x2, waiting for transfers between devices, two_ways(): return lax.ppermute(value, ('ctx', 'tp'), pairs)  5.62 us
    ppermute x2, starting transfers between devices, two_ways(): return lax.ppermute(value, ('ctx', 'tp'), pairs)  5.46 us
    unnamed x20, local copies, waits for them, and re-layouts  1.99 us
    reshape x1, local copies, waits for them, and re-layouts, split_over_ctx(): token_rows = tokens.reshape(rows, width)  1.76 us
  transfers between devices with their start and end apart: 15, of which 6 were waited for; matrix products, arithmetic and copies ran while one was open for 2% of the time, Pallas kernels for 11%

profile of v3, /device:TPU:0, one launch (start us, length us, event | category | flops | bytes accessed | tf_op | source)
XLA Modules:
  0.0 51.2 jit_solution(2673564615357723760)
XLA Ops:
  0.0 1.8 %reshape.9.tokens = bf16[128,1024]{1,0:T(8,128)(2,1)} reshape(bf16[64,2,1024]{2,1,0:T(2,128)(2,1)} %param.10) | data formatting | bytes 524288 | tf_op jit(solution)/shard_map/reshape | solution.py:280
  1.8 3.0 %prepare.1 = (bf16[136,1024]{1,0:T(8,128)(2,1)}, bf16[128,640]{1,0:T(8,128)(2,1)}, bf16[144,640]{1,0:T(8,128)(2,1)}) custom-call(s32[1,4]{1,0:T(1,128)} %bitcast.3, bf16[128,1024]{1,0:T(8,128)(2,1)} %reshape.9.tokens, f32[1,1024]{1,0:T(1,128)} %bitcast.2, bf16[512,1024]{1,0:T(8,128)(2,1)} %w_up.3, bf16[512,512]{1,0:T(8,128)(2,1)} %w_query.3, ...), custom_call_target="tpu_custom_call" | custom-call | bytes 1048576 | tf_op jit(solution)/shard_map/prepare/pallas_call | solution.py:252
  4.8 3.1 %collective-permute-start.2 = (bf16[136,1024]{1,0:T(8,128)(2,1)}, bf16[136,1024]{1,0:T(8,128)(2,1)}, u32[]{:S(2)}, u32[]{:S(2)}) collective-permute-start(bf16[136,1024]{1,0:T(8,128)(2,1)} %get-tuple-element.22.full.refs_0_), channel_id=1, source_target_pairs={{0,4},{1,9},{4,0},{5,13},{8,12},{9,1},{12,8},{13,5},{2,6},{3,11},{... | collective-permute-start | bytes 835592 | tf_op jit(solution)/shard_map/ppermute | solution.py:40
  7.9 1.5 %collective-permute-start = (bf16[144,640]{1,0:T(8,128)(2,1)}, bf16[144,640]{1,0:T(8,128)(2,1)S(1)}, u32[]{:S(2)}, u32[]{:S(2)}) collective-permute-start(bf16[144,640]{1,0:T(8,128)(2,1)} %get-tuple-element.23.after), channel_id=1, source_target_pairs={{0,2},{2,0},{1,3},{3,1},{4,6},{6,4},{5,7},{7,5},{8,10},{10,8},{9,1... | collective-permute-start | bytes 552968 | tf_op jit(solution)/shard_map/ppermute | solution.py:31
  9.9 5.4 %collective-permute-done.2.refs_1_ = bf16[136,1024]{1,0:T(8,128)(2,1)} collective-permute-done((bf16[136,1024]{1,0:T(8,128)(2,1)}, bf16[136,1024]{1,0:T(8,128)(2,1)}, u32[]{:S(2)}, u32[]{:S(2)}) %collective-permute-start.2) | collective-permute-done | bytes 278560 | tf_op jit(solution)/shard_map/ppermute | solution.py:40
  15.3 0.9 %constant_dynamic-slice_fusion = bf16[72,1024]{1,0:T(8,128)(2,1)S(1)} fusion(bf16[136,1024]{1,0:T(8,128)(2,1)} %collective-permute-done.2.refs_1_, s32[]{:T(128)S(6)} %select_n.7), kind=kLoop, calls=%fused_computation.1 | loop fusion | bytes 294916 | tf_op jit(solution)/shard_map/dynamic_slice | solution.py:308
  16.2 2.4 %collective-permute-start.4 = (bf16[72,1024]{1,0:T(8,128)(2,1)S(1)}, bf16[72,1024]{1,0:T(8,128)(2,1)S(1)}, u32[]{:S(2)}, u32[]{:S(2)}) collective-permute-start(bf16[72,1024]{1,0:T(8,128)(2,1)S(1)} %constant_dynamic-slice_fusion), channel_id=1, source_target_pairs={{0,8},{1,5},{4,12},{5,1},{8,0},{9,13},{12,4},{13,9},{2,10},{3,7},{... | collective-permute-start | bytes 442376 | tf_op jit(solution)/shard_map/ppermute | solution.py:40
  18.7 1.6 %collective-permute-start.1 = (bf16[512,512]{1,0:T(8,128)(2,1)S(1)}, bf16[512,512]{1,0:T(8,128)(2,1)S(1)}, u32[]{:S(2)}, u32[]{:S(2)}) collective-permute-start(bf16[512,512]{1,0:T(8,128)(2,1)S(1)} %constant_dynamic-slice_fusion.1), channel_id=1, source_target_pairs={{0,2},{2,0},{1,3},{3,1},{4,6},{6,4},{5,7},{7,5},{8,10},{10,8},{9,1... | collective-permute-start | bytes 1572872 | tf_op jit(solution)/shard_map/ppermute | solution.py:31
  20.2 1.5 %collective-permute-start.8 = (bf16[144,640]{1,0:T(8,128)(2,1)S(1)}, bf16[144,640]{1,0:T(8,128)(2,1)S(1)}, u32[]{:S(2)}, u32[]{:S(2)}) collective-permute-start(bf16[144,640]{1,0:T(8,128)(2,1)S(1)} %collective-permute-done.halo.refs_7_), channel_id=1, source_target_pairs={{0,16},{16,0},{1,17},{17,1},{2,18},{18,2},{3,19},{19,3},{4,20},{20... | collective-permute-start | bytes 552968 | tf_op jit(solution)/shard_map/ppermute | solution.py:31
  22.6 1.0 %copy-done.5 = bf16[512,512]{1,0:T(8,128)(2,1)S(1)} copy-done((bf16[512,512]{1,0:T(8,128)(2,1)S(1)}, bf16[512,512]{1,0:T(8,128)(2,1)}, u32[]{:S(2)}) %copy-start.5) | copy-done | bytes 524312
  23.6 0.9 %copy-done.8 = bf16[144,640]{1,0:T(8,128)(2,1)S(1)} copy-done((bf16[144,640]{1,0:T(8,128)(2,1)S(1)}, bf16[144,640]{1,0:T(8,128)(2,1)}, u32[]{:S(2)}) %copy-start.8) | copy-done | bytes 184344
  24.7 5.8 %collective-permute-done.7.refs_8_ = bf16[128,640]{1,0:T(8,128)(2,1)S(1)} collective-permute-done((bf16[128,640]{1,0:T(8,128)(2,1)S(1)}, bf16[128,640]{1,0:T(8,128)(2,1)S(1)}, u32[]{:S(2)}, u32[]{:S(2)}) %collective-permute-start.7) | collective-permute-done | bytes 163872 | tf_op jit(solution)/shard_map/ppermute | solution.py:31
  31.1 2.1 %project.1 = (bf16[128,256]{1,0:T(8,128)(2,1)S(1)}, bf16[128,256]{1,0:T(8,128)(2,1)S(1)}, bf16[128,256]{1,0:T(8,128)(2,1)S(1)}, bf16[128,256]{1,0:T(8,128)(2,1)S...) custom-call(bf16[136,1024]{1,0:T(8,128)(2,1)S(1)} %copy-done.7, ...), custom_call_target="tpu_custom_call" | custom-call | flops 2684354560 | bytes 67108864 | tf_op jit(solution)/shard_map/project/pallas_call | solution.py:252
  33.1 0.8 %attend.4 = bf16[128,384]{1,0:T(8,128)(2,1)S(1)} custom-call(bf16[128,256]{1,0:T(8,128)(2,1)S(1)} %get-tuple-element.26.activated, bf16[512,128]{1,0:T(8,128)(2,1)S(1)} %get-tuple-element.27.queries, bf16[512,128]{1,0:T(8,128)(2,1)S(1)} %get-tuple-element.28.keys, bf16[128,512]{1,0:T(8,128)(2,1)S(1)} %get-tuple-element.29.values, ...), custom_call_target="tpu_custom_call" | custom-call | flops 33554432 | bytes 1048576 | tf_op jit(solution)/shard_map/attend/pallas_call | solution.py:252
  33.9 1.6 %collective-permute-start.9 = (bf16[512,512]{1,0:T(8,128)(2,1)S(1)}, bf16[512,512]{1,0:T(8,128)(2,1)S(1)}, u32[]{:S(2)}, u32[]{:S(2)}) collective-permute-start(bf16[512,512]{1,0:T(8,128)(2,1)S(1)} %collective-permute-done.1.refs_3_), channel_id=1, source_target_pairs={{0,16},{16,0},{1,17},{17,1},{2,18},{18,2},{3,19},{19,3},{4,20},{20... | collective-permute-start | bytes 1572872 | tf_op jit(solution)/shard_map/ppermute | solution.py:31
  35.5 0.8 %attend.7 = bf16[128,384]{1,0:T(8,128)(2,1)S(1)} custom-call(bf16[128,256]{1,0:T(8,128)(2,1)S(1)} %get-tuple-element.36.activated, bf16[512,128]{1,0:T(8,128)(2,1)S(1)} %get-tuple-element.27.queries, bf16[512,128]{1,0:T(8,128)(2,1)S(1)} %get-tuple-element.28.keys, bf16[128,512]{1,0:T(8,128)(2,1)S(1)} %get-tuple-element.29.values, ...), custom_call_target="tpu_custom_call" | custom-call | flops 33554432 | bytes 1048576 | tf_op jit(solution)/shard_map/attend/pallas_call | solution.py:252
  36.3 2.4 %collective-permute-start.13 = (bf16[128,384]{1,0:T(8,128)(2,1)S(1)}, bf16[128,384]{1,0:T(8,128)(2,1)S(1)}, u32[]{:S(2)}, u32[]{:S(2)}) collective-permute-start(bf16[128,384]{1,0:T(8,128)(2,1)S(1)} %attend.7), channel_id=1, source_target_pairs={{0,12},{4,8},{8,4},{12,0},{1,13},{5,9},{9,5},{13,1},{2,14},{6,10},... | collective-permute-start | bytes 294920 | tf_op jit(solution)/shard_map/ppermute | solution.py:31
  38.7 0.8 %attend.6 = bf16[128,384]{1,0:T(8,128)(2,1)S(1)} custom-call(bf16[128,256]{1,0:T(8,128)(2,1)S(1)} %get-tuple-element.35.activated, bf16[512,128]{1,0:T(8,128)(2,1)S(1)} %get-tuple-element.27.queries, bf16[512,128]{1,0:T(8,128)(2,1)S(1)} %get-tuple-element.28.keys, bf16[128,512]{1,0:T(8,128)(2,1)S(1)} %get-tuple-element.29.values, ...), custom_call_target="tpu_custom_call" | custom-call | flops 33554432 | bytes 1048576 | tf_op jit(solution)/shard_map/attend/pallas_call | solution.py:252
  39.5 1.8 %collective-permute-start.12 = (bf16[128,384]{1,0:T(8,128)(2,1)S(1)}, bf16[128,384]{1,0:T(8,128)(2,1)S(1)}, u32[]{:S(2)}, u32[]{:S(2)}) collective-permute-start(bf16[128,384]{1,0:T(8,128)(2,1)S(1)} %attend.6), channel_id=1, source_target_pairs={{0,8},{4,12},{8,0},{12,4},{1,9},{5,13},{9,1},{13,5},{2,10},{6,14},... | collective-permute-start | bytes 294920 | tf_op jit(solution)/shard_map/ppermute | solution.py:31
  41.9 0.8 %attend.5.refs_6_ = bf16[128,384]{1,0:T(8,128)(2,1)S(1)} custom-call(bf16[128,256]{1,0:T(8,128)(2,1)S(1)} %get-tuple-element.33.activated, bf16[512,128]{1,0:T(8,128)(2,1)S(1)} %get-tuple-element.27.queries, bf16[512,128]{1,0:T(8,128)(2,1)S(1)} %get-tuple-element.28.keys, bf16[128,512]{1,0:T(8,128)(2,1)S(1)} %get-tuple-element.29.values, ...), custom_call_target="tpu_custom_call" | custom-call | flops 33554432 | bytes 1048576 | tf_op jit(solution)/shard_map/attend/pallas_call | solution.py:252
  42.6 1.7 %collective-permute-done.10.refs_5_ = bf16[512,512]{1,0:T(8,128)(2,1)S(1)} collective-permute-done((bf16[512,512]{1,0:T(8,128)(2,1)S(1)}, bf16[512,512]{1,0:T(8,128)(2,1)S(1)}, u32[]{:S(2)}, u32[]{:S(2)}) %collective-permute-start.10) | collective-permute-done | bytes 524320 | tf_op jit(solution)/shard_map/ppermute | solution.py:31
  44.3 3.7 %collective-permute-done.12.refs_8_ = bf16[128,384]{1,0:T(8,128)(2,1)S(1)} collective-permute-done((bf16[128,384]{1,0:T(8,128)(2,1)S(1)}, bf16[128,384]{1,0:T(8,128)(2,1)S(1)}, u32[]{:S(2)}, u32[]{:S(2)}) %collective-permute-start.12) | collective-permute-done | bytes 98336 | tf_op jit(solution)/shard_map/ppermute | solution.py:31
  48.0 1.0 %join.1 = (f32[128,512]{1,0:T(8,128)S(1)}, bf16[128,512]{1,0:T(8,128)(2,1)S(1)}) custom-call(bf16[1024,512]{1,0:T(8,128)(2,1)S(1)} %copy-done.2, bf16[512,512]{1,0:T(8,128)(2,1)S(1)} %copy-done.6, f32[128,512]{1,0:T(8,128)S(1)} %convolve.1.refs_2_, bf16[512,512]{1,0:T(8,128)(2,1)S(1)} %collective-permute-done.1.refs_3_, ...), custom_call_target="tpu_custom_call" | custom-call | flops 402653184 | bytes 4194304 | tf_op jit(solution)/shard_map/join/pallas_call | solution.py:252
  49.1 1.3 %collective-permute-done.14 = bf16[128,512]{1,0:T(8,128)(2,1)S(1)} collective-permute-done((bf16[128,512]{1,0:T(8,128)(2,1)S(1)}, bf16[128,512]{1,0:T(8,128)(2,1)S(1)}, u32[]{:S(2)}, u32[]{:S(2)}) %collective-permute-start.14) | collective-permute-done | bytes 131104 | tf_op jit(solution)/shard_map/ppermute | solution.py:31
  (40 shorter events, 3.6 us)
Async XLA Ops:
  1.8 16.9 %copy-start.2 = (bf16[1024,512]{1,0:T(8,128)(2,1)S(1)}, bf16[1024,512]{1,0:T(8,128)(2,1)}, u32[]{:S(2)}) copy-start(bf16[1024,512]{1,0:T(8,128)(2,1)} %refs_0_.1) | copy-start | bytes 3145732
  1.8 20.8 %copy-start.3 = (bf16[512,512]{1,0:T(8,128)(2,1)S(1)}, bf16[512,512]{1,0:T(8,128)(2,1)}, u32[]{:S(2)}) copy-start(bf16[512,512]{1,0:T(8,128)(2,1)} %w_query.3) | copy-start | bytes 1572868
  1.8 20.8 %copy-start.4 = (bf16[512,512]{1,0:T(8,128)(2,1)S(1)}, bf16[512,512]{1,0:T(8,128)(2,1)}, u32[]{:S(2)}) copy-start(bf16[512,512]{1,0:T(8,128)(2,1)} %w_key.3) | copy-start | bytes 1572868
  4.8 17.8 %copy-start = (bf16[512,1024]{1,0:T(8,128)(2,1)S(1)}, bf16[512,1024]{1,0:T(8,128)(2,1)}, u32[]{:S(2)}) copy-start(bf16[512,1024]{1,0:T(8,128)(2,1)} %w_up.3) | copy-start | bytes 3145732
  4.8 10.5 %collective-permute-start.2 = (bf16[136,1024]{1,0:T(8,128)(2,1)}, bf16[136,1024]{1,0:T(8,128)(2,1)}, u32[]{:S(2)}, u32[]{:S(2)}) collective-permute-start(bf16[136,1024]{1,0:T(8,128)(2,1)} %get-tuple-element.22.full.refs_0_), channel_id=1, source_target_pairs={{0,4},{1,9},{4,0},{5,13},{8,12},{9,1},{12,8},{13,5},{2,6},{3,11},{... | collective-permute-start | bytes 835592 | tf_op jit(solution)/shard_map/ppermute | solution.py:40
  7.9 12.4 %collective-permute-start = (bf16[144,640]{1,0:T(8,128)(2,1)}, bf16[144,640]{1,0:T(8,128)(2,1)S(1)}, u32[]{:S(2)}, u32[]{:S(2)}) collective-permute-start(bf16[144,640]{1,0:T(8,128)(2,1)} %get-tuple-element.23.after), channel_id=1, source_target_pairs={{0,2},{2,0},{1,3},{3,1},{4,6},{6,4},{5,7},{7,5},{8,10},{10,8},{9,1... | collective-permute-start | bytes 552968 | tf_op jit(solution)/shard_map/ppermute | solution.py:31
  9.4 12.4 %collective-permute-start.6 = (bf16[128,640]{1,0:T(8,128)(2,1)}, bf16[128,640]{1,0:T(8,128)(2,1)S(1)}, u32[]{:S(2)}, u32[]{:S(2)}) collective-permute-start(bf16[128,640]{1,0:T(8,128)(2,1)} %get-tuple-element.25), channel_id=1, source_target_pairs={{0,2},{2,0},{1,3},{3,1},{4,6},{6,4},{5,7},{7,5},{8,10},{10,8},{9,1... | collective-permute-start | bytes 491528 | tf_op jit(solution)/shard_map/ppermute | solution.py:31
  16.2 6.2 %collective-permute-start.4 = (bf16[72,1024]{1,0:T(8,128)(2,1)S(1)}, bf16[72,1024]{1,0:T(8,128)(2,1)S(1)}, u32[]{:S(2)}, u32[]{:S(2)}) collective-permute-start(bf16[72,1024]{1,0:T(8,128)(2,1)S(1)} %constant_dynamic-slice_fusion), channel_id=1, source_target_pairs={{0,8},{1,5},{4,12},{5,1},{8,0},{9,13},{12,4},{13,9},{2,10},{3,7},{... | collective-permute-start | bytes 442376 | tf_op jit(solution)/shard_map/ppermute | solution.py:40
  18.6 12.4 %collective-permute-start.3 = (bf16[136,1024]{1,0:T(8,128)(2,1)}, bf16[136,1024]{1,0:T(8,128)(2,1)S(1)}, u32[]{:S(2)}, u32[]{:S(2)}) collective-permute-start(bf16[136,1024]{1,0:T(8,128)(2,1)} %collective-permute-done.2.refs_1_), channel_id=1, source_target_pairs={{0,1},{1,0},{2,3},{3,2},{4,5},{5,4},{6,7},{7,6},{8,9},{9,8},{10,11... | collective-permute-start | bytes 835592 | tf_op jit(solution)/shard_map/ppermute | solution.py:31
  18.6 12.4 %copy-start.7 = (bf16[136,1024]{1,0:T(8,128)(2,1)S(1)}, bf16[136,1024]{1,0:T(8,128)(2,1)}, u32[]{:S(2)}) copy-start(bf16[136,1024]{1,0:T(8,128)(2,1)} %get-tuple-element.22.full.refs_0_) | copy-start | bytes 835588
  18.7 15.2 %collective-permute-start.1 = (bf16[512,512]{1,0:T(8,128)(2,1)S(1)}, bf16[512,512]{1,0:T(8,128)(2,1)S(1)}, u32[]{:S(2)}, u32[]{:S(2)}) collective-permute-start(bf16[512,512]{1,0:T(8,128)(2,1)S(1)} %constant_dynamic-slice_fusion.1), channel_id=1, source_target_pairs={{0,2},{2,0},{1,3},{3,1},{4,6},{6,4},{5,7},{7,5},{8,10},{10,8},{9,1... | collective-permute-start | bytes 1572872 | tf_op jit(solution)/shard_map/ppermute | solution.py:31
  20.2 10.8 %collective-permute-start.8 = (bf16[144,640]{1,0:T(8,128)(2,1)S(1)}, bf16[144,640]{1,0:T(8,128)(2,1)S(1)}, u32[]{:S(2)}, u32[]{:S(2)}) collective-permute-start(bf16[144,640]{1,0:T(8,128)(2,1)S(1)} %collective-permute-done.halo.refs_7_), channel_id=1, source_target_pairs={{0,16},{16,0},{1,17},{17,1},{2,18},{18,2},{3,19},{19,3},{4,20},{20... | collective-permute-start | bytes 552968 | tf_op jit(solution)/shard_map/ppermute | solution.py:31
  21.8 8.8 %collective-permute-start.7 = (bf16[128,640]{1,0:T(8,128)(2,1)S(1)}, bf16[128,640]{1,0:T(8,128)(2,1)S(1)}, u32[]{:S(2)}, u32[]{:S(2)}) collective-permute-start(bf16[128,640]{1,0:T(8,128)(2,1)S(1)} %collective-permute-done.6.refs_6_), channel_id=1, source_target_pairs={{0,16},{16,0},{1,17},{17,1},{2,18},{18,2},{3,19},{19,3},{4,20},{20... | collective-permute-start | bytes 491528 | tf_op jit(solution)/shard_map/ppermute | solution.py:31
  22.5 8.6 %collective-permute-start.5 = (bf16[72,1024]{1,0:T(8,128)(2,1)S(1)}, bf16[72,1024]{1,0:T(8,128)(2,1)S(1)}, u32[]{:S(2)}, u32[]{:S(2)}) collective-permute-start(bf16[72,1024]{1,0:T(8,128)(2,1)S(1)} %collective-permute-done.4.refs_3_), channel_id=1, source_target_pairs={{0,1},{1,0},{2,3},{3,2},{4,5},{5,4},{6,7},{7,6},{8,9},{9,8},{10,11... | collective-permute-start | bytes 442376 | tf_op jit(solution)/shard_map/ppermute | solution.py:31
  22.6 1.0 %copy-start.5 = (bf16[512,512]{1,0:T(8,128)(2,1)S(1)}, bf16[512,512]{1,0:T(8,128)(2,1)}, u32[]{:S(2)}) copy-start(bf16[512,512]{1,0:T(8,128)(2,1)} %w_value.3) | copy-start | bytes 1572868
  24.6 6.0 %copy-start.6 = (bf16[512,512]{1,0:T(8,128)(2,1)S(1)}, bf16[512,512]{1,0:T(8,128)(2,1)}, u32[]{:S(2)}) copy-start(bf16[512,512]{1,0:T(8,128)(2,1)} %refs_1_.1) | copy-start | bytes 1572868
  30.5 13.8 %collective-permute-start.10 = (bf16[512,512]{1,0:T(8,128)(2,1)S(1)}, bf16[512,512]{1,0:T(8,128)(2,1)S(1)}, u32[]{:S(2)}, u32[]{:S(2)}) collective-permute-start(bf16[512,512]{1,0:T(8,128)(2,1)S(1)} %copy-done.6), channel_id=1, source_target_pairs={{0,2},{2,0},{1,3},{3,1},{4,6},{6,4},{5,7},{7,5},{8,10},{10,8},{9,1... | collective-permute-start | bytes 1572872 | tf_op jit(solution)/shard_map/ppermute | solution.py:31
  33.9 14.1 %collective-permute-start.9 = (bf16[512,512]{1,0:T(8,128)(2,1)S(1)}, bf16[512,512]{1,0:T(8,128)(2,1)S(1)}, u32[]{:S(2)}, u32[]{:S(2)}) collective-permute-start(bf16[512,512]{1,0:T(8,128)(2,1)S(1)} %collective-permute-done.1.refs_3_), channel_id=1, source_target_pairs={{0,16},{16,0},{1,17},{17,1},{2,18},{18,2},{3,19},{19,3},{4,20},{20... | collective-permute-start | bytes 1572872 | tf_op jit(solution)/shard_map/ppermute | solution.py:31
  36.3 8.0 %collective-permute-start.13 = (bf16[128,384]{1,0:T(8,128)(2,1)S(1)}, bf16[128,384]{1,0:T(8,128)(2,1)S(1)}, u32[]{:S(2)}, u32[]{:S(2)}) collective-permute-start(bf16[128,384]{1,0:T(8,128)(2,1)S(1)} %attend.7), channel_id=1, source_target_pairs={{0,12},{4,8},{8,4},{12,0},{1,13},{5,9},{9,5},{13,1},{2,14},{6,10},... | collective-permute-start | bytes 294920 | tf_op jit(solution)/shard_map/ppermute | solution.py:31
  38.7 2.9 %copy-start.1 = (bf16[128,1024]{1,0:T(8,128)(2,1)S(1)}, bf16[128,1024]{1,0:T(8,128)(2,1)}, u32[]{:S(2)}) copy-start(bf16[128,1024]{1,0:T(8,128)(2,1)} %reshape.9.tokens) | copy-start | bytes 786436
  38.7 2.9 %copy-start.9 = (f32[5,512]{1,0:T(8,128)S(1)}, f32[5,512]{1,0:T(8,128)}, u32[]{:S(2)}) copy-start(f32[5,512]{1,0:T(8,128)} %taps.1) | copy-start | bytes 30724
  39.5 8.6 %collective-permute-start.12 = (bf16[128,384]{1,0:T(8,128)(2,1)S(1)}, bf16[128,384]{1,0:T(8,128)(2,1)S(1)}, u32[]{:S(2)}, u32[]{:S(2)}) collective-permute-start(bf16[128,384]{1,0:T(8,128)(2,1)S(1)} %attend.6), channel_id=1, source_target_pairs={{0,8},{4,12},{8,0},{12,4},{1,9},{5,13},{9,1},{13,5},{2,10},{6,14},... | collective-permute-start | bytes 294920 | tf_op jit(solution)/shard_map/ppermute | solution.py:31
  41.2 6.8 %collective-permute-start.11 = (bf16[128,384]{1,0:T(8,128)(2,1)S(1)}, bf16[128,384]{1,0:T(8,128)(2,1)S(1)}, u32[]{:S(2)}, u32[]{:S(2)}) collective-permute-start(bf16[128,384]{1,0:T(8,128)(2,1)S(1)} %attend.4), channel_id=1, source_target_pairs={{0,4},{4,0},{8,12},{12,8},{1,5},{5,1},{9,13},{13,9},{2,6},{6,2},{1... | collective-permute-start | bytes 294920 | tf_op jit(solution)/shard_map/ppermute | solution.py:31
  49.1 1.4 %collective-permute-start.14 = (bf16[128,512]{1,0:T(8,128)(2,1)S(1)}, bf16[128,512]{1,0:T(8,128)(2,1)S(1)}, u32[]{:S(2)}, u32[]{:S(2)}) collective-permute-start(bf16[128,512]{1,0:T(8,128)(2,1)S(1)} %get-tuple-element.38), channel_id=1, source_target_pairs={{0,1},{1,0},{2,3},{3,2},{4,5},{5,4},{6,7},{7,6},{8,9},{9,8},{10,11... | collective-permute-start | bytes 393224 | tf_op jit(solution)/shard_map/ppermute | solution.py:31
  (1 other events, 0.9 us)

commit v4 on v3

--- a/solution.py
+++ b/solution.py
@@ -70,36 +70,45 @@
     return pl.ds(pl.multiple_of(index * size, size), size)
 
 
-def prepare_kernel(
-    n_ctx, mask, tokens, gain, w_up, w_query, w_key, w_value, full, first, second, sems
-):
-    ctx, tm, groups, tp = (lax.axis_index(name) for name in AXES)
-    count = first.shape[0]
-    pairs = []
-    for step, out in enumerate((first, second)):
-        column = 0
-        for w in (w_up, w_query, w_key, w_value):
-            size = w.shape[1] // n_ctx
-            source = w.at[slot(2 * groups + step, count), slot(ctx, size)]
-            pairs.append((source, out.at[0:count, column : column + size]))
-            column += size
-    copies = begin(sems, pairs)
+def dot(left, right):
+    return jnp.dot(left, right, preferred_element_type=jnp.float32)
+
+
+def normalise_kernel(n_ctx, mask_in, tokens, gain, full, edge, mask, sems):
     rows, width = tokens.shape
+    copies = begin(sems, [(mask_in, mask)])
     values = tokens[...].astype(jnp.float32)
     square = jnp.mean(values * values, axis=-1, keepdims=True)
     full[0:rows, :] = (values * lax.rsqrt(square + 1e-05) * gain[...]).astype(jnp.bfloat16)
+    end(copies)
     entries = [
         jnp.full((8, LANES), mask[0, e].astype(jnp.float32), jnp.float32) for e in range(n_ctx)
     ]
     entries.append(jnp.zeros((8, width - n_ctx * LANES), jnp.float32))
-    full[rows:, :] = jnp.concatenate(entries, axis=1).astype(jnp.bfloat16)
-    edge = second.shape[0] - count
-    columns = width // 2
-    last_edge = full[rows - edge : rows, slot(tp, columns)]
-    first_edge = full[0:edge, slot(tp, columns)]
-    second[count:, 0:columns] = jnp.where(tm == 0, last_edge, first_edge)
-    second[count:, columns:] = jnp.zeros((edge, second.shape[1] - columns), jnp.bfloat16)
-    end(copies)
+    entries = jnp.concatenate(entries, axis=1).astype(jnp.bfloat16)
+    full[rows:, :] = entries
+    tm, tp = lax.axis_index("tm"), lax.axis_index("tp")
+    size, columns = edge.shape
+    last = full[rows - size : rows, slot(tp, columns)]
+    edge[...] = jnp.where(tm == 0, last, full[0:size, slot(tp, columns)])
+
+
+def pack_kernel(n_ctx, w_up, w_query, w_key, w_value, packed, sems):
+    ctx, groups = lax.axis_index("ctx"), lax.axis_index("groups")
+    count = packed.shape[0]
+    pairs, column = [], 0
+    for w in (w_up, w_query, w_key, w_value):
+        size = w.shape[1] // n_ctx
+        source = w.at[slot(groups, count), slot(ctx, size)]
+        pairs.append((source, packed.at[:, column : column + size]))
+        column += size
+    end(begin(sems, pairs))
+
+
+def split_kernel(block, piece):
+    size = piece.shape[0]
+    upper = lax.axis_index("tp") == 1
+    piece[...] = jnp.where(upper, block[block.shape[0] - size :, :], block[0:size, :])
 
 
 def pack_near_kernel(n_ctx, after, w_up, w_query, w_key, w_value, near, sems):
@@ -117,7 +126,7 @@
     rows, columns = base.shape
     edge = 16
     margin = 2 * per_frame
-    near = halo[halo.shape[0] - edge :, 0:columns].astype(jnp.float32)
+    near = halo[...].astype(jnp.float32)
     zeros = jnp.zeros((edge, columns), jnp.float32)
     held[0:edge, :] = jnp.where(tm == 1, near, zeros)
     held[edge : edge + rows, :] = full[0:rows, slot(tp, columns)].astype(jnp.float32)
@@ -131,11 +140,11 @@
 
 def project_kernel(n_ctx, *refs):
     own, block, other_block, piece, other_piece = refs[:5]
-    near, first, second, far_first, far_second = refs[5:10]
-    acts = refs[10 : 10 + n_ctx]
-    queries, keys, values, bias, held, far = refs[10 + n_ctx :]
+    near, far, farther = refs[5:8]
+    acts = refs[8 : 8 + n_ctx]
+    queries, keys, values, bias, held = refs[8 + n_ctx :]
     ctx, tm, groups, tp = (lax.axis_index(name) for name in AXES)
-    rows, count, depth = own.shape[0] - 8, first.shape[0], near.shape[0]
+    rows, depth = own.shape[0] - 8, near.shape[0]
     sources = (
         (own, slot(0, rows), rows),
         (block, slot(1 + tp, rows), rows),
@@ -149,12 +158,9 @@
     for source, target, size in sources:
         for to, lanes, wide in cuts:
             held[target, to : to + wide] = source[0:size, lanes]
-    far[0:count, :] = first[...]
-    far[count : 2 * count, :] = second[0:count, :]
-    far[2 * count : 3 * count, :] = far_first[...]
-    far[3 * count :, :] = far_second[0:count, :]
-    total = jnp.dot(held[:, 0:depth], near[...], preferred_element_type=jnp.float32)
-    total += jnp.dot(held[:, depth:], far[...], preferred_element_type=jnp.float32)
+    total = dot(held[:, 0:depth], near[...])
+    total += dot(held[:, depth : depth + half], far[...])
+    total += dot(held[:, depth + half :], farther[...])
     hidden, wide = acts[0].shape[1], queries.shape[1]
     activated = jax.nn.gelu(total[:, :hidden], approximate=True).astype(jnp.bfloat16)
     for d in range(n_ctx):
@@ -228,13 +234,10 @@
     pairs.append((farther_down, down.at[slot(1 - groups, count)]))
     copies = begin(sems, pairs)
 
-    def dot(left, right):
-        return jnp.dot(left[...], right[...], preferred_element_type=jnp.float32)
-
     end(copies[: 2 * n_ctx])
-    near_sum = dot(acts, near_down) + dot(atts, near_out)
+    near_sum = dot(acts[...], near_down[...]) + dot(atts[...], near_out[...])
     end(copies[2 * n_ctx :])
-    far_sum = dot(acts, down) + dot(atts, out)
+    far_sum = dot(acts[...], down[...]) + dot(atts[...], out[...])
     same = tm == tp
     keep[...] = jnp.where(same, near_sum, far_sum) + base[...]
     send[...] = jnp.where(same, far_sum, near_sum).astype(jnp.bfloat16)
@@ -246,7 +249,7 @@
 
 
 def call(
-    kernel, name, outs, ins, scratch=(), flops=0, moved=1 << 20, transcendentals=0, limit=16 << 20
+    kernel, name, outs, ins, scratch=(), flops=0, moved=1 << 20, transcendentals=0, limit=8 << 20
 ):
     specs, values = zip(*ins)
     return pl.pallas_call(
@@ -263,6 +266,10 @@
     )(*values)
 
 
+def after(value, *others):
+    return lax.optimization_barrier((value, others))[0]
+
+
 def split_over_ctx(
     tokens, norm_gain, block_mask, w_query, w_key, w_value, w_out, w_up, w_down, conv_weight
 ):
@@ -277,49 +284,38 @@
     columns = w_out.shape[1]
     packed = hidden + 3 * wide
     bf16, f32 = jnp.bfloat16, jnp.float32
-    token_rows = tokens.reshape(rows, width)
-    quarter = depth // 4
-
-    full, first, second = call(
-        functools.partial(prepare_kernel, n_ctx),
-        "prepare",
+    (packed_a,) = call(
+        functools.partial(pack_kernel, n_ctx),
+        "pack",
+        [((depth // 2, packed), bf16)],
+        [(ANY, w) for w in (w_up, w_query, w_key, w_value)],
+        [pltpu.SemaphoreType.DMA((4,))],
+        limit=(54 << 20) - (700 << 10),
+    )
+    token_rows = after(tokens, packed_a).reshape(rows, width)
+    full, edge = call(
+        functools.partial(normalise_kernel, n_ctx),
+        "normalise",
+        [((rows + 8, width), bf16), ((16, columns), bf16)],
         [
-            ((rows + 8, width), bf16),
-            ((quarter, packed), bf16),
-            ((quarter + 16, packed), bf16),
-        ],
-        [
-            (SMEM, block_mask[0]),
+            (ANY, block_mask[0]),
             (VMEM, token_rows),
             (VMEM, norm_gain.reshape(1, width)),
-        ]
-        + [(ANY, w) for w in (w_up, w_query, w_key, w_value)],
-        [pltpu.SemaphoreType.DMA((8,))],
-        limit=None,
-    )
-    (near,) = call(
-        functools.partial(pack_near_kernel, n_ctx),
-        "pack_near",
-        [((depth, packed), bf16)],
-        [(ANY, w) for w in (second, w_up, w_query, w_key, w_value)],
-        [pltpu.SemaphoreType.DMA((4,))],
+        ],
+        [pltpu.SMEM((1, n_ctx), jnp.int32), pltpu.SemaphoreType.DMA((1,))],
     )
     block = two_ways(full, (1, 2))
-    piece = lax.dynamic_slice_in_dim(block, tp * (rows // 2), rows // 2 + 8, 0)
+    (piece,) = call(split_kernel, "split", [((rows // 2 + 8, width), bf16)], [(VMEM, block)])
     piece = two_ways(piece, (2, 1))
-    x_first = across(first, "tm", 1)
-    x_second = across(second, "tm", 1)
-    y_first = across(x_first, "groups", 1)
-    y_second = across(x_second, "groups", 1)
+    x_a = across(packed_a, "tm", 1)
+    y_a = across(x_a, "groups", 1)
+    halo = across(edge, "tm", 1)
     other_block = across(block, "tp", 1)
     other_piece = across(piece, "tp", 1)
     half_down = w_down.shape[0] // 2
     sent_down = lax.dynamic_slice_in_dim(w_down, groups * half_down, half_down, 0)
-    sent_down, sent_out, _ = lax.optimization_barrier(
-        (sent_down, w_out, (second,))
-    )
-    x_down = across(sent_down, "tm", 1)
-    x_out = across(sent_out, "tm", 1)
+    x_down = across(after(sent_down, packed_a), "tm", 1)
+    x_out = across(after(w_out, packed_a), "tm", 1)
 
     (base,) = call(
         functools.partial(convolve_kernel, dancers_here),
@@ -328,10 +324,17 @@
         [
             (VMEM, token_rows),
             (VMEM, full),
-            (VMEM, x_second),
+            (VMEM, halo),
             (VMEM, conv_weight),
         ],
         [pltpu.VMEM((rows + 32, columns), f32)],
+    )
+    (near,) = call(
+        functools.partial(pack_near_kernel, n_ctx),
+        "pack_near",
+        [((depth, packed), bf16)],
+        [(ANY, w) for w in (base, w_up, w_query, w_key, w_value)],
+        [pltpu.SemaphoreType.DMA((4,))],
     )
     *acts, queries, keys, values, bias = call(
         functools.partial(project_kernel, n_ctx),
@@ -340,13 +343,12 @@
         + [((n_ctx * rows, wide), bf16)] * 2
         + [((wide, n_ctx * rows), bf16), ((8 * n_ctx, n_ctx * LANES), f32)],
         [(VMEM, value) for value in (full, block, other_block, piece, other_piece)]
-        + [(VMEM, value) for value in (near, x_first, x_second, y_first, y_second)],
+        + [(VMEM, value) for value in (near, x_a, y_a)],
         [
             pltpu.VMEM((n_ctx * rows, width), bf16),
-            pltpu.VMEM((depth, packed), bf16),
         ],
-        flops=8 * n_ctx * rows * width * packed,
-        moved=64 << 20,
+        flops=2 * n_ctx * rows * width * packed,
+        moved=4 << 20,
         transcendentals=n_ctx * rows * hidden,
     )
     parts = [None] * n_ctx
@@ -359,10 +361,9 @@
             flops=4 * wide * n_ctx * rows * rows,
             transcendentals=(wide // HEAD_DIM) * n_ctx * rows * rows,
         )
-        if i == 1:
-            x_down, part = lax.optimization_barrier((x_down, part))
-        parts[i] = across(part, "ctx", i) if i else part
-    y_down = across(x_down, "groups", 1)
+        parts[i] = part
+    y_down = across(after(x_down, queries), "groups", 1)
+    parts = parts[:1] + [across(parts[i], "ctx", i) for i in range(1, n_ctx)]
     keep, send = call(
         functools.partial(join_kernel, n_ctx),
         "join",

time: 51.5 us -> 46.8 us (0.909)
  local copies, waits for them, and re-layouts: 5.42 us -> 1.57 us
  Pallas kernels: 9.59 us -> 8.34 us
    reshape x1, local copies, waits for them, and re-layouts: 1.76 us -> 0.1 us  [split_over_ctx(): token_rows = after(tokens, packed_a).reshape(rows, width)]
    ppermute x13 -> x12, starting transfers between devices: 12.4 us -> 13.9 us  [across(): lax.ppermute(value, axis, [(source, source ^ step) for source in range(co...]
    unnamed x20, local copies, waits for them, and re-layouts: 1.99 us -> 0.73 us
    pallas_call x9 -> x11, Pallas kernels: 9.59 us -> 8.34 us  [call(): pl.pallas_call(kernel, out_shape=[jax.ShapeDtypeStruct(shape, dtype) for...]
    ppermute x2, starting transfers between devices: 5.46 us -> 4.3 us  [two_ways(): return lax.ppermute(value, ('ctx', 'tp'), pairs)]
    dynamic_slice x1 -> x0, local copies, waits for them, and re-layouts: 0.92 us -> none  [split_over_ctx(): piece = lax.dynamic_slice_in_dim(block, tp * (rows // 2), rows // 2 + 8, 0)]
    ppermute x13 -> x12, waiting for transfers between devices: 12.5 us -> 13.3 us  [across(): lax.ppermute(value, axis, [(source, source ^ step) for source in range(co...]
    ppermute x2, waiting for transfers between devices: 5.62 us -> 5.03 us  [two_ways(): return lax.ppermute(value, ('ctx', 'tp'), pairs)]
  transfers between devices with their start and end apart: 15 -> 14, of which waited for: 6 -> 8; matrix products, arithmetic and copies ran while one was open for 2% -> 0% of each run, Pallas kernels for 11% -> 13%
where the time goes in v4:
time: 46.8 us; the launch traced here: 46.7 us
  waiting for transfers between devices  18.3 us (39%)
  starting transfers between devices  18.2 us (39%)
  Pallas kernels  8.34 us (18%)
  local copies, waits for them, and re-layouts  1.57 us (3%)
    ppermute x12, starting transfers between devices, across(): lax.ppermute(value, axis, [(source, source ^ step) for source in range(co...  13.9 us
    ppermute x12, waiting for transfers between devices, across(): lax.ppermute(value, axis, [(source, source ^ step) for source in range(co...  13.3 us
    pallas_call x11, Pallas kernels, call(): pl.pallas_call(kernel, out_shape=[jax.ShapeDtypeStruct(shape, dtype) for...  8.34 us
    ppermute x2, waiting for transfers between devices, two_ways(): return lax.ppermute(value, ('ctx', 'tp'), pairs)  5.03 us
    ppermute x2, starting transfers between devices, two_ways(): return lax.ppermute(value, ('ctx', 'tp'), pairs)  4.3 us
  transfers between devices with their start and end apart: 14, of which 8 were waited for; matrix products, arithmetic and copies ran while one was open for 0% of the time, Pallas kernels for 13%

profile of v4, /device:TPU:0, one launch (start us, length us, event | category | flops | bytes accessed | tf_op | source)
XLA Modules:
  0.0 46.7 jit_solution(1536543553345098452)
XLA Ops:
  0.0 1.1 %pack.1 = bf16[256,640]{1,0:T(8,128)(2,1)S(1)} custom-call(bf16[512,1024]{1,0:T(8,128)(2,1)} %w_up.3, bf16[512,512]{1,0:T(8,128)(2,1)} %w_query.3, bf16[512,512]{1,0:T(8,128)(2,1)} %w_key.3, bf16[512,512]{1,0:T(8,128)(2,1)} %w_value.3), custom_call_target="tpu_custom_call" | custom-call | bytes 1048576 | tf_op jit(solution)/shard_map/pack/pallas_call | solution.py:255
  1.2 3.0 %collective-permute-start.6 = (bf16[256,640]{1,0:T(8,128)(2,1)S(1)}, bf16[256,640]{1,0:T(8,128)(2,1)}, u32[]{:S(2)}, u32[]{:S(2)}) collective-permute-start(bf16[256,640]{1,0:T(8,128)(2,1)S(1)} %pack.1), channel_id=1, source_target_pairs={{0,2},{2,0},{1,3},{3,1},{4,6},{6,4},{5,7},{7,5},{8,10},{10,8},{9,1... | collective-permute-start | bytes 983048 | tf_op jit(solution)/shard_map/ppermute | solution.py:31
  4.3 0.7 %copy-done.8 = s32[1,1,4]{2,1,0:T(1,128)S(1)} copy-done((s32[1,1,4]{2,1,0:T(1,128)S(1)}, s32[1,1,4]{2,1,0:T(1,128)}, u32[]{:S(2)}) %copy-start.8) | copy-done | bytes 40
  5.6 1.6 %collective-permute-start.2 = (bf16[136,1024]{1,0:T(8,128)(2,1)S(1)}, bf16[136,1024]{1,0:T(8,128)(2,1)S(1)}, u32[]{:S(2)}, u32[]{:S(2)}) collective-permute-start(bf16[136,1024]{1,0:T(8,128)(2,1)S(1)} %get-tuple-element.22.full.refs_0_), channel_id=1, source_target_pairs={{0,4},{1,9},{4,0},{5,13},{8,12},{9,1},{12,8},{13,5},{2,6},{3,11},{... | collective-permute-start | bytes 835592 | tf_op jit(solution)/shard_map/ppermute | solution.py:40
  7.9 5.0 %collective-permute-done.6.refs_6_ = bf16[256,640]{1,0:T(8,128)(2,1)} collective-permute-done((bf16[256,640]{1,0:T(8,128)(2,1)S(1)}, bf16[256,640]{1,0:T(8,128)(2,1)}, u32[]{:S(2)}, u32[]{:S(2)}) %collective-permute-start.6) | collective-permute-done | bytes 327712 | tf_op jit(solution)/shard_map/ppermute | solution.py:31
  12.8 2.1 %collective-permute-start.7 = (bf16[256,640]{1,0:T(8,128)(2,1)}, bf16[256,640]{1,0:T(8,128)(2,1)S(1)}, u32[]{:S(2)}, u32[]{:S(2)}) collective-permute-start(bf16[256,640]{1,0:T(8,128)(2,1)} %collective-permute-done.6.refs_6_), channel_id=1, source_target_pairs={{0,16},{16,0},{1,17},{17,1},{2,18},{18,2},{3,19},{19,3},{4,20},{20... | collective-permute-start | bytes 983048 | tf_op jit(solution)/shard_map/ppermute | solution.py:31
  15.0 2.7 %collective-permute-start.4 = (bf16[72,1024]{1,0:T(8,128)(2,1)S(1)}, bf16[72,1024]{1,0:T(8,128)(2,1)S(1)}, u32[]{:S(2)}, u32[]{:S(2)}) collective-permute-start(bf16[72,1024]{1,0:T(8,128)(2,1)S(1)} %split.1), channel_id=1, source_target_pairs={{0,8},{1,5},{4,12},{5,1},{8,0},{9,13},{12,4},{13,9},{2,10},{3,7},{... | collective-permute-start | bytes 442376 | tf_op jit(solution)/shard_map/ppermute | solution.py:40
  17.6 5.0 %collective-permute-done.4.refs_3_ = bf16[72,1024]{1,0:T(8,128)(2,1)S(1)} collective-permute-done((bf16[72,1024]{1,0:T(8,128)(2,1)S(1)}, bf16[72,1024]{1,0:T(8,128)(2,1)S(1)}, u32[]{:S(2)}, u32[]{:S(2)}) %collective-permute-start.4) | collective-permute-done | bytes 147488 | tf_op jit(solution)/shard_map/ppermute | solution.py:40
  22.6 1.5 %collective-permute-start = (bf16[16,512]{1,0:T(8,128)(2,1)S(1)}, bf16[16,512]{1,0:T(8,128)(2,1)S(1)}, u32[]{:S(2)}, u32[]{:S(2)}) collective-permute-start(bf16[16,512]{1,0:T(8,128)(2,1)S(1)} %get-tuple-element.23), channel_id=1, source_target_pairs={{0,2},{2,0},{1,3},{3,1},{4,6},{6,4},{5,7},{7,5},{8,10},{10,8},{9,1... | collective-permute-start | bytes 49160 | tf_op jit(solution)/shard_map/ppermute | solution.py:31
  24.1 2.2 %collective-permute-done.halo = bf16[16,512]{1,0:T(8,128)(2,1)S(1)} collective-permute-done((bf16[16,512]{1,0:T(8,128)(2,1)S(1)}, bf16[16,512]{1,0:T(8,128)(2,1)S(1)}, u32[]{:S(2)}, u32[]{:S(2)}) %collective-permute-start) | collective-permute-done | bytes 16416 | tf_op jit(solution)/shard_map/ppermute | solution.py:31
  26.4 1.5 %collective-permute-start.9 = (bf16[512,512]{1,0:T(8,128)(2,1)S(1)}, bf16[512,512]{1,0:T(8,128)(2,1)S(1)}, u32[]{:S(2)}, u32[]{:S(2)}) collective-permute-start(bf16[512,512]{1,0:T(8,128)(2,1)S(1)} %copy-done.5), channel_id=1, source_target_pairs={{0,2},{2,0},{1,3},{3,1},{4,6},{6,4},{5,7},{7,5},{8,10},{10,8},{9,1... | collective-permute-start | bytes 1572872 | tf_op jit(solution)/shard_map/ppermute | solution.py:31
  28.4 2.1 %project.1 = (bf16[128,256]{1,0:T(8,128)(2,1)S(1)}, bf16[128,256]{1,0:T(8,128)(2,1)S(1)}, bf16[128,256]{1,0:T(8,128)(2,1)S(1)}, bf16[128,256]{1,0:T(8,128)(2,1)S...) custom-call(bf16[136,1024]{1,0:T(8,128)(2,1)S(1)} %get-tuple-element, ...), custom_call_target="tpu_custom_call" | custom-call | flops 671088640 | bytes 4194304 | tf_op jit(solution)/shard_map/project/pallas_call | solution.py:255
  31.1 0.8 %attend.7 = bf16[128,384]{1,0:T(8,128)(2,1)S(1)} custom-call(bf16[128,256]{1,0:T(8,128)(2,1)S(1)} %get-tuple-element.34.activated, bf16[512,128]{1,0:T(8,128)(2,1)S(1)} %get-tuple-element.25.queries, bf16[512,128]{1,0:T(8,128)(2,1)S(1)} %get-tuple-element.29.keys, bf16[128,512]{1,0:T(8,128)(2,1)S(1)} %get-tuple-element.30.values, ...), custom_call_target="tpu_custom_call" | custom-call | flops 33554432 | bytes 1048576 | tf_op jit(solution)/shard_map/attend/pallas_call | solution.py:255
  31.8 3.6 %collective-permute-start.12 = (bf16[128,384]{1,0:T(8,128)(2,1)S(1)}, bf16[128,384]{1,0:T(8,128)(2,1)S(1)}, u32[]{:S(2)}, u32[]{:S(2)}) collective-permute-start(bf16[128,384]{1,0:T(8,128)(2,1)S(1)} %attend.7), channel_id=1, source_target_pairs={{0,12},{4,8},{8,4},{12,0},{1,13},{5,9},{9,5},{13,1},{2,14},{6,10},... | collective-permute-start | bytes 294920 | tf_op jit(solution)/shard_map/ppermute | solution.py:31
  35.4 0.8 %attend.6 = bf16[128,384]{1,0:T(8,128)(2,1)S(1)} custom-call(bf16[128,256]{1,0:T(8,128)(2,1)S(1)} %get-tuple-element.33.activated, bf16[512,128]{1,0:T(8,128)(2,1)S(1)} %get-tuple-element.25.queries, bf16[512,128]{1,0:T(8,128)(2,1)S(1)} %get-tuple-element.29.keys, bf16[128,512]{1,0:T(8,128)(2,1)S(1)} %get-tuple-element.30.values, ...), custom_call_target="tpu_custom_call" | custom-call | flops 33554432 | bytes 1048576 | tf_op jit(solution)/shard_map/attend/pallas_call | solution.py:255
  36.2 0.8 %attend.5 = bf16[128,384]{1,0:T(8,128)(2,1)S(1)} custom-call(bf16[128,256]{1,0:T(8,128)(2,1)S(1)} %get-tuple-element.32.activated, bf16[512,128]{1,0:T(8,128)(2,1)S(1)} %get-tuple-element.25.queries, bf16[512,128]{1,0:T(8,128)(2,1)S(1)} %get-tuple-element.29.keys, bf16[128,512]{1,0:T(8,128)(2,1)S(1)} %get-tuple-element.30.values, ...), custom_call_target="tpu_custom_call" | custom-call | flops 33554432 | bytes 1048576 | tf_op jit(solution)/shard_map/attend/pallas_call | solution.py:255
  37.0 0.9 %collective-permute-start.10 = (bf16[128,384]{1,0:T(8,128)(2,1)S(1)}, bf16[128,384]{1,0:T(8,128)(2,1)S(1)}, u32[]{:S(2)}, u32[]{:S(2)}) collective-permute-start(bf16[128,384]{1,0:T(8,128)(2,1)S(1)} %attend.5), channel_id=1, source_target_pairs={{0,4},{4,0},{8,12},{12,8},{1,5},{5,1},{9,13},{13,9},{2,6},{6,2},{1... | collective-permute-start | bytes 294920 | tf_op jit(solution)/shard_map/ppermute | solution.py:31
  38.0 0.8 %attend.4.refs_6_ = bf16[128,384]{1,0:T(8,128)(2,1)S(1)} custom-call(bf16[128,256]{1,0:T(8,128)(2,1)S(1)} %get-tuple-element.28.activated, bf16[512,128]{1,0:T(8,128)(2,1)S(1)} %get-tuple-element.25.queries, bf16[512,128]{1,0:T(8,128)(2,1)S(1)} %get-tuple-element.29.keys, bf16[128,512]{1,0:T(8,128)(2,1)S(1)} %get-tuple-element.30.values, ...), custom_call_target="tpu_custom_call" | custom-call | flops 33554432 | bytes 1048576 | tf_op jit(solution)/shard_map/attend/pallas_call | solution.py:255
  38.7 0.8 %collective-permute-done.9.refs_5_ = bf16[512,512]{1,0:T(8,128)(2,1)S(1)} collective-permute-done((bf16[512,512]{1,0:T(8,128)(2,1)S(1)}, bf16[512,512]{1,0:T(8,128)(2,1)S(1)}, u32[]{:S(2)}, u32[]{:S(2)}) %collective-permute-start.9) | collective-permute-done | bytes 524320 | tf_op jit(solution)/shard_map/ppermute | solution.py:31
  39.6 3.0 %collective-permute-done.11.refs_8_ = bf16[128,384]{1,0:T(8,128)(2,1)S(1)} collective-permute-done((bf16[128,384]{1,0:T(8,128)(2,1)S(1)}, bf16[128,384]{1,0:T(8,128)(2,1)S(1)}, u32[]{:S(2)}, u32[]{:S(2)}) %collective-permute-start.11) | collective-permute-done | bytes 98336 | tf_op jit(solution)/shard_map/ppermute | solution.py:31
  42.6 0.6 %collective-permute-done.10.refs_7_ = bf16[128,384]{1,0:T(8,128)(2,1)S(1)} collective-permute-done((bf16[128,384]{1,0:T(8,128)(2,1)S(1)}, bf16[128,384]{1,0:T(8,128)(2,1)S(1)}, u32[]{:S(2)}, u32[]{:S(2)}) %collective-permute-start.10) | collective-permute-done | bytes 98336 | tf_op jit(solution)/shard_map/ppermute | solution.py:31
  43.5 1.0 %join.1 = (f32[128,512]{1,0:T(8,128)S(1)}, bf16[128,512]{1,0:T(8,128)(2,1)S(1)}) custom-call(bf16[1024,512]{1,0:T(8,128)(2,1)S(1)} %copy-done.1, bf16[512,512]{1,0:T(8,128)(2,1)S(1)} %copy-done.5, f32[128,512]{1,0:T(8,128)S(1)} %convolve.1.after.refs_2_, bf16[512,512]{1,0:T(8,128)(2,1)S(1)} %collective-permute-done.1.refs_3_, ...), custom_call_target="tpu_custom_call" | custom-call | flops 402653184 | bytes 4194304 | tf_op jit(solution)/shard_map/join/pallas_call | solution.py:255
  44.6 1.3 %collective-permute-done.13 = bf16[128,512]{1,0:T(8,128)(2,1)S(1)} collective-permute-done((bf16[128,512]{1,0:T(8,128)(2,1)S(1)}, bf16[128,512]{1,0:T(8,128)(2,1)S(1)}, u32[]{:S(2)}, u32[]{:S(2)}) %collective-permute-start.13) | collective-permute-done | bytes 131104 | tf_op jit(solution)/shard_map/ppermute | solution.py:31
  46.0 0.7 %reshape.11 = bf16[64,2,512]{2,1,0:T(2,128)(2,1)} reshape(bf16[128,512]{1,0:T(8,128)(2,1)S(1)} %add_convert_fusion) | data formatting | bytes 262144 | tf_op jit(solution)/shard_map/reshape | solution.py:385
  (39 shorter events, 2.8 us)
Async XLA Ops:
  0.0 4.2 %copy-start.9 = (bf16[64,2,1024]{2,1,0:T(2,128)(2,1)S(1)}, bf16[64,2,1024]{2,1,0:T(2,128)(2,1)}, u32[]{:S(2)}) copy-start(bf16[64,2,1024]{2,1,0:T(2,128)(2,1)} %param.10) | copy-start | bytes 786436
  0.0 4.3 %copy-start.7 = (f32[1024]{0:T(1024)S(1)}, f32[1024]{0:T(1024)}, u32[]{:S(2)}) copy-start(f32[1024]{0:T(1024)} %param.11) | copy-start | bytes 12292
  0.0 7.2 %copy-start.1 = (bf16[1024,512]{1,0:T(8,128)(2,1)S(1)}, bf16[1024,512]{1,0:T(8,128)(2,1)}, u32[]{:S(2)}) copy-start(bf16[1024,512]{1,0:T(8,128)(2,1)} %refs_0_.1) | copy-start | bytes 3145732
  0.0 26.4 %copy-start.5 = (bf16[512,512]{1,0:T(8,128)(2,1)S(1)}, bf16[512,512]{1,0:T(8,128)(2,1)}, u32[]{:S(2)}) copy-start(bf16[512,512]{1,0:T(8,128)(2,1)} %refs_1_.1) | copy-start | bytes 1572868
  1.2 11.7 %collective-permute-start.6 = (bf16[256,640]{1,0:T(8,128)(2,1)S(1)}, bf16[256,640]{1,0:T(8,128)(2,1)}, u32[]{:S(2)}, u32[]{:S(2)}) collective-permute-start(bf16[256,640]{1,0:T(8,128)(2,1)S(1)} %pack.1), channel_id=1, source_target_pairs={{0,2},{2,0},{1,3},{3,1},{4,6},{6,4},{5,7},{7,5},{8,10},{10,8},{9,1... | collective-permute-start | bytes 983048 | tf_op jit(solution)/shard_map/ppermute | solution.py:31
  4.2 24.0 %copy-start.4 = (bf16[512,512]{1,0:T(8,128)(2,1)S(1)}, bf16[512,512]{1,0:T(8,128)(2,1)}, u32[]{:S(2)}) copy-start(bf16[512,512]{1,0:T(8,128)(2,1)} %w_value.3) | copy-start | bytes 1572868
  4.3 0.7 %copy-start.8 = (s32[1,1,4]{2,1,0:T(1,128)S(1)}, s32[1,1,4]{2,1,0:T(1,128)}, u32[]{:S(2)}) copy-start(s32[1,1,4]{2,1,0:T(1,128)} %param.12) | copy-start | bytes 52
  5.6 9.3 %collective-permute-start.2 = (bf16[136,1024]{1,0:T(8,128)(2,1)S(1)}, bf16[136,1024]{1,0:T(8,128)(2,1)S(1)}, u32[]{:S(2)}, u32[]{:S(2)}) collective-permute-start(bf16[136,1024]{1,0:T(8,128)(2,1)S(1)} %get-tuple-element.22.full.refs_0_), channel_id=1, source_target_pairs={{0,4},{1,9},{4,0},{5,13},{8,12},{9,1},{12,8},{13,5},{2,6},{3,11},{... | collective-permute-start | bytes 835592 | tf_op jit(solution)/shard_map/ppermute | solution.py:40
  7.2 21.0 %copy-start = (bf16[512,1024]{1,0:T(8,128)(2,1)S(1)}, bf16[512,1024]{1,0:T(8,128)(2,1)}, u32[]{:S(2)}) copy-start(bf16[512,1024]{1,0:T(8,128)(2,1)} %w_up.3) | copy-start | bytes 3145732
  7.3 20.6 %copy-start.6 = (f32[5,512]{1,0:T(8,128)S(1)}, f32[5,512]{1,0:T(8,128)}, u32[]{:S(2)}) copy-start(f32[5,512]{1,0:T(8,128)} %taps.1) | copy-start | bytes 30724
  7.3 23.2 %collective-permute-start.1 = (bf16[512,512]{1,0:T(8,128)(2,1)S(1)}, bf16[512,512]{1,0:T(8,128)(2,1)S(1)}, u32[]{:S(2)}, u32[]{:S(2)}) collective-permute-start(bf16[512,512]{1,0:T(8,128)(2,1)S(1)} %constant_dynamic-slice_fusion), channel_id=1, source_target_pairs={{0,2},{2,0},{1,3},{3,1},{4,6},{6,4},{5,7},{7,5},{8,10},{10,8},{9,1... | collective-permute-start | bytes 1572872 | tf_op jit(solution)/shard_map/ppermute | solution.py:31
  12.8 15.6 %collective-permute-start.7 = (bf16[256,640]{1,0:T(8,128)(2,1)}, bf16[256,640]{1,0:T(8,128)(2,1)S(1)}, u32[]{:S(2)}, u32[]{:S(2)}) collective-permute-start(bf16[256,640]{1,0:T(8,128)(2,1)} %collective-permute-done.6.refs_6_), channel_id=1, source_target_pairs={{0,16},{16,0},{1,17},{17,1},{2,18},{18,2},{3,19},{19,3},{4,20},{20... | collective-permute-start | bytes 983048 | tf_op jit(solution)/shard_map/ppermute | solution.py:31
  14.9 13.3 %copy-start.3 = (bf16[512,512]{1,0:T(8,128)(2,1)S(1)}, bf16[512,512]{1,0:T(8,128)(2,1)}, u32[]{:S(2)}) copy-start(bf16[512,512]{1,0:T(8,128)(2,1)} %w_key.3) | copy-start | bytes 1572868
  14.9 13.2 %copy-start.2 = (bf16[512,512]{1,0:T(8,128)(2,1)S(1)}, bf16[512,512]{1,0:T(8,128)(2,1)}, u32[]{:S(2)}) copy-start(bf16[512,512]{1,0:T(8,128)(2,1)} %w_query.3) | copy-start | bytes 1572868
  15.0 7.7 %collective-permute-start.4 = (bf16[72,1024]{1,0:T(8,128)(2,1)S(1)}, bf16[72,1024]{1,0:T(8,128)(2,1)S(1)}, u32[]{:S(2)}, u32[]{:S(2)}) collective-permute-start(bf16[72,1024]{1,0:T(8,128)(2,1)S(1)} %split.1), channel_id=1, source_target_pairs={{0,8},{1,5},{4,12},{5,1},{8,0},{9,13},{12,4},{13,9},{2,10},{3,7},{... | collective-permute-start | bytes 442376 | tf_op jit(solution)/shard_map/ppermute | solution.py:40
  17.6 10.8 %collective-permute-start.3 = (bf16[136,1024]{1,0:T(8,128)(2,1)S(1)}, bf16[136,1024]{1,0:T(8,128)(2,1)S(1)}, u32[]{:S(2)}, u32[]{:S(2)}) collective-permute-start(bf16[136,1024]{1,0:T(8,128)(2,1)S(1)} %collective-permute-done.2.block.refs_1_), channel_id=1, source_target_pairs={{0,1},{1,0},{2,3},{3,2},{4,5},{5,4},{6,7},{7,6},{8,9},{9,8},{10,11... | collective-permute-start | bytes 835592 | tf_op jit(solution)/shard_map/ppermute | solution.py:31
  22.6 5.7 %collective-permute-start.5 = (bf16[72,1024]{1,0:T(8,128)(2,1)S(1)}, bf16[72,1024]{1,0:T(8,128)(2,1)S(1)}, u32[]{:S(2)}, u32[]{:S(2)}) collective-permute-start(bf16[72,1024]{1,0:T(8,128)(2,1)S(1)} %collective-permute-done.4.refs_3_), channel_id=1, source_target_pairs={{0,1},{1,0},{2,3},{3,2},{4,5},{5,4},{6,7},{7,6},{8,9},{9,8},{10,11... | collective-permute-start | bytes 442376 | tf_op jit(solution)/shard_map/ppermute | solution.py:31
  22.6 3.7 %collective-permute-start = (bf16[16,512]{1,0:T(8,128)(2,1)S(1)}, bf16[16,512]{1,0:T(8,128)(2,1)S(1)}, u32[]{:S(2)}, u32[]{:S(2)}) collective-permute-start(bf16[16,512]{1,0:T(8,128)(2,1)S(1)} %get-tuple-element.23), channel_id=1, source_target_pairs={{0,2},{2,0},{1,3},{3,1},{4,6},{6,4},{5,7},{7,5},{8,10},{10,8},{9,1... | collective-permute-start | bytes 49160 | tf_op jit(solution)/shard_map/ppermute | solution.py:31
  26.4 13.2 %collective-permute-start.9 = (bf16[512,512]{1,0:T(8,128)(2,1)S(1)}, bf16[512,512]{1,0:T(8,128)(2,1)S(1)}, u32[]{:S(2)}, u32[]{:S(2)}) collective-permute-start(bf16[512,512]{1,0:T(8,128)(2,1)S(1)} %copy-done.5), channel_id=1, source_target_pairs={{0,2},{2,0},{1,3},{3,1},{4,6},{6,4},{5,7},{7,5},{8,10},{10,8},{9,1... | collective-permute-start | bytes 1572872 | tf_op jit(solution)/shard_map/ppermute | solution.py:31
  30.5 13.0 %collective-permute-start.8 = (bf16[512,512]{1,0:T(8,128)(2,1)S(1)}, bf16[512,512]{1,0:T(8,128)(2,1)S(1)}, u32[]{:S(2)}, u32[]{:S(2)}) collective-permute-start(bf16[512,512]{1,0:T(8,128)(2,1)S(1)} %collective-permute-done.1.refs_3_), channel_id=1, source_target_pairs={{0,16},{16,0},{1,17},{17,1},{2,18},{18,2},{3,19},{19,3},{4,20},{20... | collective-permute-start | bytes 1572872 | tf_op jit(solution)/shard_map/ppermute | solution.py:31
  31.8 7.7 %collective-permute-start.12 = (bf16[128,384]{1,0:T(8,128)(2,1)S(1)}, bf16[128,384]{1,0:T(8,128)(2,1)S(1)}, u32[]{:S(2)}, u32[]{:S(2)}) collective-permute-start(bf16[128,384]{1,0:T(8,128)(2,1)S(1)} %attend.7), channel_id=1, source_target_pairs={{0,12},{4,8},{8,4},{12,0},{1,13},{5,9},{9,5},{13,1},{2,14},{6,10},... | collective-permute-start | bytes 294920 | tf_op jit(solution)/shard_map/ppermute | solution.py:31
  36.2 6.4 %collective-permute-start.11 = (bf16[128,384]{1,0:T(8,128)(2,1)S(1)}, bf16[128,384]{1,0:T(8,128)(2,1)S(1)}, u32[]{:S(2)}, u32[]{:S(2)}) collective-permute-start(bf16[128,384]{1,0:T(8,128)(2,1)S(1)} %attend.6), channel_id=1, source_target_pairs={{0,8},{4,12},{8,0},{12,4},{1,9},{5,13},{9,1},{13,5},{2,10},{6,14},... | collective-permute-start | bytes 294920 | tf_op jit(solution)/shard_map/ppermute | solution.py:31
  37.0 6.2 %collective-permute-start.10 = (bf16[128,384]{1,0:T(8,128)(2,1)S(1)}, bf16[128,384]{1,0:T(8,128)(2,1)S(1)}, u32[]{:S(2)}, u32[]{:S(2)}) collective-permute-start(bf16[128,384]{1,0:T(8,128)(2,1)S(1)} %attend.5), channel_id=1, source_target_pairs={{0,4},{4,0},{8,12},{12,8},{1,5},{5,1},{9,13},{13,9},{2,6},{6,2},{1... | collective-permute-start | bytes 294920 | tf_op jit(solution)/shard_map/ppermute | solution.py:31
  44.5 1.4 %collective-permute-start.13 = (bf16[128,512]{1,0:T(8,128)(2,1)S(1)}, bf16[128,512]{1,0:T(8,128)(2,1)S(1)}, u32[]{:S(2)}, u32[]{:S(2)}) collective-permute-start(bf16[128,512]{1,0:T(8,128)(2,1)S(1)} %get-tuple-element.36), channel_id=1, source_target_pairs={{0,1},{1,0},{2,3},{3,2},{4,5},{5,4},{6,7},{7,6},{8,9},{9,8},{10,11... | collective-permute-start | bytes 393224 | tf_op jit(solution)/shard_map/ppermute | solution.py:31

commit v5 on v4

--- a/solution.py
+++ b/solution.py
@@ -121,12 +121,12 @@
     end(begin(sems, pairs))
 
 
-def convolve_kernel(per_frame, tokens, full, halo, taps, base, held):
+def convolve_kernel(per_frame, tokens, full, received, taps, base, held):
     tm, tp = lax.axis_index("tm"), lax.axis_index("tp")
     rows, columns = base.shape
     edge = 16
     margin = 2 * per_frame
-    near = halo[...].astype(jnp.float32)
+    near = received[received.shape[0] - edge :, :].astype(jnp.float32)
     zeros = jnp.zeros((edge, columns), jnp.float32)
     held[0:edge, :] = jnp.where(tm == 1, near, zeros)
     held[edge : edge + rows, :] = full[0:rows, slot(tp, columns)].astype(jnp.float32)
@@ -224,14 +224,14 @@
     keep, send, down, out, acts, atts, sems = refs[6 + n_ctx :]
     ctx, tm, groups, tp = (lax.axis_index(name) for name in AXES)
     hidden, wide = acts.shape[1] // n_ctx, atts.shape[1] // n_ctx
-    count = far_down.shape[0]
+    count = near_down.shape[0] // 2
     pairs = []
     for d in range(n_ctx):
         pairs.append((parts[d].at[:, 0:hidden], acts.at[:, slot(ctx ^ d, hidden)]))
         pairs.append((parts[d].at[:, hidden:], atts.at[:, slot(ctx ^ d, wide)]))
     pairs.append((far_out, out))
-    pairs.append((far_down, down.at[slot(groups, count)]))
-    pairs.append((farther_down, down.at[slot(1 - groups, count)]))
+    pairs.append((far_down.at[0:count], down.at[slot(groups, count)]))
+    pairs.append((farther_down.at[0:count], down.at[slot(1 - groups, count)]))
     copies = begin(sems, pairs)
 
     end(copies[: 2 * n_ctx])
@@ -304,38 +304,26 @@
         ],
         [pltpu.SMEM((1, n_ctx), jnp.int32), pltpu.SemaphoreType.DMA((1,))],
     )
-    block = two_ways(full, (1, 2))
-    (piece,) = call(split_kernel, "split", [((rows // 2 + 8, width), bf16)], [(VMEM, block)])
-    piece = two_ways(piece, (2, 1))
     x_a = across(packed_a, "tm", 1)
     y_a = across(x_a, "groups", 1)
-    halo = across(edge, "tm", 1)
-    other_block = across(block, "tp", 1)
-    other_piece = across(piece, "tp", 1)
     half_down = w_down.shape[0] // 2
     sent_down = lax.dynamic_slice_in_dim(w_down, groups * half_down, half_down, 0)
+    sent_down = jnp.concatenate([sent_down, edge], axis=0)
     x_down = across(after(sent_down, packed_a), "tm", 1)
     x_out = across(after(w_out, packed_a), "tm", 1)
 
-    (base,) = call(
-        functools.partial(convolve_kernel, dancers_here),
-        "convolve",
-        [((rows, columns), f32)],
-        [
-            (VMEM, token_rows),
-            (VMEM, full),
-            (VMEM, halo),
-            (VMEM, conv_weight),
-        ],
-        [pltpu.VMEM((rows + 32, columns), f32)],
-    )
     (near,) = call(
         functools.partial(pack_near_kernel, n_ctx),
         "pack_near",
         [((depth, packed), bf16)],
-        [(ANY, w) for w in (base, w_up, w_query, w_key, w_value)],
+        [(ANY, w) for w in (packed_a, w_up, w_query, w_key, w_value)],
         [pltpu.SemaphoreType.DMA((4,))],
     )
+    block = two_ways(full, (1, 2))
+    other_block = across(block, "tp", 1)
+    (piece,) = call(split_kernel, "split", [((rows // 2 + 8, width), bf16)], [(VMEM, block)])
+    piece = two_ways(piece, (2, 1))
+    other_piece = across(piece, "tp", 1)
     *acts, queries, keys, values, bias = call(
         functools.partial(project_kernel, n_ctx),
         "project",
@@ -364,6 +352,18 @@
         parts[i] = part
     y_down = across(after(x_down, queries), "groups", 1)
     parts = parts[:1] + [across(parts[i], "ctx", i) for i in range(1, n_ctx)]
+    (base,) = call(
+        functools.partial(convolve_kernel, dancers_here),
+        "convolve",
+        [((rows, columns), f32)],
+        [
+            (VMEM, token_rows),
+            (VMEM, full),
+            (VMEM, x_down),
+            (VMEM, conv_weight),
+        ],
+        [pltpu.VMEM((rows + 32, columns), f32)],
+    )
     keep, send = call(
         functools.partial(join_kernel, n_ctx),
         "join",

time: 46.8 us -> 42.9 us (0.917)
  starting transfers between devices: 18.2 us -> 16.7 us
  Pallas kernels: 8.34 us -> 7.32 us
  waiting for transfers between devices: 18.3 us -> 17.6 us
  local copies, waits for them, and re-layouts: 1.57 us -> 0.9 us
    ppermute x12 -> x11, starting transfers between devices: 13.9 us -> 12.4 us  [across(): lax.ppermute(value, axis, [(source, source ^ step) for source in range(co...]
    pallas_call x11, Pallas kernels: 8.34 us -> 7.32 us  [call(): pl.pallas_call(kernel, out_shape=[jax.ShapeDtypeStruct(shape, dtype) for...]
    ppermute x12 -> x11, waiting for transfers between devices: 13.3 us -> 12.5 us  [across(): lax.ppermute(value, axis, [(source, source ^ step) for source in range(co...]
    unnamed x20, local copies, waits for them, and re-layouts: 0.73 us -> 0.04 us
  transfers between devices with their start and end apart: 14 -> 13, of which waited for: 8 -> 7; matrix products, arithmetic and copies ran while one was open for 0% -> 0% of each run, Pallas kernels for 13% -> 12%
where the time goes in v5:
time: 42.9 us; the launch traced here: 42.8 us
  waiting for transfers between devices  17.6 us (41%)
  starting transfers between devices  16.7 us (39%)
  Pallas kernels  7.32 us (17%)
  local copies, waits for them, and re-layouts  0.9 us (2%)
    ppermute x11, waiting for transfers between devices, across(): lax.ppermute(value, axis, [(source, source ^ step) for source in range(co...  12.5 us
    ppermute x11, starting transfers between devices, across(): lax.ppermute(value, axis, [(source, source ^ step) for source in range(co...  12.4 us
    pallas_call x11, Pallas kernels, call(): pl.pallas_call(kernel, out_shape=[jax.ShapeDtypeStruct(shape, dtype) for...  7.32 us
    ppermute x2, waiting for transfers between devices, two_ways(): return lax.ppermute(value, ('ctx', 'tp'), pairs)  5.03 us
    ppermute x2, starting transfers between devices, two_ways(): return lax.ppermute(value, ('ctx', 'tp'), pairs)  4.3 us
  transfers between devices with their start and end apart: 13, of which 7 were waited for; matrix products, arithmetic and copies ran while one was open for 0% of the time, Pallas kernels for 12%

profile of v5, /device:TPU:0, one launch (start us, length us, event | category | flops | bytes accessed | tf_op | source)
XLA Modules:
  0.0 42.8 jit_solution(1263017877456102243)
XLA Ops:
  0.0 1.1 %pack.1.after = bf16[256,640]{1,0:T(8,128)(2,1)S(1)} custom-call(bf16[512,1024]{1,0:T(8,128)(2,1)} %w_up.3, bf16[512,512]{1,0:T(8,128)(2,1)} %w_query.3, bf16[512,512]{1,0:T(8,128)(2,1)} %w_key.3, bf16[512,512]{1,0:T(8,128)(2,1)} %w_value.3), custom_call_target="tpu_custom_call" | custom-call | bytes 1048576 | tf_op jit(solution)/shard_map/pack/pallas_call | solution.py:255
  1.1 3.0 %collective-permute-start.5 = (bf16[256,640]{1,0:T(8,128)(2,1)S(1)}, bf16[256,640]{1,0:T(8,128)(2,1)S(1)}, u32[]{:S(2)}, u32[]{:S(2)}) collective-permute-start(bf16[256,640]{1,0:T(8,128)(2,1)S(1)} %pack.1.after), channel_id=1, source_target_pairs={{0,2},{2,0},{1,3},{3,1},{4,6},{6,4},{5,7},{7,5},{8,10},{10,8},{9,1... | collective-permute-start | bytes 983048 | tf_op jit(solution)/shard_map/ppermute | solution.py:31
  4.3 0.6 %normalise.1 = (bf16[136,1024]{1,0:T(8,128)(2,1)S(1)}, bf16[16,512]{1,0:T(8,128)(2,1)S(1)}) custom-call(s32[1,4]{1,0:T(1,128)S(1)} %bitcast.3, bf16[128,1024]{1,0:T(8,128)(2,1)S(1)} %reshape.9.tokens, f32[1,1024]{1,0:T(1,128)S(1)} %bitcast.2), custom_call_target="tpu_custom_call" | custom-call | bytes 1048576 | tf_op jit(solution)/shard_map/normalise/pallas_call | solution.py:255
  4.9 1.6 %collective-permute-start.1 = (bf16[136,1024]{1,0:T(8,128)(2,1)S(1)}, bf16[136,1024]{1,0:T(8,128)(2,1)S(1)}, u32[]{:S(2)}, u32[]{:S(2)}) collective-permute-start(bf16[136,1024]{1,0:T(8,128)(2,1)S(1)} %get-tuple-element.22.full.refs_0_), channel_id=1, source_target_pairs={{0,4},{1,9},{4,0},{5,13},{8,12},{9,1},{12,8},{13,5},{2,6},{3,11},{... | collective-permute-start | bytes 835592 | tf_op jit(solution)/shard_map/ppermute | solution.py:40
  6.6 0.6 %collective-permute-start = (bf16[528,512]{1,0:T(8,128)(2,1)S(1)}, bf16[528,512]{1,0:T(8,128)(2,1)S(1)}, u32[]{:S(2)}, u32[]{:S(2)}) collective-permute-start(bf16[528,512]{1,0:T(8,128)(2,1)S(1)} %pad_maximum_fusion), channel_id=1, source_target_pairs={{0,2},{2,0},{1,3},{3,1},{4,6},{6,4},{5,7},{7,5},{8,10},{10,8},{9,1... | collective-permute-start | bytes 1622024 | tf_op jit(solution)/shard_map/ppermute | solution.py:31
  7.2 5.5 %collective-permute-done.5.refs_6_ = bf16[256,640]{1,0:T(8,128)(2,1)S(1)} collective-permute-done((bf16[256,640]{1,0:T(8,128)(2,1)S(1)}, bf16[256,640]{1,0:T(8,128)(2,1)S(1)}, u32[]{:S(2)}, u32[]{:S(2)}) %collective-permute-start.5) | collective-permute-done | bytes 327712 | tf_op jit(solution)/shard_map/ppermute | solution.py:31
  12.7 2.1 %collective-permute-start.6 = (bf16[256,640]{1,0:T(8,128)(2,1)S(1)}, bf16[256,640]{1,0:T(8,128)(2,1)S(1)}, u32[]{:S(2)}, u32[]{:S(2)}) collective-permute-start(bf16[256,640]{1,0:T(8,128)(2,1)S(1)} %collective-permute-done.5.refs_6_), channel_id=1, source_target_pairs={{0,16},{16,0},{1,17},{17,1},{2,18},{18,2},{3,19},{19,3},{4,20},{20... | collective-permute-start | bytes 983048 | tf_op jit(solution)/shard_map/ppermute | solution.py:31
  14.8 2.7 %collective-permute-start.3 = (bf16[72,1024]{1,0:T(8,128)(2,1)S(1)}, bf16[72,1024]{1,0:T(8,128)(2,1)S(1)}, u32[]{:S(2)}, u32[]{:S(2)}) collective-permute-start(bf16[72,1024]{1,0:T(8,128)(2,1)S(1)} %split.1), channel_id=1, source_target_pairs={{0,8},{1,5},{4,12},{5,1},{8,0},{9,13},{12,4},{13,9},{2,10},{3,7},{... | collective-permute-start | bytes 442376 | tf_op jit(solution)/shard_map/ppermute | solution.py:40
  17.5 5.0 %collective-permute-done.3.refs_3_ = bf16[72,1024]{1,0:T(8,128)(2,1)S(1)} collective-permute-done((bf16[72,1024]{1,0:T(8,128)(2,1)S(1)}, bf16[72,1024]{1,0:T(8,128)(2,1)S(1)}, u32[]{:S(2)}, u32[]{:S(2)}) %collective-permute-start.3) | collective-permute-done | bytes 147488 | tf_op jit(solution)/shard_map/ppermute | solution.py:40
  22.7 1.1 %collective-permute-done.4.refs_4_ = bf16[72,1024]{1,0:T(8,128)(2,1)S(1)} collective-permute-done((bf16[72,1024]{1,0:T(8,128)(2,1)S(1)}, bf16[72,1024]{1,0:T(8,128)(2,1)S(1)}, u32[]{:S(2)}, u32[]{:S(2)}) %collective-permute-start.4) | collective-permute-done | bytes 147488 | tf_op jit(solution)/shard_map/ppermute | solution.py:31
  23.9 1.1 %project.1 = (bf16[128,256]{1,0:T(8,128)(2,1)S(1)}, bf16[128,256]{1,0:T(8,128)(2,1)S(1)}, bf16[128,256]{1,0:T(8,128)(2,1)S(1)}, bf16[128,256]{1,0:T(8,128)(2,1)S...) custom-call(bf16[136,1024]{1,0:T(8,128)(2,1)S(1)} %get-tuple-element, ...), custom_call_target="tpu_custom_call" | custom-call | flops 671088640 | bytes 4194304 | tf_op jit(solution)/shard_map/project/pallas_call | solution.py:255
  25.0 0.2 collective-permute-start.7
  25.2 1.8 %collective-permute-start.8 = (bf16[512,512]{1,0:T(8,128)(2,1)S(1)}, bf16[512,512]{1,0:T(8,128)(2,1)S(1)}, u32[]{:S(2)}, u32[]{:S(2)}) collective-permute-start(bf16[512,512]{1,0:T(8,128)(2,1)S(1)} %copy-done.5), channel_id=1, source_target_pairs={{0,2},{2,0},{1,3},{3,1},{4,6},{6,4},{5,7},{7,5},{8,10},{10,8},{9,1... | collective-permute-start | bytes 1572872 | tf_op jit(solution)/shard_map/ppermute | solution.py:31
  27.0 0.8 %attend.7 = bf16[128,384]{1,0:T(8,128)(2,1)S(1)} custom-call(bf16[128,256]{1,0:T(8,128)(2,1)S(1)} %get-tuple-element.34.activated, bf16[512,128]{1,0:T(8,128)(2,1)S(1)} %get-tuple-element.25.queries, bf16[512,128]{1,0:T(8,128)(2,1)S(1)} %get-tuple-element.29.keys, bf16[128,512]{1,0:T(8,128)(2,1)S(1)} %get-tuple-element.30.values, ...), custom_call_target="tpu_custom_call" | custom-call | flops 33554432 | bytes 1048576 | tf_op jit(solution)/shard_map/attend/pallas_call | solution.py:255
  27.8 3.6 %collective-permute-start.11 = (bf16[128,384]{1,0:T(8,128)(2,1)S(1)}, bf16[128,384]{1,0:T(8,128)(2,1)S(1)}, u32[]{:S(2)}, u32[]{:S(2)}) collective-permute-start(bf16[128,384]{1,0:T(8,128)(2,1)S(1)} %attend.7), channel_id=1, source_target_pairs={{0,12},{4,8},{8,4},{12,0},{1,13},{5,9},{9,5},{13,1},{2,14},{6,10},... | collective-permute-start | bytes 294920 | tf_op jit(solution)/shard_map/ppermute | solution.py:31
  31.4 0.8 %attend.6 = bf16[128,384]{1,0:T(8,128)(2,1)S(1)} custom-call(bf16[128,256]{1,0:T(8,128)(2,1)S(1)} %get-tuple-element.33.activated, bf16[512,128]{1,0:T(8,128)(2,1)S(1)} %get-tuple-element.25.queries, bf16[512,128]{1,0:T(8,128)(2,1)S(1)} %get-tuple-element.29.keys, bf16[128,512]{1,0:T(8,128)(2,1)S(1)} %get-tuple-element.30.values, ...), custom_call_target="tpu_custom_call" | custom-call | flops 33554432 | bytes 1048576 | tf_op jit(solution)/shard_map/attend/pallas_call | solution.py:255
  32.2 0.8 %attend.5 = bf16[128,384]{1,0:T(8,128)(2,1)S(1)} custom-call(bf16[128,256]{1,0:T(8,128)(2,1)S(1)} %get-tuple-element.32.activated, bf16[512,128]{1,0:T(8,128)(2,1)S(1)} %get-tuple-element.25.queries, bf16[512,128]{1,0:T(8,128)(2,1)S(1)} %get-tuple-element.29.keys, bf16[128,512]{1,0:T(8,128)(2,1)S(1)} %get-tuple-element.30.values, ...), custom_call_target="tpu_custom_call" | custom-call | flops 33554432 | bytes 1048576 | tf_op jit(solution)/shard_map/attend/pallas_call | solution.py:255
  33.0 1.0 %collective-permute-start.9 = (bf16[128,384]{1,0:T(8,128)(2,1)S(1)}, bf16[128,384]{1,0:T(8,128)(2,1)S(1)}, u32[]{:S(2)}, u32[]{:S(2)}) collective-permute-start(bf16[128,384]{1,0:T(8,128)(2,1)S(1)} %attend.5), channel_id=1, source_target_pairs={{0,4},{4,0},{8,12},{12,8},{1,5},{5,1},{9,13},{13,9},{2,6},{6,2},{1... | collective-permute-start | bytes 294920 | tf_op jit(solution)/shard_map/ppermute | solution.py:31
  34.0 0.3 convolve.1.refs_2_
  34.2 0.8 %attend.4.refs_6_ = bf16[128,384]{1,0:T(8,128)(2,1)S(1)} custom-call(bf16[128,256]{1,0:T(8,128)(2,1)S(1)} %get-tuple-element.28.activated, bf16[512,128]{1,0:T(8,128)(2,1)S(1)} %get-tuple-element.25.queries, bf16[512,128]{1,0:T(8,128)(2,1)S(1)} %get-tuple-element.29.keys, bf16[128,512]{1,0:T(8,128)(2,1)S(1)} %get-tuple-element.30.values, ...), custom_call_target="tpu_custom_call" | custom-call | flops 33554432 | bytes 1048576 | tf_op jit(solution)/shard_map/attend/pallas_call | solution.py:255
  35.0 4.1 %collective-permute-done.8.refs_5_ = bf16[512,512]{1,0:T(8,128)(2,1)S(1)} collective-permute-done((bf16[512,512]{1,0:T(8,128)(2,1)S(1)}, bf16[512,512]{1,0:T(8,128)(2,1)S(1)}, u32[]{:S(2)}, u32[]{:S(2)}) %collective-permute-start.8) | collective-permute-done | bytes 524320 | tf_op jit(solution)/shard_map/ppermute | solution.py:31
  39.6 1.0 %join.1 = (f32[128,512]{1,0:T(8,128)S(1)}, bf16[128,512]{1,0:T(8,128)(2,1)S(1)}) custom-call(bf16[1024,512]{1,0:T(8,128)(2,1)S(1)} %copy-done.1, bf16[512,512]{1,0:T(8,128)(2,1)S(1)} %copy-done.5, f32[128,512]{1,0:T(8,128)S(1)} %convolve.1.refs_2_, bf16[528,512]{1,0:T(8,128)(2,1)S(1)} %collective-permute-done.received.refs_3_, ...), custom_call_target="tpu_custom_call" | custom-call | flops 402653184 | bytes 4194304 | tf_op jit(solution)/shard_map/join/pallas_call | solution.py:255
  40.7 1.3 %collective-permute-done.12 = bf16[128,512]{1,0:T(8,128)(2,1)S(1)} collective-permute-done((bf16[128,512]{1,0:T(8,128)(2,1)S(1)}, bf16[128,512]{1,0:T(8,128)(2,1)S(1)}, u32[]{:S(2)}, u32[]{:S(2)}) %collective-permute-start.12) | collective-permute-done | bytes 131104 | tf_op jit(solution)/shard_map/ppermute | solution.py:31
  42.1 0.7 %reshape.11 = bf16[64,2,512]{2,1,0:T(2,128)(2,1)} reshape(bf16[128,512]{1,0:T(8,128)(2,1)S(1)} %add_convert_fusion) | data formatting | bytes 262144 | tf_op jit(solution)/shard_map/reshape | solution.py:385
  (38 shorter events, 1.1 us)
Async XLA Ops:
  0.0 4.2 %copy-start.9 = (bf16[64,2,1024]{2,1,0:T(2,128)(2,1)S(1)}, bf16[64,2,1024]{2,1,0:T(2,128)(2,1)}, u32[]{:S(2)}) copy-start(bf16[64,2,1024]{2,1,0:T(2,128)(2,1)} %param.10) | copy-start | bytes 786436
  0.0 4.3 %copy-start.8 = (s32[1,1,4]{2,1,0:T(1,128)S(1)}, s32[1,1,4]{2,1,0:T(1,128)}, u32[]{:S(2)}) copy-start(s32[1,1,4]{2,1,0:T(1,128)} %param.12) | copy-start | bytes 52
  0.0 4.3 %copy-start.7 = (f32[1024]{0:T(1024)S(1)}, f32[1024]{0:T(1024)}, u32[]{:S(2)}) copy-start(f32[1024]{0:T(1024)} %param.11) | copy-start | bytes 12292
  0.0 6.5 %copy-start.1 = (bf16[1024,512]{1,0:T(8,128)(2,1)S(1)}, bf16[1024,512]{1,0:T(8,128)(2,1)}, u32[]{:S(2)}) copy-start(bf16[1024,512]{1,0:T(8,128)(2,1)} %refs_0_.1) | copy-start | bytes 3145732
  1.1 11.6 %collective-permute-start.5 = (bf16[256,640]{1,0:T(8,128)(2,1)S(1)}, bf16[256,640]{1,0:T(8,128)(2,1)S(1)}, u32[]{:S(2)}, u32[]{:S(2)}) collective-permute-start(bf16[256,640]{1,0:T(8,128)(2,1)S(1)} %pack.1.after), channel_id=1, source_target_pairs={{0,2},{2,0},{1,3},{3,1},{4,6},{6,4},{5,7},{7,5},{8,10},{10,8},{9,1... | collective-permute-start | bytes 983048 | tf_op jit(solution)/shard_map/ppermute | solution.py:31
  4.3 18.2 %copy-start.4 = (bf16[512,512]{1,0:T(8,128)(2,1)S(1)}, bf16[512,512]{1,0:T(8,128)(2,1)}, u32[]{:S(2)}) copy-start(bf16[512,512]{1,0:T(8,128)(2,1)} %w_value.3) | copy-start | bytes 1572868
  4.9 9.9 %collective-permute-start.1 = (bf16[136,1024]{1,0:T(8,128)(2,1)S(1)}, bf16[136,1024]{1,0:T(8,128)(2,1)S(1)}, u32[]{:S(2)}, u32[]{:S(2)}) collective-permute-start(bf16[136,1024]{1,0:T(8,128)(2,1)S(1)} %get-tuple-element.22.full.refs_0_), channel_id=1, source_target_pairs={{0,4},{1,9},{4,0},{5,13},{8,12},{9,1},{12,8},{13,5},{2,6},{3,11},{... | collective-permute-start | bytes 835592 | tf_op jit(solution)/shard_map/ppermute | solution.py:40
  6.5 16.0 %copy-start = (bf16[512,1024]{1,0:T(8,128)(2,1)S(1)}, bf16[512,1024]{1,0:T(8,128)(2,1)}, u32[]{:S(2)}) copy-start(bf16[512,1024]{1,0:T(8,128)(2,1)} %w_up.3) | copy-start | bytes 3145732
  6.5 16.0 %copy-start.2 = (bf16[512,512]{1,0:T(8,128)(2,1)S(1)}, bf16[512,512]{1,0:T(8,128)(2,1)}, u32[]{:S(2)}) copy-start(bf16[512,512]{1,0:T(8,128)(2,1)} %w_query.3) | copy-start | bytes 1572868
  6.5 16.0 %copy-start.3 = (bf16[512,512]{1,0:T(8,128)(2,1)S(1)}, bf16[512,512]{1,0:T(8,128)(2,1)}, u32[]{:S(2)}) copy-start(bf16[512,512]{1,0:T(8,128)(2,1)} %w_key.3) | copy-start | bytes 1572868
  6.6 18.4 %collective-permute-start = (bf16[528,512]{1,0:T(8,128)(2,1)S(1)}, bf16[528,512]{1,0:T(8,128)(2,1)S(1)}, u32[]{:S(2)}, u32[]{:S(2)}) collective-permute-start(bf16[528,512]{1,0:T(8,128)(2,1)S(1)} %pad_maximum_fusion), channel_id=1, source_target_pairs={{0,2},{2,0},{1,3},{3,1},{4,6},{6,4},{5,7},{7,5},{8,10},{10,8},{9,1... | collective-permute-start | bytes 1622024 | tf_op jit(solution)/shard_map/ppermute | solution.py:31
  12.7 11.2 %collective-permute-start.6 = (bf16[256,640]{1,0:T(8,128)(2,1)S(1)}, bf16[256,640]{1,0:T(8,128)(2,1)S(1)}, u32[]{:S(2)}, u32[]{:S(2)}) collective-permute-start(bf16[256,640]{1,0:T(8,128)(2,1)S(1)} %collective-permute-done.5.refs_6_), channel_id=1, source_target_pairs={{0,16},{16,0},{1,17},{17,1},{2,18},{18,2},{3,19},{19,3},{4,20},{20... | collective-permute-start | bytes 983048 | tf_op jit(solution)/shard_map/ppermute | solution.py:31
  14.8 7.7 %collective-permute-start.3 = (bf16[72,1024]{1,0:T(8,128)(2,1)S(1)}, bf16[72,1024]{1,0:T(8,128)(2,1)S(1)}, u32[]{:S(2)}, u32[]{:S(2)}) collective-permute-start(bf16[72,1024]{1,0:T(8,128)(2,1)S(1)} %split.1), channel_id=1, source_target_pairs={{0,8},{1,5},{4,12},{5,1},{8,0},{9,13},{12,4},{13,9},{2,10},{3,7},{... | collective-permute-start | bytes 442376 | tf_op jit(solution)/shard_map/ppermute | solution.py:40
  17.5 5.2 %collective-permute-start.2 = (bf16[136,1024]{1,0:T(8,128)(2,1)S(1)}, bf16[136,1024]{1,0:T(8,128)(2,1)S(1)}, u32[]{:S(2)}, u32[]{:S(2)}) collective-permute-start(bf16[136,1024]{1,0:T(8,128)(2,1)S(1)} %collective-permute-done.1.block.refs_1_), channel_id=1, source_target_pairs={{0,1},{1,0},{2,3},{3,2},{4,5},{5,4},{6,7},{7,6},{8,9},{9,8},{10,11... | collective-permute-start | bytes 835592 | tf_op jit(solution)/shard_map/ppermute | solution.py:31
  22.5 1.4 %collective-permute-start.4 = (bf16[72,1024]{1,0:T(8,128)(2,1)S(1)}, bf16[72,1024]{1,0:T(8,128)(2,1)S(1)}, u32[]{:S(2)}, u32[]{:S(2)}) collective-permute-start(bf16[72,1024]{1,0:T(8,128)(2,1)S(1)} %collective-permute-done.3.refs_3_), channel_id=1, source_target_pairs={{0,1},{1,0},{2,3},{3,2},{4,5},{5,4},{6,7},{7,6},{8,9},{9,8},{10,11... | collective-permute-start | bytes 442376 | tf_op jit(solution)/shard_map/ppermute | solution.py:31
  22.7 2.5 %copy-start.5 = (bf16[512,512]{1,0:T(8,128)(2,1)S(1)}, bf16[512,512]{1,0:T(8,128)(2,1)}, u32[]{:S(2)}) copy-start(bf16[512,512]{1,0:T(8,128)(2,1)} %refs_1_.1) | copy-start | bytes 1572868
  25.0 9.0 %copy-start.6 = (f32[5,512]{1,0:T(8,128)S(1)}, f32[5,512]{1,0:T(8,128)}, u32[]{:S(2)}) copy-start(f32[5,512]{1,0:T(8,128)} %taps.1) | copy-start | bytes 30724
  25.0 14.6 %collective-permute-start.7 = (bf16[528,512]{1,0:T(8,128)(2,1)S(1)}, bf16[528,512]{1,0:T(8,128)(2,1)S(1)}, u32[]{:S(2)}, u32[]{:S(2)}) collective-permute-start(bf16[528,512]{1,0:T(8,128)(2,1)S(1)} %collective-permute-done.received.refs_3_), channel_id=1, source_target_pairs={{0,16},{16,0},{1,17},{17,1},{2,18},{18,2},{3,19},{19,3},{4,20},{20... | collective-permute-start | bytes 1622024 | tf_op jit(solution)/shard_map/ppermute | solution.py:31
  25.2 13.9 %collective-permute-start.8 = (bf16[512,512]{1,0:T(8,128)(2,1)S(1)}, bf16[512,512]{1,0:T(8,128)(2,1)S(1)}, u32[]{:S(2)}, u32[]{:S(2)}) collective-permute-start(bf16[512,512]{1,0:T(8,128)(2,1)S(1)} %copy-done.5), channel_id=1, source_target_pairs={{0,2},{2,0},{1,3},{3,1},{4,6},{6,4},{5,7},{7,5},{8,10},{10,8},{9,1... | collective-permute-start | bytes 1572872 | tf_op jit(solution)/shard_map/ppermute | solution.py:31
  27.8 11.3 %collective-permute-start.11 = (bf16[128,384]{1,0:T(8,128)(2,1)S(1)}, bf16[128,384]{1,0:T(8,128)(2,1)S(1)}, u32[]{:S(2)}, u32[]{:S(2)}) collective-permute-start(bf16[128,384]{1,0:T(8,128)(2,1)S(1)} %attend.7), channel_id=1, source_target_pairs={{0,12},{4,8},{8,4},{12,0},{1,13},{5,9},{9,5},{13,1},{2,14},{6,10},... | collective-permute-start | bytes 294920 | tf_op jit(solution)/shard_map/ppermute | solution.py:31
  32.1 7.2 %collective-permute-start.10 = (bf16[128,384]{1,0:T(8,128)(2,1)S(1)}, bf16[128,384]{1,0:T(8,128)(2,1)S(1)}, u32[]{:S(2)}, u32[]{:S(2)}) collective-permute-start(bf16[128,384]{1,0:T(8,128)(2,1)S(1)} %attend.6), channel_id=1, source_target_pairs={{0,8},{4,12},{8,0},{12,4},{1,9},{5,13},{9,1},{13,5},{2,10},{6,14},... | collective-permute-start | bytes 294920 | tf_op jit(solution)/shard_map/ppermute | solution.py:31
  33.0 6.6 %collective-permute-start.9 = (bf16[128,384]{1,0:T(8,128)(2,1)S(1)}, bf16[128,384]{1,0:T(8,128)(2,1)S(1)}, u32[]{:S(2)}, u32[]{:S(2)}) collective-permute-start(bf16[128,384]{1,0:T(8,128)(2,1)S(1)} %attend.5), channel_id=1, source_target_pairs={{0,4},{4,0},{8,12},{12,8},{1,5},{5,1},{9,13},{13,9},{2,6},{6,2},{1... | collective-permute-start | bytes 294920 | tf_op jit(solution)/shard_map/ppermute | solution.py:31
  40.6 1.4 %collective-permute-start.12 = (bf16[128,512]{1,0:T(8,128)(2,1)S(1)}, bf16[128,512]{1,0:T(8,128)(2,1)S(1)}, u32[]{:S(2)}, u32[]{:S(2)}) collective-permute-start(bf16[128,512]{1,0:T(8,128)(2,1)S(1)} %get-tuple-element.36), channel_id=1, source_target_pairs={{0,1},{1,0},{2,3},{3,2},{4,5},{5,4},{6,7},{7,6},{8,9},{9,8},{10,11... | collective-permute-start | bytes 393224 | tf_op jit(solution)/shard_map/ppermute | solution.py:31

commit v6 on v5

--- a/solution.py
+++ b/solution.py
@@ -74,7 +74,7 @@
     return jnp.dot(left, right, preferred_element_type=jnp.float32)
 
 
-def normalise_kernel(n_ctx, mask_in, tokens, gain, full, edge, mask, sems):
+def normalise_kernel(n_ctx, mask_in, tokens, gain, full, own, mine, edge, mask, sems):
     rows, width = tokens.shape
     copies = begin(sems, [(mask_in, mask)])
     values = tokens[...].astype(jnp.float32)
@@ -88,9 +88,10 @@
     entries = jnp.concatenate(entries, axis=1).astype(jnp.bfloat16)
     full[rows:, :] = entries
     tm, tp = lax.axis_index("tm"), lax.axis_index("tp")
+    own[...] = full[...]
     size, columns = edge.shape
-    last = full[rows - size : rows, slot(tp, columns)]
-    edge[...] = jnp.where(tm == 0, last, full[0:size, slot(tp, columns)])
+    mine[...] = full[0:rows, slot(tp, columns)]
+    edge[...] = jnp.where(tm == 0, mine[rows - size :, :], mine[0:size, :])
 
 
 def pack_kernel(n_ctx, w_up, w_query, w_key, w_value, packed, sems):
@@ -121,7 +122,7 @@
     end(begin(sems, pairs))
 
 
-def convolve_kernel(per_frame, tokens, full, received, taps, base, held):
+def convolve_kernel(per_frame, tokens, mine, received, taps, last0, last1, base, held):
     tm, tp = lax.axis_index("tm"), lax.axis_index("tp")
     rows, columns = base.shape
     edge = 16
@@ -129,7 +130,7 @@
     near = received[received.shape[0] - edge :, :].astype(jnp.float32)
     zeros = jnp.zeros((edge, columns), jnp.float32)
     held[0:edge, :] = jnp.where(tm == 1, near, zeros)
-    held[edge : edge + rows, :] = full[0:rows, slot(tp, columns)].astype(jnp.float32)
+    held[edge : edge + rows, :] = mine[...].astype(jnp.float32)
     held[edge + rows :, :] = jnp.where(tm == 0, near, zeros)
     total = tokens[:, slot(tp, columns)].astype(jnp.float32)
     for offset in range(KERNEL):
@@ -185,36 +186,40 @@
             bias[8 * i : 8 * (i + 1), target] = jnp.where(flag > 0, 0.0, MASKED)
 
 
-def attend_kernel(n_ctx, i, activated, queries, keys, values, bias, out):
-    rows, hidden = activated.shape
-    wide = out.shape[1] - hidden
-    block = queries[i * rows : (i + 1) * rows, :]
+def attend_kernel(n_ctx, blocks, *refs):
+    count = len(blocks)
+    acts, (queries, keys, values, bias) = refs[:count], refs[count : count + 4]
+    outs = refs[count + 4 :]
+    rows, hidden = acts[0].shape
+    wide = outs[0].shape[1] - hidden
     lane_head = lax.broadcasted_iota(jnp.int32, (1, wide), 1) // HEAD_DIM
-    allowed = jnp.concatenate(
-        [
-            jnp.broadcast_to(bias[8 * i : 8 * i + 1, j * LANES : (j + 1) * LANES], (rows, rows))
-            for j in range(n_ctx)
-        ],
-        axis=0,
-    )
-    results = []
-    for head in range(wide // HEAD_DIM):
-        one = jnp.where(lane_head == head, block, jnp.zeros_like(block))
-        scores = lax.dot_general(
-            keys[...], one, (((1,), (1,)), ((), ())), preferred_element_type=jnp.float32
+    for n, i in enumerate(blocks):
+        block = queries[i * rows : (i + 1) * rows, :]
+        allowed = jnp.concatenate(
+            [
+                jnp.broadcast_to(
+                    bias[8 * i : 8 * i + 1, j * LANES : (j + 1) * LANES], (rows, rows)
+                )
+                for j in range(n_ctx)
+            ],
+            axis=0,
         )
-        scores = scores * 0.125 + allowed
-        peak = jnp.max(scores, axis=0, keepdims=True)
-        expo = jnp.exp(scores - peak)
-        total = jnp.sum(expo, axis=0, keepdims=True)
-        mixed = jnp.dot(
-            values[head * HEAD_DIM : (head + 1) * HEAD_DIM, :],
-            expo.astype(jnp.bfloat16),
-            preferred_element_type=jnp.float32,
-        )
-        results.append(mixed / total)
-    out[:, 0:hidden] = activated[...]
-    out[:, hidden:] = jnp.concatenate(results, axis=0).T.astype(jnp.bfloat16)
+        results = []
+        for head in range(wide // HEAD_DIM):
+            one = jnp.where(lane_head == head, block, jnp.zeros_like(block))
+            scores = lax.dot_general(
+                keys[...], one, (((1,), (1,)), ((), ())), preferred_element_type=jnp.float32
+            )
+            scores = scores * 0.125 + allowed
+            peak = jnp.max(scores, axis=0, keepdims=True)
+            expo = jnp.exp(scores - peak)
+            total = jnp.sum(expo, axis=0, keepdims=True)
+            mixed = dot(
+                values[head * HEAD_DIM : (head + 1) * HEAD_DIM, :], expo.astype(jnp.bfloat16)
+            )
+            results.append(mixed / total)
+        outs[n][:, 0:hidden] = acts[n][...]
+        outs[n][:, hidden:] = jnp.concatenate(results, axis=0).T.astype(jnp.bfloat16)
 
 
 def join_kernel(n_ctx, *refs):
@@ -224,12 +229,13 @@
     keep, send, down, out, acts, atts, sems = refs[6 + n_ctx :]
     ctx, tm, groups, tp = (lax.axis_index(name) for name in AXES)
     hidden, wide = acts.shape[1] // n_ctx, atts.shape[1] // n_ctx
-    count = near_down.shape[0] // 2
+    count = farther_down.shape[0] - 16
     pairs = []
     for d in range(n_ctx):
         pairs.append((parts[d].at[:, 0:hidden], acts.at[:, slot(ctx ^ d, hidden)]))
         pairs.append((parts[d].at[:, hidden:], atts.at[:, slot(ctx ^ d, wide)]))
-    pairs.append((far_out, out))
+    pairs.append((far_out.at[0 : out.shape[0]], out))
+    pairs.append((far_out.at[out.shape[0] :], down.at[2 * count :]))
     pairs.append((far_down.at[0:count], down.at[slot(groups, count)]))
     pairs.append((farther_down.at[0:count], down.at[slot(1 - groups, count)]))
     copies = begin(sems, pairs)
@@ -293,10 +299,10 @@
         limit=(54 << 20) - (700 << 10),
     )
     token_rows = after(tokens, packed_a).reshape(rows, width)
-    full, edge = call(
+    full, own, mine, edge = call(
         functools.partial(normalise_kernel, n_ctx),
         "normalise",
-        [((rows + 8, width), bf16), ((16, columns), bf16)],
+        [((rows + 8, width), bf16)] * 2 + [((rows, columns), bf16), ((16, columns), bf16)],
         [
             (ANY, block_mask[0]),
             (VMEM, token_rows),
@@ -306,11 +312,10 @@
     )
     x_a = across(packed_a, "tm", 1)
     y_a = across(x_a, "groups", 1)
-    half_down = w_down.shape[0] // 2
-    sent_down = lax.dynamic_slice_in_dim(w_down, groups * half_down, half_down, 0)
+    shared = w_down.shape[0] * 7 // 16
+    sent_down = lax.dynamic_slice_in_dim(w_down, groups * shared, shared, 0)
     sent_down = jnp.concatenate([sent_down, edge], axis=0)
     x_down = across(after(sent_down, packed_a), "tm", 1)
-    x_out = across(after(w_out, packed_a), "tm", 1)
 
     (near,) = call(
         functools.partial(pack_near_kernel, n_ctx),
@@ -324,13 +329,15 @@
     (piece,) = call(split_kernel, "split", [((rows // 2 + 8, width), bf16)], [(VMEM, block)])
     piece = two_ways(piece, (2, 1))
     other_piece = across(piece, "tp", 1)
+    sent_out = jnp.concatenate([w_out, w_down[2 * shared :]], axis=0)
+    x_out = across(after(sent_out, block), "tm", 1)
     *acts, queries, keys, values, bias = call(
         functools.partial(project_kernel, n_ctx),
         "project",
         [((rows, hidden), bf16)] * n_ctx
         + [((n_ctx * rows, wide), bf16)] * 2
         + [((wide, n_ctx * rows), bf16), ((8 * n_ctx, n_ctx * LANES), f32)],
-        [(VMEM, value) for value in (full, block, other_block, piece, other_piece)]
+        [(VMEM, value) for value in (own, block, other_block, piece, other_piece)]
         + [(VMEM, value) for value in (near, x_a, y_a)],
         [
             pltpu.VMEM((n_ctx * rows, width), bf16),
@@ -340,17 +347,19 @@
         transcendentals=n_ctx * rows * hidden,
     )
     parts = [None] * n_ctx
-    for i in (2, 3, 1, 0):
-        (part,) = call(
-            functools.partial(attend_kernel, n_ctx, i),
+    for blocks in ((2, 3), (1,), (0,)):
+        done = call(
+            functools.partial(attend_kernel, n_ctx, blocks),
             "attend",
-            [((rows, hidden + wide), bf16)],
-            [(VMEM, value) for value in (acts[i], queries, keys, values, bias)],
-            flops=4 * wide * n_ctx * rows * rows,
-            transcendentals=(wide // HEAD_DIM) * n_ctx * rows * rows,
+            [((rows, hidden + wide), bf16)] * len(blocks),
+            [(VMEM, acts[i]) for i in blocks]
+            + [(VMEM, value) for value in (queries, keys, values, bias)],
+            flops=4 * len(blocks) * wide * n_ctx * rows * rows,
+            transcendentals=len(blocks) * (wide // HEAD_DIM) * n_ctx * rows * rows,
         )
-        parts[i] = part
-    y_down = across(after(x_down, queries), "groups", 1)
+        for i, part in zip(blocks, done):
+            parts[i] = part
+    y_down = across(after(x_down, near), "groups", 1)
     parts = parts[:1] + [across(parts[i], "ctx", i) for i in range(1, n_ctx)]
     (base,) = call(
         functools.partial(convolve_kernel, dancers_here),
@@ -358,11 +367,14 @@
         [((rows, columns), f32)],
         [
             (VMEM, token_rows),
-            (VMEM, full),
+            (VMEM, mine),
             (VMEM, x_down),
             (VMEM, conv_weight),
+            (ANY, x_out),
+            (ANY, parts[0]),
         ],
         [pltpu.VMEM((rows + 32, columns), f32)],
+        flops=3000000000,
     )
     keep, send = call(
         functools.partial(join_kernel, n_ctx),
@@ -376,7 +388,7 @@
             pltpu.VMEM(w_out.shape, bf16),
             pltpu.VMEM((rows, w_down.shape[0]), bf16),
             pltpu.VMEM((rows, w_out.shape[0]), bf16),
-            pltpu.SemaphoreType.DMA((2 * n_ctx + 3,)),
+            pltpu.SemaphoreType.DMA((2 * n_ctx + 4,)),
         ],
         flops=4 * rows * columns * n_ctx * (hidden + wide),
         moved=4 << 20,

time: 42.9 us -> 42.1 us (0.981)
  waiting for transfers between devices: 17.6 us -> 16.4 us
    ppermute x11, waiting for transfers between devices: 12.5 us -> 7.16 us  [across(): lax.ppermute(value, axis, [(source, source ^ step) for source in range(co...]
    ppermute x2, waiting for transfers between devices: 5.03 us -> 9.25 us  [two_ways(): return lax.ppermute(value, ('ctx', 'tp'), pairs)]
    pallas_call x11 -> x10, Pallas kernels: 7.32 us -> 7.61 us  [call(): pl.pallas_call(kernel, out_shape=[jax.ShapeDtypeStruct(shape, dtype) for...]
  transfers between devices with their start and end apart: 13 -> 13, of which waited for: 7 -> 7; matrix products, arithmetic and copies ran while one was open for 0% -> 0% of each run, Pallas kernels for 12% -> 11%
where the time goes in v6:
time: 42.1 us; the launch traced here: 42 us
  starting transfers between devices  16.4 us (39%)
  waiting for transfers between devices  16.4 us (39%)
  Pallas kernels  7.61 us (18%)
  local copies, waits for them, and re-layouts  1.28 us (3%)
    ppermute x11, starting transfers between devices, across(): lax.ppermute(value, axis, [(source, source ^ step) for source in range(co...  12.1 us
    ppermute x2, waiting for transfers between devices, two_ways(): return lax.ppermute(value, ('ctx', 'tp'), pairs)  9.25 us
    pallas_call x10, Pallas kernels, call(): pl.pallas_call(kernel, out_shape=[jax.ShapeDtypeStruct(shape, dtype) for...  7.61 us
    ppermute x11, waiting for transfers between devices, across(): lax.ppermute(value, axis, [(source, source ^ step) for source in range(co...  7.16 us
    ppermute x2, starting transfers between devices, two_ways(): return lax.ppermute(value, ('ctx', 'tp'), pairs)  4.28 us
  transfers between devices with their start and end apart: 13, of which 7 were waited for; matrix products, arithmetic and copies ran while one was open for 0% of the time, Pallas kernels for 11%

profile of v6, /device:TPU:0, one launch (start us, length us, event | category | flops | bytes accessed | tf_op | source)
XLA Modules:
  0.0 42.0 jit_solution(702714459490412250)
XLA Ops:
  0.0 1.1 %pack.1.after = bf16[256,640]{1,0:T(8,128)(2,1)S(1)} custom-call(bf16[512,1024]{1,0:T(8,128)(2,1)} %w_up.3, bf16[512,512]{1,0:T(8,128)(2,1)} %w_query.3, bf16[512,512]{1,0:T(8,128)(2,1)} %w_key.3, bf16[512,512]{1,0:T(8,128)(2,1)} %w_value.3), custom_call_target="tpu_custom_call" | custom-call | bytes 1048576 | tf_op jit(solution)/shard_map/pack/pallas_call | solution.py:261
  1.1 3.0 %collective-permute-start.6 = (bf16[256,640]{1,0:T(8,128)(2,1)S(1)}, bf16[256,640]{1,0:T(8,128)(2,1)S(1)}, u32[]{:S(2)}, u32[]{:S(2)}) collective-permute-start(bf16[256,640]{1,0:T(8,128)(2,1)S(1)} %pack.1.after), channel_id=1, source_target_pairs={{0,2},{2,0},{1,3},{3,1},{4,6},{6,4},{5,7},{7,5},{8,10},{10,8},{9,1... | collective-permute-start | bytes 983048 | tf_op jit(solution)/shard_map/ppermute | solution.py:31
  4.3 0.6 %normalise.1 = (bf16[136,1024]{1,0:T(8,128)(2,1)S(1)}, bf16[136,1024]{1,0:T(8,128)(2,1)S(1)}, bf16[128,512]{1,0:T(8,128)(2,1)S(1)}, bf16[16,512]{1,0:T(8,128)(2,1)S(1)}) custom-call(s32[1,4]{1,0:T(1,128)S(1)} %bitcast.3, bf16[128,1024]{1,0:T(8,128)(2,1)S(1)} %reshape.9.tokens, f32[1,1024]{1,0:T(1,128)S(1)} %bitcast.2), custom_call_target="tpu_custom_call" | custom-call | bytes 1048576 | tf_op jit(solution)/shard_map/normalise/pallas_call | solution.py:261
  4.9 1.6 %collective-permute-start.1 = (bf16[136,1024]{1,0:T(8,128)(2,1)S(1)}, bf16[136,1024]{1,0:T(8,128)(2,1)S(1)}, u32[]{:S(2)}, u32[]{:S(2)}) collective-permute-start(bf16[136,1024]{1,0:T(8,128)(2,1)S(1)} %get-tuple-element.29), channel_id=1, source_target_pairs={{0,4},{1,9},{4,0},{5,13},{8,12},{9,1},{12,8},{13,5},{2,6},{3,11},{... | collective-permute-start | bytes 835592 | tf_op jit(solution)/shard_map/ppermute | solution.py:40
  6.6 0.6 %collective-permute-start = (bf16[464,512]{1,0:T(8,128)(2,1)S(1)}, bf16[464,512]{1,0:T(8,128)(2,1)S(1)}, u32[]{:S(2)}, u32[]{:S(2)}) collective-permute-start(bf16[464,512]{1,0:T(8,128)(2,1)S(1)} %pad_maximum_fusion.1), channel_id=1, source_target_pairs={{0,2},{2,0},{1,3},{3,1},{4,6},{6,4},{5,7},{7,5},{8,10},{10,8},{9,1... | collective-permute-start | bytes 1425416 | tf_op jit(solution)/shard_map/ppermute | solution.py:31
  7.7 5.8 %collective-permute-done.1.block.refs_1_ = bf16[136,1024]{1,0:T(8,128)(2,1)S(1)} collective-permute-done((bf16[136,1024]{1,0:T(8,128)(2,1)S(1)}, bf16[136,1024]{1,0:T(8,128)(2,1)S(1)}, u32[]{:S(2)}, u32[]{:S(2)}) %collective-permute-start.1) | collective-permute-done | bytes 278560 | tf_op jit(solution)/shard_map/ppermute | solution.py:40
  13.5 0.5 %collective-permute-start.2 = (bf16[640,512]{1,0:T(8,128)(2,1)S(1)}, bf16[640,512]{1,0:T(8,128)(2,1)S(1)}, u32[]{:S(2)}, u32[]{:S(2)}) collective-permute-start(bf16[640,512]{1,0:T(8,128)(2,1)S(1)} %pad_maximum_fusion), channel_id=1, source_target_pairs={{0,2},{2,0},{1,3},{3,1},{4,6},{6,4},{5,7},{7,5},{8,10},{10,8},{9,1... | collective-permute-start | bytes 1966088 | tf_op jit(solution)/shard_map/ppermute | solution.py:31
  14.0 1.5 %collective-permute-start.7 = (bf16[256,640]{1,0:T(8,128)(2,1)S(1)}, bf16[256,640]{1,0:T(8,128)(2,1)S(1)}, u32[]{:S(2)}, u32[]{:S(2)}) collective-permute-start(bf16[256,640]{1,0:T(8,128)(2,1)S(1)} %collective-permute-done.6.refs_6_), channel_id=1, source_target_pairs={{0,16},{16,0},{1,17},{17,1},{2,18},{18,2},{3,19},{19,3},{4,20},{20... | collective-permute-start | bytes 983048 | tf_op jit(solution)/shard_map/ppermute | solution.py:31
  15.5 2.6 %collective-permute-start.4 = (bf16[72,1024]{1,0:T(8,128)(2,1)S(1)}, bf16[72,1024]{1,0:T(8,128)(2,1)S(1)}, u32[]{:S(2)}, u32[]{:S(2)}) collective-permute-start(bf16[72,1024]{1,0:T(8,128)(2,1)S(1)} %split.1), channel_id=1, source_target_pairs={{0,8},{1,5},{4,12},{5,1},{8,0},{9,13},{12,4},{13,9},{2,10},{3,7},{... | collective-permute-start | bytes 442376 | tf_op jit(solution)/shard_map/ppermute | solution.py:40
  18.2 3.5 %collective-permute-done.4.refs_3_ = bf16[72,1024]{1,0:T(8,128)(2,1)S(1)} collective-permute-done((bf16[72,1024]{1,0:T(8,128)(2,1)S(1)}, bf16[72,1024]{1,0:T(8,128)(2,1)S(1)}, u32[]{:S(2)}, u32[]{:S(2)}) %collective-permute-start.4) | collective-permute-done | bytes 147488 | tf_op jit(solution)/shard_map/ppermute | solution.py:40
  21.8 1.0 %collective-permute-done.received.refs_3_ = bf16[464,512]{1,0:T(8,128)(2,1)S(1)} collective-permute-done((bf16[464,512]{1,0:T(8,128)(2,1)S(1)}, bf16[464,512]{1,0:T(8,128)(2,1)S(1)}, u32[]{:S(2)}, u32[]{:S(2)}) %collective-permute-start) | collective-permute-done | bytes 475168 | tf_op jit(solution)/shard_map/ppermute | solution.py:31
  22.9 2.1 %collective-permute-start.8 = (bf16[464,512]{1,0:T(8,128)(2,1)S(1)}, bf16[464,512]{1,0:T(8,128)(2,1)S(1)}, u32[]{:S(2)}, u32[]{:S(2)}) collective-permute-start(bf16[464,512]{1,0:T(8,128)(2,1)S(1)} %collective-permute-done.received.refs_3_), channel_id=1, source_target_pairs={{0,16},{16,0},{1,17},{17,1},{2,18},{18,2},{3,19},{19,3},{4,20},{20... | collective-permute-start | bytes 1425416 | tf_op jit(solution)/shard_map/ppermute | solution.py:31
  25.0 1.1 %project.1 = (bf16[128,256]{1,0:T(8,128)(2,1)S(1)}, bf16[128,256]{1,0:T(8,128)(2,1)S(1)}, bf16[128,256]{1,0:T(8,128)(2,1)S(1)}, bf16[128,256]{1,0:T(8,128)(2,1)S...) custom-call(bf16[136,1024]{1,0:T(8,128)(2,1)S(1)} %get-tuple-element, ...), custom_call_target="tpu_custom_call" | custom-call | flops 671088640 | bytes 4194304 | tf_op jit(solution)/shard_map/project/pallas_call | solution.py:261
  26.1 1.1 %attend.5 = (bf16[128,384]{1,0:T(8,128)(2,1)S(1)}, bf16[128,384]{1,0:T(8,128)(2,1)S(1)}) custom-call(bf16[128,256]{1,0:T(8,128)(2,1)S(1)} %get-tuple-element.39.refs_0_, bf16[128,256]{1,0:T(8,128)(2,1)S(1)} %get-tuple-element.40.refs_1_, bf16[512,128]{1,0:T(8,128)(2,1)S(1)} %get-tuple-element.33.refs_1_.refs_2_, ...), custom_call_target="tpu_custom_call" | custom-call | flops 67108864 | bytes 1048576 | tf_op jit(solution)/shard_map/attend/pallas_call | solution.py:261
  27.2 2.7 %collective-permute-start.10 = (bf16[128,384]{1,0:T(8,128)(2,1)S(1)}, bf16[128,384]{1,0:T(8,128)(2,1)S(1)}, u32[]{:S(2)}, u32[]{:S(2)}) collective-permute-start(bf16[128,384]{1,0:T(8,128)(2,1)S(1)} %get-tuple-element.41), channel_id=1, source_target_pairs={{0,8},{4,12},{8,0},{12,4},{1,9},{5,13},{9,1},{13,5},{2,10},{6,14},... | collective-permute-start | bytes 294920 | tf_op jit(solution)/shard_map/ppermute | solution.py:31
  29.9 1.4 %collective-permute-start.11 = (bf16[128,384]{1,0:T(8,128)(2,1)S(1)}, bf16[128,384]{1,0:T(8,128)(2,1)S(1)}, u32[]{:S(2)}, u32[]{:S(2)}) collective-permute-start(bf16[128,384]{1,0:T(8,128)(2,1)S(1)} %get-tuple-element.42), channel_id=1, source_target_pairs={{0,12},{4,8},{8,4},{12,0},{1,13},{5,9},{9,5},{13,1},{2,14},{6,10},... | collective-permute-start | bytes 294920 | tf_op jit(solution)/shard_map/ppermute | solution.py:31
  31.2 0.8 %attend.4 = bf16[128,384]{1,0:T(8,128)(2,1)S(1)} custom-call(bf16[128,256]{1,0:T(8,128)(2,1)S(1)} %get-tuple-element.38.refs_0_, bf16[512,128]{1,0:T(8,128)(2,1)S(1)} %get-tuple-element.33.refs_1_.refs_2_, bf16[512,128]{1,0:T(8,128)(2,1)S(1)} %get-tuple-element.34.refs_2_.refs_3_, bf16[128,512]{1,0:T(8,128)(2,1)S(1)} %get-tuple-element.35.refs_3_.refs_4_, ...), custom_call_target="tpu_custom_call" | custom-call | flops 33554432 | bytes 1048576 | tf_op jit(solution)/shard_map/attend/pallas_call | solution.py:261
  32.3 0.8 %attend.3.last1.refs_6_ = bf16[128,384]{1,0:T(8,128)(2,1)S(1)} custom-call(bf16[128,256]{1,0:T(8,128)(2,1)S(1)} %get-tuple-element.32.refs_0_, bf16[512,128]{1,0:T(8,128)(2,1)S(1)} %get-tuple-element.33.refs_1_.refs_2_, bf16[512,128]{1,0:T(8,128)(2,1)S(1)} %get-tuple-element.34.refs_2_.refs_3_, bf16[128,512]{1,0:T(8,128)(2,1)S(1)} %get-tuple-element.35.refs_3_.refs_4_, ...), custom_call_target="tpu_custom_call" | custom-call | flops 33554432 | bytes 1048576 | tf_op jit(solution)/shard_map/attend/pallas_call | solution.py:261
  33.1 3.0 %collective-permute-done.2.last0.refs_5_ = bf16[640,512]{1,0:T(8,128)(2,1)S(1)} collective-permute-done((bf16[640,512]{1,0:T(8,128)(2,1)S(1)}, bf16[640,512]{1,0:T(8,128)(2,1)S(1)}, u32[]{:S(2)}, u32[]{:S(2)}) %collective-permute-start.2) | collective-permute-done | bytes 655392 | tf_op jit(solution)/shard_map/ppermute | solution.py:31
  36.4 1.2 %collective-permute-done.10.refs_8_ = bf16[128,384]{1,0:T(8,128)(2,1)S(1)} collective-permute-done((bf16[128,384]{1,0:T(8,128)(2,1)S(1)}, bf16[128,384]{1,0:T(8,128)(2,1)S(1)}, u32[]{:S(2)}, u32[]{:S(2)}) %collective-permute-start.10) | collective-permute-done | bytes 98336 | tf_op jit(solution)/shard_map/ppermute | solution.py:31
  37.6 0.5 %collective-permute-done.9.refs_7_ = bf16[128,384]{1,0:T(8,128)(2,1)S(1)} collective-permute-done((bf16[128,384]{1,0:T(8,128)(2,1)S(1)}, bf16[128,384]{1,0:T(8,128)(2,1)S(1)}, u32[]{:S(2)}, u32[]{:S(2)}) %collective-permute-start.9) | collective-permute-done | bytes 98336 | tf_op jit(solution)/shard_map/ppermute | solution.py:31
  38.1 1.7 %join.1 = (f32[128,512]{1,0:T(8,128)S(1)}, bf16[128,512]{1,0:T(8,128)(2,1)S(1)}) custom-call(bf16[1024,512]{1,0:T(8,128)(2,1)S(1)} %copy-done.1, bf16[512,512]{1,0:T(8,128)(2,1)S(1)} %copy-done.5, f32[128,512]{1,0:T(8,128)S(1)} %convolve.1.refs_2_, bf16[464,512]{1,0:T(8,128)(2,1)S(1)} %collective-permute-done.received.refs_3_, ...), custom_call_target="tpu_custom_call" | custom-call | flops 402653184 | bytes 4194304 | tf_op jit(solution)/shard_map/join/pallas_call | solution.py:261
  39.9 1.3 %collective-permute-done.12 = bf16[128,512]{1,0:T(8,128)(2,1)S(1)} collective-permute-done((bf16[128,512]{1,0:T(8,128)(2,1)S(1)}, bf16[128,512]{1,0:T(8,128)(2,1)S(1)}, u32[]{:S(2)}, u32[]{:S(2)}) %collective-permute-start.12) | collective-permute-done | bytes 131104 | tf_op jit(solution)/shard_map/ppermute | solution.py:31
  41.3 0.7 %reshape.11 = bf16[64,2,512]{2,1,0:T(2,128)(2,1)} reshape(bf16[128,512]{1,0:T(8,128)(2,1)S(1)} %add_convert_fusion) | data formatting | bytes 262144 | tf_op jit(solution)/shard_map/reshape | solution.py:397
  (40 shorter events, 1.5 us)
Async XLA Ops:
  0.0 4.2 %copy-start.9 = (bf16[64,2,1024]{2,1,0:T(2,128)(2,1)S(1)}, bf16[64,2,1024]{2,1,0:T(2,128)(2,1)}, u32[]{:S(2)}) copy-start(bf16[64,2,1024]{2,1,0:T(2,128)(2,1)} %param.10) | copy-start | bytes 786436
  0.0 4.3 %copy-start.7 = (s32[1,1,4]{2,1,0:T(1,128)S(1)}, s32[1,1,4]{2,1,0:T(1,128)}, u32[]{:S(2)}) copy-start(s32[1,1,4]{2,1,0:T(1,128)} %param.12) | copy-start | bytes 52
  0.0 4.3 %copy-start.6 = (f32[1024]{0:T(1024)S(1)}, f32[1024]{0:T(1024)}, u32[]{:S(2)}) copy-start(f32[1024]{0:T(1024)} %param.11) | copy-start | bytes 12292
  0.0 6.5 %copy-start.1 = (bf16[1024,512]{1,0:T(8,128)(2,1)S(1)}, bf16[1024,512]{1,0:T(8,128)(2,1)}, u32[]{:S(2)}) copy-start(bf16[1024,512]{1,0:T(8,128)(2,1)} %refs_0_.1) | copy-start | bytes 3145732
  1.1 12.9 %collective-permute-start.6 = (bf16[256,640]{1,0:T(8,128)(2,1)S(1)}, bf16[256,640]{1,0:T(8,128)(2,1)S(1)}, u32[]{:S(2)}, u32[]{:S(2)}) collective-permute-start(bf16[256,640]{1,0:T(8,128)(2,1)S(1)} %pack.1.after), channel_id=1, source_target_pairs={{0,2},{2,0},{1,3},{3,1},{4,6},{6,4},{5,7},{7,5},{8,10},{10,8},{9,1... | collective-permute-start | bytes 983048 | tf_op jit(solution)/shard_map/ppermute | solution.py:31
  4.9 8.6 %collective-permute-start.1 = (bf16[136,1024]{1,0:T(8,128)(2,1)S(1)}, bf16[136,1024]{1,0:T(8,128)(2,1)S(1)}, u32[]{:S(2)}, u32[]{:S(2)}) collective-permute-start(bf16[136,1024]{1,0:T(8,128)(2,1)S(1)} %get-tuple-element.29), channel_id=1, source_target_pairs={{0,4},{1,9},{4,0},{5,13},{8,12},{9,1},{12,8},{13,5},{2,6},{3,11},{... | collective-permute-start | bytes 835592 | tf_op jit(solution)/shard_map/ppermute | solution.py:40
  6.5 0.9 %slice-start = ((bf16[1024,512]{1,0:T(8,128)(2,1)}), bf16[128,512]{1,0:T(8,128)(2,1)S(1)}, s32[]{:S(2)}) async-start(bf16[1024,512]{1,0:T(8,128)(2,1)} %refs_0_.1), calls=%async_computation | async-start | bytes 262144 | tf_op jit(solution)/shard_map/slice | solution.py:332
  6.5 1.1 %copy-start.5 = (bf16[512,512]{1,0:T(8,128)(2,1)S(1)}, bf16[512,512]{1,0:T(8,128)(2,1)}, u32[]{:S(2)}) copy-start(bf16[512,512]{1,0:T(8,128)(2,1)} %refs_1_.1) | copy-start | bytes 1572868
  6.5 15.1 %copy-start.3 = (bf16[512,512]{1,0:T(8,128)(2,1)S(1)}, bf16[512,512]{1,0:T(8,128)(2,1)}, u32[]{:S(2)}) copy-start(bf16[512,512]{1,0:T(8,128)(2,1)} %w_key.3) | copy-start | bytes 1572868
  6.6 15.1 %copy-start.4 = (bf16[512,512]{1,0:T(8,128)(2,1)S(1)}, bf16[512,512]{1,0:T(8,128)(2,1)}, u32[]{:S(2)}) copy-start(bf16[512,512]{1,0:T(8,128)(2,1)} %w_value.3) | copy-start | bytes 1572868
  6.6 15.0 %copy-start = (bf16[512,1024]{1,0:T(8,128)(2,1)S(1)}, bf16[512,1024]{1,0:T(8,128)(2,1)}, u32[]{:S(2)}) copy-start(bf16[512,1024]{1,0:T(8,128)(2,1)} %w_up.3) | copy-start | bytes 3145732
  6.6 15.0 %copy-start.2 = (bf16[512,512]{1,0:T(8,128)(2,1)S(1)}, bf16[512,512]{1,0:T(8,128)(2,1)}, u32[]{:S(2)}) copy-start(bf16[512,512]{1,0:T(8,128)(2,1)} %w_query.3) | copy-start | bytes 1572868
  6.6 16.2 %collective-permute-start = (bf16[464,512]{1,0:T(8,128)(2,1)S(1)}, bf16[464,512]{1,0:T(8,128)(2,1)S(1)}, u32[]{:S(2)}, u32[]{:S(2)}) collective-permute-start(bf16[464,512]{1,0:T(8,128)(2,1)S(1)} %pad_maximum_fusion.1), channel_id=1, source_target_pairs={{0,2},{2,0},{1,3},{3,1},{4,6},{6,4},{5,7},{7,5},{8,10},{10,8},{9,1... | collective-permute-start | bytes 1425416 | tf_op jit(solution)/shard_map/ppermute | solution.py:31
  13.5 22.6 %collective-permute-start.2 = (bf16[640,512]{1,0:T(8,128)(2,1)S(1)}, bf16[640,512]{1,0:T(8,128)(2,1)S(1)}, u32[]{:S(2)}, u32[]{:S(2)}) collective-permute-start(bf16[640,512]{1,0:T(8,128)(2,1)S(1)} %pad_maximum_fusion), channel_id=1, source_target_pairs={{0,2},{2,0},{1,3},{3,1},{4,6},{6,4},{5,7},{7,5},{8,10},{10,8},{9,1... | collective-permute-start | bytes 1966088 | tf_op jit(solution)/shard_map/ppermute | solution.py:31
  14.0 11.0 %collective-permute-start.7 = (bf16[256,640]{1,0:T(8,128)(2,1)S(1)}, bf16[256,640]{1,0:T(8,128)(2,1)S(1)}, u32[]{:S(2)}, u32[]{:S(2)}) collective-permute-start(bf16[256,640]{1,0:T(8,128)(2,1)S(1)} %collective-permute-done.6.refs_6_), channel_id=1, source_target_pairs={{0,16},{16,0},{1,17},{17,1},{2,18},{18,2},{3,19},{19,3},{4,20},{20... | collective-permute-start | bytes 983048 | tf_op jit(solution)/shard_map/ppermute | solution.py:31
  15.5 6.1 %collective-permute-start.4 = (bf16[72,1024]{1,0:T(8,128)(2,1)S(1)}, bf16[72,1024]{1,0:T(8,128)(2,1)S(1)}, u32[]{:S(2)}, u32[]{:S(2)}) collective-permute-start(bf16[72,1024]{1,0:T(8,128)(2,1)S(1)} %split.1), channel_id=1, source_target_pairs={{0,8},{1,5},{4,12},{5,1},{8,0},{9,13},{12,4},{13,9},{2,10},{3,7},{... | collective-permute-start | bytes 442376 | tf_op jit(solution)/shard_map/ppermute | solution.py:40
  18.2 6.8 %collective-permute-start.3 = (bf16[136,1024]{1,0:T(8,128)(2,1)S(1)}, bf16[136,1024]{1,0:T(8,128)(2,1)S(1)}, u32[]{:S(2)}, u32[]{:S(2)}) collective-permute-start(bf16[136,1024]{1,0:T(8,128)(2,1)S(1)} %collective-permute-done.1.block.refs_1_), channel_id=1, source_target_pairs={{0,1},{1,0},{2,3},{3,2},{4,5},{5,4},{6,7},{7,6},{8,9},{9,8},{10,11... | collective-permute-start | bytes 835592 | tf_op jit(solution)/shard_map/ppermute | solution.py:31
  21.6 3.3 %collective-permute-start.5 = (bf16[72,1024]{1,0:T(8,128)(2,1)S(1)}, bf16[72,1024]{1,0:T(8,128)(2,1)S(1)}, u32[]{:S(2)}, u32[]{:S(2)}) collective-permute-start(bf16[72,1024]{1,0:T(8,128)(2,1)S(1)} %collective-permute-done.4.refs_3_), channel_id=1, source_target_pairs={{0,1},{1,0},{2,3},{3,2},{4,5},{5,4},{6,7},{7,6},{8,9},{9,8},{10,11... | collective-permute-start | bytes 442376 | tf_op jit(solution)/shard_map/ppermute | solution.py:31
  22.9 15.3 %collective-permute-start.8 = (bf16[464,512]{1,0:T(8,128)(2,1)S(1)}, bf16[464,512]{1,0:T(8,128)(2,1)S(1)}, u32[]{:S(2)}, u32[]{:S(2)}) collective-permute-start(bf16[464,512]{1,0:T(8,128)(2,1)S(1)} %collective-permute-done.received.refs_3_), channel_id=1, source_target_pairs={{0,16},{16,0},{1,17},{17,1},{2,18},{18,2},{3,19},{19,3},{4,20},{20... | collective-permute-start | bytes 1425416 | tf_op jit(solution)/shard_map/ppermute | solution.py:31
  26.1 10.0 %copy-start.8 = (f32[5,512]{1,0:T(8,128)S(1)}, f32[5,512]{1,0:T(8,128)}, u32[]{:S(2)}) copy-start(f32[5,512]{1,0:T(8,128)} %taps.1) | copy-start | bytes 30724
  27.2 10.4 %collective-permute-start.10 = (bf16[128,384]{1,0:T(8,128)(2,1)S(1)}, bf16[128,384]{1,0:T(8,128)(2,1)S(1)}, u32[]{:S(2)}, u32[]{:S(2)}) collective-permute-start(bf16[128,384]{1,0:T(8,128)(2,1)S(1)} %get-tuple-element.41), channel_id=1, source_target_pairs={{0,8},{4,12},{8,0},{12,4},{1,9},{5,13},{9,1},{13,5},{2,10},{6,14},... | collective-permute-start | bytes 294920 | tf_op jit(solution)/shard_map/ppermute | solution.py:31
  29.9 7.7 %collective-permute-start.11 = (bf16[128,384]{1,0:T(8,128)(2,1)S(1)}, bf16[128,384]{1,0:T(8,128)(2,1)S(1)}, u32[]{:S(2)}, u32[]{:S(2)}) collective-permute-start(bf16[128,384]{1,0:T(8,128)(2,1)S(1)} %get-tuple-element.42), channel_id=1, source_target_pairs={{0,12},{4,8},{8,4},{12,0},{1,13},{5,9},{9,5},{13,1},{2,14},{6,10},... | collective-permute-start | bytes 294920 | tf_op jit(solution)/shard_map/ppermute | solution.py:31
  32.0 6.1 %collective-permute-start.9 = (bf16[128,384]{1,0:T(8,128)(2,1)S(1)}, bf16[128,384]{1,0:T(8,128)(2,1)S(1)}, u32[]{:S(2)}, u32[]{:S(2)}) collective-permute-start(bf16[128,384]{1,0:T(8,128)(2,1)S(1)} %attend.4), channel_id=1, source_target_pairs={{0,4},{4,0},{8,12},{12,8},{1,5},{5,1},{9,13},{13,9},{2,6},{6,2},{1... | collective-permute-start | bytes 294920 | tf_op jit(solution)/shard_map/ppermute | solution.py:31
  39.8 1.4 %collective-permute-start.12 = (bf16[128,512]{1,0:T(8,128)(2,1)S(1)}, bf16[128,512]{1,0:T(8,128)(2,1)S(1)}, u32[]{:S(2)}, u32[]{:S(2)}) collective-permute-start(bf16[128,512]{1,0:T(8,128)(2,1)S(1)} %get-tuple-element.44), channel_id=1, source_target_pairs={{0,1},{1,0},{2,3},{3,2},{4,5},{5,4},{6,7},{7,6},{8,9},{9,8},{10,11... | collective-permute-start | bytes 393224 | tf_op jit(solution)/shard_map/ppermute | solution.py:31

commit v7 on v6

--- a/solution.py
+++ b/solution.py
@@ -226,24 +226,18 @@
     near_down, near_out, base = refs[:3]
     far_down, farther_down, far_out = refs[3:6]
     parts = refs[6 : 6 + n_ctx]
-    keep, send, down, out, acts, atts, sems = refs[6 + n_ctx :]
+    keep, send, down, acts, atts = refs[6 + n_ctx :]
     ctx, tm, groups, tp = (lax.axis_index(name) for name in AXES)
     hidden, wide = acts.shape[1] // n_ctx, atts.shape[1] // n_ctx
-    count = farther_down.shape[0] - 16
-    pairs = []
+    count, depth = farther_down.shape[0] - 16, near_out.shape[0]
+    down[slot(groups, count), :] = far_down[0:count, :]
+    down[slot(1 - groups, count), :] = farther_down[0:count, :]
+    down[2 * count :, :] = far_out[depth:, :]
     for d in range(n_ctx):
-        pairs.append((parts[d].at[:, 0:hidden], acts.at[:, slot(ctx ^ d, hidden)]))
-        pairs.append((parts[d].at[:, hidden:], atts.at[:, slot(ctx ^ d, wide)]))
-    pairs.append((far_out.at[0 : out.shape[0]], out))
-    pairs.append((far_out.at[out.shape[0] :], down.at[2 * count :]))
-    pairs.append((far_down.at[0:count], down.at[slot(groups, count)]))
-    pairs.append((farther_down.at[0:count], down.at[slot(1 - groups, count)]))
-    copies = begin(sems, pairs)
-
-    end(copies[: 2 * n_ctx])
+        acts[:, slot(ctx ^ d, hidden)] = parts[d][:, 0:hidden]
+        atts[:, slot(ctx ^ d, wide)] = parts[d][:, hidden:]
     near_sum = dot(acts[...], near_down[...]) + dot(atts[...], near_out[...])
-    end(copies[2 * n_ctx :])
-    far_sum = dot(acts[...], down[...]) + dot(atts[...], out[...])
+    far_sum = dot(acts[...], down[...]) + dot(atts[...], far_out[0:depth, :])
     same = tm == tp
     keep[...] = jnp.where(same, near_sum, far_sum) + base[...]
     send[...] = jnp.where(same, far_sum, near_sum).astype(jnp.bfloat16)
@@ -381,14 +375,12 @@
         "join",
         [((rows, columns), f32), ((rows, columns), bf16)],
         [(VMEM, w_down), (VMEM, w_out), (VMEM, base)]
-        + [(ANY, value) for value in (x_down, y_down, x_out)]
-        + [(ANY, value) for value in parts],
+        + [(VMEM, value) for value in (x_down, y_down, x_out)]
+        + [(VMEM, value) for value in parts],
         [
             pltpu.VMEM(w_down.shape, bf16),
-            pltpu.VMEM(w_out.shape, bf16),
             pltpu.VMEM((rows, w_down.shape[0]), bf16),
             pltpu.VMEM((rows, w_out.shape[0]), bf16),
-            pltpu.SemaphoreType.DMA((2 * n_ctx + 4,)),
         ],
         flops=4 * rows * columns * n_ctx * (hidden + wide),
         moved=4 << 20,

time: 42.1 us -> 41.1 us (0.976)
  Pallas kernels: 7.61 us -> 6.54 us
    pallas_call x10, Pallas kernels: 7.61 us -> 6.54 us  [call(): pl.pallas_call(kernel, out_shape=[jax.ShapeDtypeStruct(shape, dtype) for...]
  transfers between devices with their start and end apart: 13 -> 13, of which waited for: 7 -> 7; matrix products, arithmetic and copies ran while one was open for 0% -> 1% of each run, Pallas kernels for 11% -> 12%
where the time goes in v7:
time: 41.1 us; the launch traced here: 40.9 us
  starting transfers between devices  16.4 us (40%)
  waiting for transfers between devices  16.4 us (40%)
  Pallas kernels  6.54 us (16%)
  local copies, waits for them, and re-layouts  1.28 us (3%)
    ppermute x11, starting transfers between devices, across(): lax.ppermute(value, axis, [(source, source ^ step) for source in range(co...  12.1 us
    ppermute x2, waiting for transfers between devices, two_ways(): return lax.ppermute(value, ('ctx', 'tp'), pairs)  9.25 us
    ppermute x11, waiting for transfers between devices, across(): lax.ppermute(value, axis, [(source, source ^ step) for source in range(co...  7.16 us
    pallas_call x10, Pallas kernels, call(): pl.pallas_call(kernel, out_shape=[jax.ShapeDtypeStruct(shape, dtype) for...  6.54 us
    ppermute x2, starting transfers between devices, two_ways(): return lax.ppermute(value, ('ctx', 'tp'), pairs)  4.28 us
  transfers between devices with their start and end apart: 13, of which 7 were waited for; matrix products, arithmetic and copies ran while one was open for 1% of the time, Pallas kernels for 12%

profile of v7, /device:TPU:0, one launch (start us, length us, event | category | flops | bytes accessed | tf_op | source)
XLA Modules:
  0.0 40.9 jit_solution(13280201702400062127)
XLA Ops:
  0.0 1.1 %pack.1.after = bf16[256,640]{1,0:T(8,128)(2,1)S(1)} custom-call(bf16[512,1024]{1,0:T(8,128)(2,1)} %w_up.3, bf16[512,512]{1,0:T(8,128)(2,1)} %w_query.3, bf16[512,512]{1,0:T(8,128)(2,1)} %w_key.3, bf16[512,512]{1,0:T(8,128)(2,1)} %w_value.3), custom_call_target="tpu_custom_call" | custom-call | bytes 1048576 | tf_op jit(solution)/shard_map/pack/pallas_call | solution.py:255
  1.1 3.0 %collective-permute-start.6 = (bf16[256,640]{1,0:T(8,128)(2,1)S(1)}, bf16[256,640]{1,0:T(8,128)(2,1)S(1)}, u32[]{:S(2)}, u32[]{:S(2)}) collective-permute-start(bf16[256,640]{1,0:T(8,128)(2,1)S(1)} %pack.1.after), channel_id=1, source_target_pairs={{0,2},{2,0},{1,3},{3,1},{4,6},{6,4},{5,7},{7,5},{8,10},{10,8},{9,1... | collective-permute-start | bytes 983048 | tf_op jit(solution)/shard_map/ppermute | solution.py:31
  4.3 0.6 %normalise.1 = (bf16[136,1024]{1,0:T(8,128)(2,1)S(1)}, bf16[136,1024]{1,0:T(8,128)(2,1)S(1)}, bf16[128,512]{1,0:T(8,128)(2,1)S(1)}, bf16[16,512]{1,0:T(8,128)(2,1)S(1)}) custom-call(s32[1,4]{1,0:T(1,128)S(1)} %bitcast.3, bf16[128,1024]{1,0:T(8,128)(2,1)S(1)} %reshape.9.tokens, f32[1,1024]{1,0:T(1,128)S(1)} %bitcast.2), custom_call_target="tpu_custom_call" | custom-call | bytes 1048576 | tf_op jit(solution)/shard_map/normalise/pallas_call | solution.py:255
  4.9 1.6 %collective-permute-start.1 = (bf16[136,1024]{1,0:T(8,128)(2,1)S(1)}, bf16[136,1024]{1,0:T(8,128)(2,1)S(1)}, u32[]{:S(2)}, u32[]{:S(2)}) collective-permute-start(bf16[136,1024]{1,0:T(8,128)(2,1)S(1)} %get-tuple-element.29), channel_id=1, source_target_pairs={{0,4},{1,9},{4,0},{5,13},{8,12},{9,1},{12,8},{13,5},{2,6},{3,11},{... | collective-permute-start | bytes 835592 | tf_op jit(solution)/shard_map/ppermute | solution.py:40
  6.6 0.6 %collective-permute-start = (bf16[464,512]{1,0:T(8,128)(2,1)S(1)}, bf16[464,512]{1,0:T(8,128)(2,1)S(1)}, u32[]{:S(2)}, u32[]{:S(2)}) collective-permute-start(bf16[464,512]{1,0:T(8,128)(2,1)S(1)} %pad_maximum_fusion.1), channel_id=1, source_target_pairs={{0,2},{2,0},{1,3},{3,1},{4,6},{6,4},{5,7},{7,5},{8,10},{10,8},{9,1... | collective-permute-start | bytes 1425416 | tf_op jit(solution)/shard_map/ppermute | solution.py:31
  7.7 5.8 %collective-permute-done.1.block.refs_1_ = bf16[136,1024]{1,0:T(8,128)(2,1)S(1)} collective-permute-done((bf16[136,1024]{1,0:T(8,128)(2,1)S(1)}, bf16[136,1024]{1,0:T(8,128)(2,1)S(1)}, u32[]{:S(2)}, u32[]{:S(2)}) %collective-permute-start.1) | collective-permute-done | bytes 278560 | tf_op jit(solution)/shard_map/ppermute | solution.py:40
  13.5 0.5 %collective-permute-start.2 = (bf16[640,512]{1,0:T(8,128)(2,1)S(1)}, bf16[640,512]{1,0:T(8,128)(2,1)S(1)}, u32[]{:S(2)}, u32[]{:S(2)}) collective-permute-start(bf16[640,512]{1,0:T(8,128)(2,1)S(1)} %pad_maximum_fusion), channel_id=1, source_target_pairs={{0,2},{2,0},{1,3},{3,1},{4,6},{6,4},{5,7},{7,5},{8,10},{10,8},{9,1... | collective-permute-start | bytes 1966088 | tf_op jit(solution)/shard_map/ppermute | solution.py:31
  14.0 1.5 %collective-permute-start.7 = (bf16[256,640]{1,0:T(8,128)(2,1)S(1)}, bf16[256,640]{1,0:T(8,128)(2,1)S(1)}, u32[]{:S(2)}, u32[]{:S(2)}) collective-permute-start(bf16[256,640]{1,0:T(8,128)(2,1)S(1)} %collective-permute-done.6.refs_6_), channel_id=1, source_target_pairs={{0,16},{16,0},{1,17},{17,1},{2,18},{18,2},{3,19},{19,3},{4,20},{20... | collective-permute-start | bytes 983048 | tf_op jit(solution)/shard_map/ppermute | solution.py:31
  15.5 2.6 %collective-permute-start.4 = (bf16[72,1024]{1,0:T(8,128)(2,1)S(1)}, bf16[72,1024]{1,0:T(8,128)(2,1)S(1)}, u32[]{:S(2)}, u32[]{:S(2)}) collective-permute-start(bf16[72,1024]{1,0:T(8,128)(2,1)S(1)} %split.1), channel_id=1, source_target_pairs={{0,8},{1,5},{4,12},{5,1},{8,0},{9,13},{12,4},{13,9},{2,10},{3,7},{... | collective-permute-start | bytes 442376 | tf_op jit(solution)/shard_map/ppermute | solution.py:40
  18.2 3.5 %collective-permute-done.4.refs_3_ = bf16[72,1024]{1,0:T(8,128)(2,1)S(1)} collective-permute-done((bf16[72,1024]{1,0:T(8,128)(2,1)S(1)}, bf16[72,1024]{1,0:T(8,128)(2,1)S(1)}, u32[]{:S(2)}, u32[]{:S(2)}) %collective-permute-start.4) | collective-permute-done | bytes 147488 | tf_op jit(solution)/shard_map/ppermute | solution.py:40
  21.8 1.0 %collective-permute-done.received.refs_3_ = bf16[464,512]{1,0:T(8,128)(2,1)S(1)} collective-permute-done((bf16[464,512]{1,0:T(8,128)(2,1)S(1)}, bf16[464,512]{1,0:T(8,128)(2,1)S(1)}, u32[]{:S(2)}, u32[]{:S(2)}) %collective-permute-start) | collective-permute-done | bytes 475168 | tf_op jit(solution)/shard_map/ppermute | solution.py:31
  22.9 2.1 %collective-permute-start.8 = (bf16[464,512]{1,0:T(8,128)(2,1)S(1)}, bf16[464,512]{1,0:T(8,128)(2,1)S(1)}, u32[]{:S(2)}, u32[]{:S(2)}) collective-permute-start(bf16[464,512]{1,0:T(8,128)(2,1)S(1)} %collective-permute-done.received.refs_3_), channel_id=1, source_target_pairs={{0,16},{16,0},{1,17},{17,1},{2,18},{18,2},{3,19},{19,3},{4,20},{20... | collective-permute-start | bytes 1425416 | tf_op jit(solution)/shard_map/ppermute | solution.py:31
  25.0 1.1 %project.1 = (bf16[128,256]{1,0:T(8,128)(2,1)S(1)}, bf16[128,256]{1,0:T(8,128)(2,1)S(1)}, bf16[128,256]{1,0:T(8,128)(2,1)S(1)}, bf16[128,256]{1,0:T(8,128)(2,1)S...) custom-call(bf16[136,1024]{1,0:T(8,128)(2,1)S(1)} %get-tuple-element, ...), custom_call_target="tpu_custom_call" | custom-call | flops 671088640 | bytes 4194304 | tf_op jit(solution)/shard_map/project/pallas_call | solution.py:255
  26.1 1.1 %attend.5 = (bf16[128,384]{1,0:T(8,128)(2,1)S(1)}, bf16[128,384]{1,0:T(8,128)(2,1)S(1)}) custom-call(bf16[128,256]{1,0:T(8,128)(2,1)S(1)} %get-tuple-element.39.refs_0_, bf16[128,256]{1,0:T(8,128)(2,1)S(1)} %get-tuple-element.40.refs_1_, bf16[512,128]{1,0:T(8,128)(2,1)S(1)} %get-tuple-element.33.refs_1_.refs_2_, ...), custom_call_target="tpu_custom_call" | custom-call | flops 67108864 | bytes 1048576 | tf_op jit(solution)/shard_map/attend/pallas_call | solution.py:255
  27.2 2.7 %collective-permute-start.10 = (bf16[128,384]{1,0:T(8,128)(2,1)S(1)}, bf16[128,384]{1,0:T(8,128)(2,1)S(1)}, u32[]{:S(2)}, u32[]{:S(2)}) collective-permute-start(bf16[128,384]{1,0:T(8,128)(2,1)S(1)} %get-tuple-element.41), channel_id=1, source_target_pairs={{0,8},{4,12},{8,0},{12,4},{1,9},{5,13},{9,1},{13,5},{2,10},{6,14},... | collective-permute-start | bytes 294920 | tf_op jit(solution)/shard_map/ppermute | solution.py:31
  29.9 1.4 %collective-permute-start.11 = (bf16[128,384]{1,0:T(8,128)(2,1)S(1)}, bf16[128,384]{1,0:T(8,128)(2,1)S(1)}, u32[]{:S(2)}, u32[]{:S(2)}) collective-permute-start(bf16[128,384]{1,0:T(8,128)(2,1)S(1)} %get-tuple-element.42), channel_id=1, source_target_pairs={{0,12},{4,8},{8,4},{12,0},{1,13},{5,9},{9,5},{13,1},{2,14},{6,10},... | collective-permute-start | bytes 294920 | tf_op jit(solution)/shard_map/ppermute | solution.py:31
  31.2 0.8 %attend.4 = bf16[128,384]{1,0:T(8,128)(2,1)S(1)} custom-call(bf16[128,256]{1,0:T(8,128)(2,1)S(1)} %get-tuple-element.38.refs_0_, bf16[512,128]{1,0:T(8,128)(2,1)S(1)} %get-tuple-element.33.refs_1_.refs_2_, bf16[512,128]{1,0:T(8,128)(2,1)S(1)} %get-tuple-element.34.refs_2_.refs_3_, bf16[128,512]{1,0:T(8,128)(2,1)S(1)} %get-tuple-element.35.refs_3_.refs_4_, ...), custom_call_target="tpu_custom_call" | custom-call | flops 33554432 | bytes 1048576 | tf_op jit(solution)/shard_map/attend/pallas_call | solution.py:255
  32.3 0.8 %attend.3.last1.refs_6_ = bf16[128,384]{1,0:T(8,128)(2,1)S(1)} custom-call(bf16[128,256]{1,0:T(8,128)(2,1)S(1)} %get-tuple-element.32.refs_0_, bf16[512,128]{1,0:T(8,128)(2,1)S(1)} %get-tuple-element.33.refs_1_.refs_2_, bf16[512,128]{1,0:T(8,128)(2,1)S(1)} %get-tuple-element.34.refs_2_.refs_3_, bf16[128,512]{1,0:T(8,128)(2,1)S(1)} %get-tuple-element.35.refs_3_.refs_4_, ...), custom_call_target="tpu_custom_call" | custom-call | flops 33554432 | bytes 1048576 | tf_op jit(solution)/shard_map/attend/pallas_call | solution.py:255
  33.1 3.0 %collective-permute-done.2.last0.refs_5_ = bf16[640,512]{1,0:T(8,128)(2,1)S(1)} collective-permute-done((bf16[640,512]{1,0:T(8,128)(2,1)S(1)}, bf16[640,512]{1,0:T(8,128)(2,1)S(1)}, u32[]{:S(2)}, u32[]{:S(2)}) %collective-permute-start.2) | collective-permute-done | bytes 655392 | tf_op jit(solution)/shard_map/ppermute | solution.py:31
  36.4 1.2 %collective-permute-done.10.refs_8_ = bf16[128,384]{1,0:T(8,128)(2,1)S(1)} collective-permute-done((bf16[128,384]{1,0:T(8,128)(2,1)S(1)}, bf16[128,384]{1,0:T(8,128)(2,1)S(1)}, u32[]{:S(2)}, u32[]{:S(2)}) %collective-permute-start.10) | collective-permute-done | bytes 98336 | tf_op jit(solution)/shard_map/ppermute | solution.py:31
  37.6 0.5 %collective-permute-done.9.refs_7_ = bf16[128,384]{1,0:T(8,128)(2,1)S(1)} collective-permute-done((bf16[128,384]{1,0:T(8,128)(2,1)S(1)}, bf16[128,384]{1,0:T(8,128)(2,1)S(1)}, u32[]{:S(2)}, u32[]{:S(2)}) %collective-permute-start.9) | collective-permute-done | bytes 98336 | tf_op jit(solution)/shard_map/ppermute | solution.py:31
  38.1 0.6 %join.1 = (f32[128,512]{1,0:T(8,128)S(1)}, bf16[128,512]{1,0:T(8,128)(2,1)S(1)}) custom-call(bf16[1024,512]{1,0:T(8,128)(2,1)S(1)} %copy-done.1, bf16[512,512]{1,0:T(8,128)(2,1)S(1)} %copy-done.5, f32[128,512]{1,0:T(8,128)S(1)} %convolve.1.refs_2_, bf16[464,512]{1,0:T(8,128)(2,1)S(1)} %collective-permute-done.received.refs_3_, ...), custom_call_target="tpu_custom_call" | custom-call | flops 402653184 | bytes 4194304 | tf_op jit(solution)/shard_map/join/pallas_call | solution.py:255
  38.9 1.3 %collective-permute-done.12 = bf16[128,512]{1,0:T(8,128)(2,1)S(1)} collective-permute-done((bf16[128,512]{1,0:T(8,128)(2,1)S(1)}, bf16[128,512]{1,0:T(8,128)(2,1)S(1)}, u32[]{:S(2)}, u32[]{:S(2)}) %collective-permute-start.12) | collective-permute-done | bytes 131104 | tf_op jit(solution)/shard_map/ppermute | solution.py:31
  40.2 0.7 %reshape.11 = bf16[64,2,512]{2,1,0:T(2,128)(2,1)} reshape(bf16[128,512]{1,0:T(8,128)(2,1)S(1)} %add_convert_fusion) | data formatting | bytes 262144 | tf_op jit(solution)/shard_map/reshape | solution.py:389
  (40 shorter events, 1.5 us)
Async XLA Ops:
  0.0 4.2 %copy-start.9 = (bf16[64,2,1024]{2,1,0:T(2,128)(2,1)S(1)}, bf16[64,2,1024]{2,1,0:T(2,128)(2,1)}, u32[]{:S(2)}) copy-start(bf16[64,2,1024]{2,1,0:T(2,128)(2,1)} %param.10) | copy-start | bytes 786436
  0.0 4.3 %copy-start.7 = (s32[1,1,4]{2,1,0:T(1,128)S(1)}, s32[1,1,4]{2,1,0:T(1,128)}, u32[]{:S(2)}) copy-start(s32[1,1,4]{2,1,0:T(1,128)} %param.12) | copy-start | bytes 52
  0.0 4.3 %copy-start.6 = (f32[1024]{0:T(1024)S(1)}, f32[1024]{0:T(1024)}, u32[]{:S(2)}) copy-start(f32[1024]{0:T(1024)} %param.11) | copy-start | bytes 12292
  0.0 6.5 %copy-start.1 = (bf16[1024,512]{1,0:T(8,128)(2,1)S(1)}, bf16[1024,512]{1,0:T(8,128)(2,1)}, u32[]{:S(2)}) copy-start(bf16[1024,512]{1,0:T(8,128)(2,1)} %refs_0_.1) | copy-start | bytes 3145732
  1.1 12.9 %collective-permute-start.6 = (bf16[256,640]{1,0:T(8,128)(2,1)S(1)}, bf16[256,640]{1,0:T(8,128)(2,1)S(1)}, u32[]{:S(2)}, u32[]{:S(2)}) collective-permute-start(bf16[256,640]{1,0:T(8,128)(2,1)S(1)} %pack.1.after), channel_id=1, source_target_pairs={{0,2},{2,0},{1,3},{3,1},{4,6},{6,4},{5,7},{7,5},{8,10},{10,8},{9,1... | collective-permute-start | bytes 983048 | tf_op jit(solution)/shard_map/ppermute | solution.py:31
  4.9 8.6 %collective-permute-start.1 = (bf16[136,1024]{1,0:T(8,128)(2,1)S(1)}, bf16[136,1024]{1,0:T(8,128)(2,1)S(1)}, u32[]{:S(2)}, u32[]{:S(2)}) collective-permute-start(bf16[136,1024]{1,0:T(8,128)(2,1)S(1)} %get-tuple-element.29), channel_id=1, source_target_pairs={{0,4},{1,9},{4,0},{5,13},{8,12},{9,1},{12,8},{13,5},{2,6},{3,11},{... | collective-permute-start | bytes 835592 | tf_op jit(solution)/shard_map/ppermute | solution.py:40
  6.5 0.9 %slice-start = ((bf16[1024,512]{1,0:T(8,128)(2,1)}), bf16[128,512]{1,0:T(8,128)(2,1)S(1)}, s32[]{:S(2)}) async-start(bf16[1024,512]{1,0:T(8,128)(2,1)} %refs_0_.1), calls=%async_computation | async-start | bytes 262144 | tf_op jit(solution)/shard_map/slice | solution.py:326
  6.5 1.1 %copy-start.5 = (bf16[512,512]{1,0:T(8,128)(2,1)S(1)}, bf16[512,512]{1,0:T(8,128)(2,1)}, u32[]{:S(2)}) copy-start(bf16[512,512]{1,0:T(8,128)(2,1)} %refs_1_.1) | copy-start | bytes 1572868
  6.5 15.1 %copy-start.3 = (bf16[512,512]{1,0:T(8,128)(2,1)S(1)}, bf16[512,512]{1,0:T(8,128)(2,1)}, u32[]{:S(2)}) copy-start(bf16[512,512]{1,0:T(8,128)(2,1)} %w_key.3) | copy-start | bytes 1572868
  6.6 15.1 %copy-start.4 = (bf16[512,512]{1,0:T(8,128)(2,1)S(1)}, bf16[512,512]{1,0:T(8,128)(2,1)}, u32[]{:S(2)}) copy-start(bf16[512,512]{1,0:T(8,128)(2,1)} %w_value.3) | copy-start | bytes 1572868
  6.6 15.0 %copy-start = (bf16[512,1024]{1,0:T(8,128)(2,1)S(1)}, bf16[512,1024]{1,0:T(8,128)(2,1)}, u32[]{:S(2)}) copy-start(bf16[512,1024]{1,0:T(8,128)(2,1)} %w_up.3) | copy-start | bytes 3145732
  6.6 15.0 %copy-start.2 = (bf16[512,512]{1,0:T(8,128)(2,1)S(1)}, bf16[512,512]{1,0:T(8,128)(2,1)}, u32[]{:S(2)}) copy-start(bf16[512,512]{1,0:T(8,128)(2,1)} %w_query.3) | copy-start | bytes 1572868
  6.6 16.2 %collective-permute-start = (bf16[464,512]{1,0:T(8,128)(2,1)S(1)}, bf16[464,512]{1,0:T(8,128)(2,1)S(1)}, u32[]{:S(2)}, u32[]{:S(2)}) collective-permute-start(bf16[464,512]{1,0:T(8,128)(2,1)S(1)} %pad_maximum_fusion.1), channel_id=1, source_target_pairs={{0,2},{2,0},{1,3},{3,1},{4,6},{6,4},{5,7},{7,5},{8,10},{10,8},{9,1... | collective-permute-start | bytes 1425416 | tf_op jit(solution)/shard_map/ppermute | solution.py:31
  13.5 22.6 %collective-permute-start.2 = (bf16[640,512]{1,0:T(8,128)(2,1)S(1)}, bf16[640,512]{1,0:T(8,128)(2,1)S(1)}, u32[]{:S(2)}, u32[]{:S(2)}) collective-permute-start(bf16[640,512]{1,0:T(8,128)(2,1)S(1)} %pad_maximum_fusion), channel_id=1, source_target_pairs={{0,2},{2,0},{1,3},{3,1},{4,6},{6,4},{5,7},{7,5},{8,10},{10,8},{9,1... | collective-permute-start | bytes 1966088 | tf_op jit(solution)/shard_map/ppermute | solution.py:31
  14.0 11.0 %collective-permute-start.7 = (bf16[256,640]{1,0:T(8,128)(2,1)S(1)}, bf16[256,640]{1,0:T(8,128)(2,1)S(1)}, u32[]{:S(2)}, u32[]{:S(2)}) collective-permute-start(bf16[256,640]{1,0:T(8,128)(2,1)S(1)} %collective-permute-done.6.refs_6_), channel_id=1, source_target_pairs={{0,16},{16,0},{1,17},{17,1},{2,18},{18,2},{3,19},{19,3},{4,20},{20... | collective-permute-start | bytes 983048 | tf_op jit(solution)/shard_map/ppermute | solution.py:31
  15.5 6.1 %collective-permute-start.4 = (bf16[72,1024]{1,0:T(8,128)(2,1)S(1)}, bf16[72,1024]{1,0:T(8,128)(2,1)S(1)}, u32[]{:S(2)}, u32[]{:S(2)}) collective-permute-start(bf16[72,1024]{1,0:T(8,128)(2,1)S(1)} %split.1), channel_id=1, source_target_pairs={{0,8},{1,5},{4,12},{5,1},{8,0},{9,13},{12,4},{13,9},{2,10},{3,7},{... | collective-permute-start | bytes 442376 | tf_op jit(solution)/shard_map/ppermute | solution.py:40
  18.2 6.8 %collective-permute-start.3 = (bf16[136,1024]{1,0:T(8,128)(2,1)S(1)}, bf16[136,1024]{1,0:T(8,128)(2,1)S(1)}, u32[]{:S(2)}, u32[]{:S(2)}) collective-permute-start(bf16[136,1024]{1,0:T(8,128)(2,1)S(1)} %collective-permute-done.1.block.refs_1_), channel_id=1, source_target_pairs={{0,1},{1,0},{2,3},{3,2},{4,5},{5,4},{6,7},{7,6},{8,9},{9,8},{10,11... | collective-permute-start | bytes 835592 | tf_op jit(solution)/shard_map/ppermute | solution.py:31
  21.6 3.3 %collective-permute-start.5 = (bf16[72,1024]{1,0:T(8,128)(2,1)S(1)}, bf16[72,1024]{1,0:T(8,128)(2,1)S(1)}, u32[]{:S(2)}, u32[]{:S(2)}) collective-permute-start(bf16[72,1024]{1,0:T(8,128)(2,1)S(1)} %collective-permute-done.4.refs_3_), channel_id=1, source_target_pairs={{0,1},{1,0},{2,3},{3,2},{4,5},{5,4},{6,7},{7,6},{8,9},{9,8},{10,11... | collective-permute-start | bytes 442376 | tf_op jit(solution)/shard_map/ppermute | solution.py:31
  22.9 15.3 %collective-permute-start.8 = (bf16[464,512]{1,0:T(8,128)(2,1)S(1)}, bf16[464,512]{1,0:T(8,128)(2,1)S(1)}, u32[]{:S(2)}, u32[]{:S(2)}) collective-permute-start(bf16[464,512]{1,0:T(8,128)(2,1)S(1)} %collective-permute-done.received.refs_3_), channel_id=1, source_target_pairs={{0,16},{16,0},{1,17},{17,1},{2,18},{18,2},{3,19},{19,3},{4,20},{20... | collective-permute-start | bytes 1425416 | tf_op jit(solution)/shard_map/ppermute | solution.py:31
  26.1 10.0 %copy-start.8 = (f32[5,512]{1,0:T(8,128)S(1)}, f32[5,512]{1,0:T(8,128)}, u32[]{:S(2)}) copy-start(f32[5,512]{1,0:T(8,128)} %taps.1) | copy-start | bytes 30724
  27.2 10.4 %collective-permute-start.10 = (bf16[128,384]{1,0:T(8,128)(2,1)S(1)}, bf16[128,384]{1,0:T(8,128)(2,1)S(1)}, u32[]{:S(2)}, u32[]{:S(2)}) collective-permute-start(bf16[128,384]{1,0:T(8,128)(2,1)S(1)} %get-tuple-element.41), channel_id=1, source_target_pairs={{0,8},{4,12},{8,0},{12,4},{1,9},{5,13},{9,1},{13,5},{2,10},{6,14},... | collective-permute-start | bytes 294920 | tf_op jit(solution)/shard_map/ppermute | solution.py:31
  29.9 7.7 %collective-permute-start.11 = (bf16[128,384]{1,0:T(8,128)(2,1)S(1)}, bf16[128,384]{1,0:T(8,128)(2,1)S(1)}, u32[]{:S(2)}, u32[]{:S(2)}) collective-permute-start(bf16[128,384]{1,0:T(8,128)(2,1)S(1)} %get-tuple-element.42), channel_id=1, source_target_pairs={{0,12},{4,8},{8,4},{12,0},{1,13},{5,9},{9,5},{13,1},{2,14},{6,10},... | collective-permute-start | bytes 294920 | tf_op jit(solution)/shard_map/ppermute | solution.py:31
  32.0 6.1 %collective-permute-start.9 = (bf16[128,384]{1,0:T(8,128)(2,1)S(1)}, bf16[128,384]{1,0:T(8,128)(2,1)S(1)}, u32[]{:S(2)}, u32[]{:S(2)}) collective-permute-start(bf16[128,384]{1,0:T(8,128)(2,1)S(1)} %attend.4), channel_id=1, source_target_pairs={{0,4},{4,0},{8,12},{12,8},{1,5},{5,1},{9,13},{13,9},{2,6},{6,2},{1... | collective-permute-start | bytes 294920 | tf_op jit(solution)/shard_map/ppermute | solution.py:31
  38.8 1.4 %collective-permute-start.12 = (bf16[128,512]{1,0:T(8,128)(2,1)S(1)}, bf16[128,512]{1,0:T(8,128)(2,1)S(1)}, u32[]{:S(2)}, u32[]{:S(2)}) collective-permute-start(bf16[128,512]{1,0:T(8,128)(2,1)S(1)} %get-tuple-element.44), channel_id=1, source_target_pairs={{0,1},{1,0},{2,3},{3,2},{4,5},{5,4},{6,7},{7,6},{8,9},{9,8},{10,11... | collective-permute-start | bytes 393224 | tf_op jit(solution)/shard_map/ppermute | solution.py:31

commit v8 on v7

--- a/solution.py
+++ b/solution.py
@@ -243,6 +243,11 @@
     send[...] = jnp.where(same, far_sum, near_sum).astype(jnp.bfloat16)
 
 
+def finish_kernel(keep, other, out):
+    total = keep[...] + other[...].astype(jnp.float32)
+    out[...] = total.reshape(out.shape).astype(jnp.bfloat16)
+
+
 SMEM = pl.BlockSpec(memory_space=pltpu.SMEM)
 VMEM = pl.BlockSpec(memory_space=pltpu.VMEM)
 ANY = pl.BlockSpec(memory_space=pl.ANY)
@@ -385,8 +390,14 @@
         flops=4 * rows * columns * n_ctx * (hidden + wide),
         moved=4 << 20,
     )
-    other = across(send, "tp", 1).astype(f32)
-    return (keep + other).astype(bf16).reshape(frames_here, dancers_here, columns)
+    other = across(send, "tp", 1)
+    (denoised,) = call(
+        finish_kernel,
+        "finish",
+        [((frames_here, dancers_here, columns), bf16)],
+        [(VMEM, keep), (VMEM, other)],
+    )
+    return denoised
 
 
 def gather_all(

time: 41.1 us -> 41.1 us (level)
  Pallas kernels: 6.54 us -> 7.33 us
  local copies, waits for them, and re-layouts: 1.28 us -> 0.57 us
    pallas_call x10 -> x11, Pallas kernels: 6.54 us -> 7.33 us  [call(): pl.pallas_call(kernel, out_shape=[jax.ShapeDtypeStruct(shape, dtype) for...]
    reshape x1 -> x0, local copies, waits for them, and re-layouts: 0.71 us -> none  [split_over_ctx(): (keep + other).astype(bf16).reshape(frames_here, dancers_here, columns)]
where the time goes in v8:
time: 41.1 us; the launch traced here: 41 us
  starting transfers between devices  16.4 us (40%)
  waiting for transfers between devices  16.4 us (40%)
  Pallas kernels  7.33 us (18%)
  local copies, waits for them, and re-layouts  0.57 us (1%)
    ppermute x11, starting transfers between devices, across(): lax.ppermute(value, axis, [(source, source ^ step) for source in range(co...  12.1 us
    ppermute x2, waiting for transfers between devices, two_ways(): return lax.ppermute(value, ('ctx', 'tp'), pairs)  9.25 us
    pallas_call x11, Pallas kernels, call(): pl.pallas_call(kernel, out_shape=[jax.ShapeDtypeStruct(shape, dtype) for...  7.33 us
    ppermute x11, waiting for transfers between devices, across(): lax.ppermute(value, axis, [(source, source ^ step) for source in range(co...  7.16 us
    ppermute x2, starting transfers between devices, two_ways(): return lax.ppermute(value, ('ctx', 'tp'), pairs)  4.28 us
  transfers between devices with their start and end apart: 13, of which 7 were waited for; matrix products, arithmetic and copies ran while one was open for 1% of the time, Pallas kernels for 12%

profile of v8, /device:TPU:0, one launch (start us, length us, event | category | flops | bytes accessed | tf_op | source)
XLA Modules:
  0.0 41.0 jit_solution(7606432916634501078)
XLA Ops:
  0.0 1.1 %pack.1.after = bf16[256,640]{1,0:T(8,128)(2,1)S(1)} custom-call(bf16[512,1024]{1,0:T(8,128)(2,1)} %w_up.3, bf16[512,512]{1,0:T(8,128)(2,1)} %w_query.3, bf16[512,512]{1,0:T(8,128)(2,1)} %w_key.3, bf16[512,512]{1,0:T(8,128)(2,1)} %w_value.3), custom_call_target="tpu_custom_call" | custom-call | bytes 1048576 | tf_op jit(solution)/shard_map/pack/pallas_call | solution.py:260
  1.1 3.0 %collective-permute-start.6 = (bf16[256,640]{1,0:T(8,128)(2,1)S(1)}, bf16[256,640]{1,0:T(8,128)(2,1)S(1)}, u32[]{:S(2)}, u32[]{:S(2)}) collective-permute-start(bf16[256,640]{1,0:T(8,128)(2,1)S(1)} %pack.1.after), channel_id=1, source_target_pairs={{0,2},{2,0},{1,3},{3,1},{4,6},{6,4},{5,7},{7,5},{8,10},{10,8},{9,1... | collective-permute-start | bytes 983048 | tf_op jit(solution)/shard_map/ppermute | solution.py:31
  4.3 0.6 %normalise.1 = (bf16[136,1024]{1,0:T(8,128)(2,1)S(1)}, bf16[136,1024]{1,0:T(8,128)(2,1)S(1)}, bf16[128,512]{1,0:T(8,128)(2,1)S(1)}, bf16[16,512]{1,0:T(8,128)(2,1)S(1)}) custom-call(s32[1,4]{1,0:T(1,128)S(1)} %bitcast.3, bf16[128,1024]{1,0:T(8,128)(2,1)S(1)} %reshape.6.tokens, f32[1,1024]{1,0:T(1,128)S(1)} %bitcast.2), custom_call_target="tpu_custom_call" | custom-call | bytes 1048576 | tf_op jit(solution)/shard_map/normalise/pallas_call | solution.py:260
  4.9 1.6 %collective-permute-start.1 = (bf16[136,1024]{1,0:T(8,128)(2,1)S(1)}, bf16[136,1024]{1,0:T(8,128)(2,1)S(1)}, u32[]{:S(2)}, u32[]{:S(2)}) collective-permute-start(bf16[136,1024]{1,0:T(8,128)(2,1)S(1)} %get-tuple-element.29), channel_id=1, source_target_pairs={{0,4},{1,9},{4,0},{5,13},{8,12},{9,1},{12,8},{13,5},{2,6},{3,11},{... | collective-permute-start | bytes 835592 | tf_op jit(solution)/shard_map/ppermute | solution.py:40
  6.6 0.6 %collective-permute-start = (bf16[464,512]{1,0:T(8,128)(2,1)S(1)}, bf16[464,512]{1,0:T(8,128)(2,1)S(1)}, u32[]{:S(2)}, u32[]{:S(2)}) collective-permute-start(bf16[464,512]{1,0:T(8,128)(2,1)S(1)} %pad_maximum_fusion.1), channel_id=1, source_target_pairs={{0,2},{2,0},{1,3},{3,1},{4,6},{6,4},{5,7},{7,5},{8,10},{10,8},{9,1... | collective-permute-start | bytes 1425416 | tf_op jit(solution)/shard_map/ppermute | solution.py:31
  7.7 5.8 %collective-permute-done.1.block.refs_1_ = bf16[136,1024]{1,0:T(8,128)(2,1)S(1)} collective-permute-done((bf16[136,1024]{1,0:T(8,128)(2,1)S(1)}, bf16[136,1024]{1,0:T(8,128)(2,1)S(1)}, u32[]{:S(2)}, u32[]{:S(2)}) %collective-permute-start.1) | collective-permute-done | bytes 278560 | tf_op jit(solution)/shard_map/ppermute | solution.py:40
  13.5 0.5 %collective-permute-start.2 = (bf16[640,512]{1,0:T(8,128)(2,1)S(1)}, bf16[640,512]{1,0:T(8,128)(2,1)S(1)}, u32[]{:S(2)}, u32[]{:S(2)}) collective-permute-start(bf16[640,512]{1,0:T(8,128)(2,1)S(1)} %pad_maximum_fusion), channel_id=1, source_target_pairs={{0,2},{2,0},{1,3},{3,1},{4,6},{6,4},{5,7},{7,5},{8,10},{10,8},{9,1... | collective-permute-start | bytes 1966088 | tf_op jit(solution)/shard_map/ppermute | solution.py:31
  14.0 1.5 %collective-permute-start.7 = (bf16[256,640]{1,0:T(8,128)(2,1)S(1)}, bf16[256,640]{1,0:T(8,128)(2,1)S(1)}, u32[]{:S(2)}, u32[]{:S(2)}) collective-permute-start(bf16[256,640]{1,0:T(8,128)(2,1)S(1)} %collective-permute-done.6.refs_6_), channel_id=1, source_target_pairs={{0,16},{16,0},{1,17},{17,1},{2,18},{18,2},{3,19},{19,3},{4,20},{20... | collective-permute-start | bytes 983048 | tf_op jit(solution)/shard_map/ppermute | solution.py:31
  15.5 2.6 %collective-permute-start.4 = (bf16[72,1024]{1,0:T(8,128)(2,1)S(1)}, bf16[72,1024]{1,0:T(8,128)(2,1)S(1)}, u32[]{:S(2)}, u32[]{:S(2)}) collective-permute-start(bf16[72,1024]{1,0:T(8,128)(2,1)S(1)} %split.1), channel_id=1, source_target_pairs={{0,8},{1,5},{4,12},{5,1},{8,0},{9,13},{12,4},{13,9},{2,10},{3,7},{... | collective-permute-start | bytes 442376 | tf_op jit(solution)/shard_map/ppermute | solution.py:40
  18.2 3.5 %collective-permute-done.4.refs_3_ = bf16[72,1024]{1,0:T(8,128)(2,1)S(1)} collective-permute-done((bf16[72,1024]{1,0:T(8,128)(2,1)S(1)}, bf16[72,1024]{1,0:T(8,128)(2,1)S(1)}, u32[]{:S(2)}, u32[]{:S(2)}) %collective-permute-start.4) | collective-permute-done | bytes 147488 | tf_op jit(solution)/shard_map/ppermute | solution.py:40
  21.8 1.0 %collective-permute-done.received.refs_3_ = bf16[464,512]{1,0:T(8,128)(2,1)S(1)} collective-permute-done((bf16[464,512]{1,0:T(8,128)(2,1)S(1)}, bf16[464,512]{1,0:T(8,128)(2,1)S(1)}, u32[]{:S(2)}, u32[]{:S(2)}) %collective-permute-start) | collective-permute-done | bytes 475168 | tf_op jit(solution)/shard_map/ppermute | solution.py:31
  22.9 2.1 %collective-permute-start.8 = (bf16[464,512]{1,0:T(8,128)(2,1)S(1)}, bf16[464,512]{1,0:T(8,128)(2,1)S(1)}, u32[]{:S(2)}, u32[]{:S(2)}) collective-permute-start(bf16[464,512]{1,0:T(8,128)(2,1)S(1)} %collective-permute-done.received.refs_3_), channel_id=1, source_target_pairs={{0,16},{16,0},{1,17},{17,1},{2,18},{18,2},{3,19},{19,3},{4,20},{20... | collective-permute-start | bytes 1425416 | tf_op jit(solution)/shard_map/ppermute | solution.py:31
  25.0 1.1 %project.1 = (bf16[128,256]{1,0:T(8,128)(2,1)S(1)}, bf16[128,256]{1,0:T(8,128)(2,1)S(1)}, bf16[128,256]{1,0:T(8,128)(2,1)S(1)}, bf16[128,256]{1,0:T(8,128)(2,1)S...) custom-call(bf16[136,1024]{1,0:T(8,128)(2,1)S(1)} %get-tuple-element, ...), custom_call_target="tpu_custom_call" | custom-call | flops 671088640 | bytes 4194304 | tf_op jit(solution)/shard_map/project/pallas_call | solution.py:260
  26.1 1.1 %attend.5 = (bf16[128,384]{1,0:T(8,128)(2,1)S(1)}, bf16[128,384]{1,0:T(8,128)(2,1)S(1)}) custom-call(bf16[128,256]{1,0:T(8,128)(2,1)S(1)} %get-tuple-element.39.refs_0_, bf16[128,256]{1,0:T(8,128)(2,1)S(1)} %get-tuple-element.40.refs_1_, bf16[512,128]{1,0:T(8,128)(2,1)S(1)} %get-tuple-element.33.refs_1_.refs_2_, ...), custom_call_target="tpu_custom_call" | custom-call | flops 67108864 | bytes 1048576 | tf_op jit(solution)/shard_map/attend/pallas_call | solution.py:260
  27.2 2.7 %collective-permute-start.10 = (bf16[128,384]{1,0:T(8,128)(2,1)S(1)}, bf16[128,384]{1,0:T(8,128)(2,1)S(1)}, u32[]{:S(2)}, u32[]{:S(2)}) collective-permute-start(bf16[128,384]{1,0:T(8,128)(2,1)S(1)} %get-tuple-element.41), channel_id=1, source_target_pairs={{0,8},{4,12},{8,0},{12,4},{1,9},{5,13},{9,1},{13,5},{2,10},{6,14},... | collective-permute-start | bytes 294920 | tf_op jit(solution)/shard_map/ppermute | solution.py:31
  29.9 1.4 %collective-permute-start.11 = (bf16[128,384]{1,0:T(8,128)(2,1)S(1)}, bf16[128,384]{1,0:T(8,128)(2,1)S(1)}, u32[]{:S(2)}, u32[]{:S(2)}) collective-permute-start(bf16[128,384]{1,0:T(8,128)(2,1)S(1)} %get-tuple-element.42), channel_id=1, source_target_pairs={{0,12},{4,8},{8,4},{12,0},{1,13},{5,9},{9,5},{13,1},{2,14},{6,10},... | collective-permute-start | bytes 294920 | tf_op jit(solution)/shard_map/ppermute | solution.py:31
  31.2 0.8 %attend.4 = bf16[128,384]{1,0:T(8,128)(2,1)S(1)} custom-call(bf16[128,256]{1,0:T(8,128)(2,1)S(1)} %get-tuple-element.38.refs_0_, bf16[512,128]{1,0:T(8,128)(2,1)S(1)} %get-tuple-element.33.refs_1_.refs_2_, bf16[512,128]{1,0:T(8,128)(2,1)S(1)} %get-tuple-element.34.refs_2_.refs_3_, bf16[128,512]{1,0:T(8,128)(2,1)S(1)} %get-tuple-element.35.refs_3_.refs_4_, ...), custom_call_target="tpu_custom_call" | custom-call | flops 33554432 | bytes 1048576 | tf_op jit(solution)/shard_map/attend/pallas_call | solution.py:260
  32.3 0.8 %attend.3.last1.refs_6_ = bf16[128,384]{1,0:T(8,128)(2,1)S(1)} custom-call(bf16[128,256]{1,0:T(8,128)(2,1)S(1)} %get-tuple-element.32.refs_0_, bf16[512,128]{1,0:T(8,128)(2,1)S(1)} %get-tuple-element.33.refs_1_.refs_2_, bf16[512,128]{1,0:T(8,128)(2,1)S(1)} %get-tuple-element.34.refs_2_.refs_3_, bf16[128,512]{1,0:T(8,128)(2,1)S(1)} %get-tuple-element.35.refs_3_.refs_4_, ...), custom_call_target="tpu_custom_call" | custom-call | flops 33554432 | bytes 1048576 | tf_op jit(solution)/shard_map/attend/pallas_call | solution.py:260
  33.1 3.0 %collective-permute-done.2.last0.refs_5_ = bf16[640,512]{1,0:T(8,128)(2,1)S(1)} collective-permute-done((bf16[640,512]{1,0:T(8,128)(2,1)S(1)}, bf16[640,512]{1,0:T(8,128)(2,1)S(1)}, u32[]{:S(2)}, u32[]{:S(2)}) %collective-permute-start.2) | collective-permute-done | bytes 655392 | tf_op jit(solution)/shard_map/ppermute | solution.py:31
  36.4 1.2 %collective-permute-done.10.refs_8_ = bf16[128,384]{1,0:T(8,128)(2,1)S(1)} collective-permute-done((bf16[128,384]{1,0:T(8,128)(2,1)S(1)}, bf16[128,384]{1,0:T(8,128)(2,1)S(1)}, u32[]{:S(2)}, u32[]{:S(2)}) %collective-permute-start.10) | collective-permute-done | bytes 98336 | tf_op jit(solution)/shard_map/ppermute | solution.py:31
  37.6 0.5 %collective-permute-done.9.refs_7_ = bf16[128,384]{1,0:T(8,128)(2,1)S(1)} collective-permute-done((bf16[128,384]{1,0:T(8,128)(2,1)S(1)}, bf16[128,384]{1,0:T(8,128)(2,1)S(1)}, u32[]{:S(2)}, u32[]{:S(2)}) %collective-permute-start.9) | collective-permute-done | bytes 98336 | tf_op jit(solution)/shard_map/ppermute | solution.py:31
  38.1 0.6 %join.1 = (f32[128,512]{1,0:T(8,128)S(1)}, bf16[128,512]{1,0:T(8,128)(2,1)S(1)}) custom-call(bf16[1024,512]{1,0:T(8,128)(2,1)S(1)} %copy-done.1, bf16[512,512]{1,0:T(8,128)(2,1)S(1)} %copy-done.5, f32[128,512]{1,0:T(8,128)S(1)} %convolve.1.refs_2_, bf16[464,512]{1,0:T(8,128)(2,1)S(1)} %collective-permute-done.received.refs_3_, ...), custom_call_target="tpu_custom_call" | custom-call | flops 402653184 | bytes 4194304 | tf_op jit(solution)/shard_map/join/pallas_call | solution.py:260
  38.9 1.3 %collective-permute-done.12.other = bf16[128,512]{1,0:T(8,128)(2,1)S(1)} collective-permute-done((bf16[128,512]{1,0:T(8,128)(2,1)S(1)}, bf16[128,512]{1,0:T(8,128)(2,1)S(1)}, u32[]{:S(2)}, u32[]{:S(2)}) %collective-permute-start.12) | collective-permute-done | bytes 131104 | tf_op jit(solution)/shard_map/ppermute | solution.py:31
  40.2 0.8 %finish.1 = bf16[64,2,512]{2,1,0:T(2,128)(2,1)} custom-call(f32[128,512]{1,0:T(8,128)S(1)} %get-tuple-element.43.keep, bf16[128,512]{1,0:T(8,128)(2,1)S(1)} %collective-permute-done.12.other), custom_call_target="tpu_custom_call" | custom-call | bytes 1048576 | tf_op jit(solution)/shard_map/finish/pallas_call | solution.py:260
  (39 shorter events, 1.5 us)
Async XLA Ops:
  0.0 4.2 %copy-start.9 = (bf16[64,2,1024]{2,1,0:T(2,128)(2,1)S(1)}, bf16[64,2,1024]{2,1,0:T(2,128)(2,1)}, u32[]{:S(2)}) copy-start(bf16[64,2,1024]{2,1,0:T(2,128)(2,1)} %param.10) | copy-start | bytes 786436
  0.0 4.3 %copy-start.7 = (s32[1,1,4]{2,1,0:T(1,128)S(1)}, s32[1,1,4]{2,1,0:T(1,128)}, u32[]{:S(2)}) copy-start(s32[1,1,4]{2,1,0:T(1,128)} %param.12) | copy-start | bytes 52
  0.0 4.3 %copy-start.6 = (f32[1024]{0:T(1024)S(1)}, f32[1024]{0:T(1024)}, u32[]{:S(2)}) copy-start(f32[1024]{0:T(1024)} %param.11) | copy-start | bytes 12292
  0.0 6.5 %copy-start.1 = (bf16[1024,512]{1,0:T(8,128)(2,1)S(1)}, bf16[1024,512]{1,0:T(8,128)(2,1)}, u32[]{:S(2)}) copy-start(bf16[1024,512]{1,0:T(8,128)(2,1)} %refs_0_.1) | copy-start | bytes 3145732
  1.1 12.9 %collective-permute-start.6 = (bf16[256,640]{1,0:T(8,128)(2,1)S(1)}, bf16[256,640]{1,0:T(8,128)(2,1)S(1)}, u32[]{:S(2)}, u32[]{:S(2)}) collective-permute-start(bf16[256,640]{1,0:T(8,128)(2,1)S(1)} %pack.1.after), channel_id=1, source_target_pairs={{0,2},{2,0},{1,3},{3,1},{4,6},{6,4},{5,7},{7,5},{8,10},{10,8},{9,1... | collective-permute-start | bytes 983048 | tf_op jit(solution)/shard_map/ppermute | solution.py:31
  4.9 8.6 %collective-permute-start.1 = (bf16[136,1024]{1,0:T(8,128)(2,1)S(1)}, bf16[136,1024]{1,0:T(8,128)(2,1)S(1)}, u32[]{:S(2)}, u32[]{:S(2)}) collective-permute-start(bf16[136,1024]{1,0:T(8,128)(2,1)S(1)} %get-tuple-element.29), channel_id=1, source_target_pairs={{0,4},{1,9},{4,0},{5,13},{8,12},{9,1},{12,8},{13,5},{2,6},{3,11},{... | collective-permute-start | bytes 835592 | tf_op jit(solution)/shard_map/ppermute | solution.py:40
  6.5 0.9 %slice-start = ((bf16[1024,512]{1,0:T(8,128)(2,1)}), bf16[128,512]{1,0:T(8,128)(2,1)S(1)}, s32[]{:S(2)}) async-start(bf16[1024,512]{1,0:T(8,128)(2,1)} %refs_0_.1), calls=%async_computation | async-start | bytes 262144 | tf_op jit(solution)/shard_map/slice | solution.py:331
  6.5 1.1 %copy-start.5 = (bf16[512,512]{1,0:T(8,128)(2,1)S(1)}, bf16[512,512]{1,0:T(8,128)(2,1)}, u32[]{:S(2)}) copy-start(bf16[512,512]{1,0:T(8,128)(2,1)} %refs_1_.1) | copy-start | bytes 1572868
  6.5 15.1 %copy-start.3 = (bf16[512,512]{1,0:T(8,128)(2,1)S(1)}, bf16[512,512]{1,0:T(8,128)(2,1)}, u32[]{:S(2)}) copy-start(bf16[512,512]{1,0:T(8,128)(2,1)} %w_key.3) | copy-start | bytes 1572868
  6.6 15.1 %copy-start.4 = (bf16[512,512]{1,0:T(8,128)(2,1)S(1)}, bf16[512,512]{1,0:T(8,128)(2,1)}, u32[]{:S(2)}) copy-start(bf16[512,512]{1,0:T(8,128)(2,1)} %w_value.3) | copy-start | bytes 1572868
  6.6 15.0 %copy-start = (bf16[512,1024]{1,0:T(8,128)(2,1)S(1)}, bf16[512,1024]{1,0:T(8,128)(2,1)}, u32[]{:S(2)}) copy-start(bf16[512,1024]{1,0:T(8,128)(2,1)} %w_up.3) | copy-start | bytes 3145732
  6.6 15.0 %copy-start.2 = (bf16[512,512]{1,0:T(8,128)(2,1)S(1)}, bf16[512,512]{1,0:T(8,128)(2,1)}, u32[]{:S(2)}) copy-start(bf16[512,512]{1,0:T(8,128)(2,1)} %w_query.3) | copy-start | bytes 1572868
  6.6 16.2 %collective-permute-start = (bf16[464,512]{1,0:T(8,128)(2,1)S(1)}, bf16[464,512]{1,0:T(8,128)(2,1)S(1)}, u32[]{:S(2)}, u32[]{:S(2)}) collective-permute-start(bf16[464,512]{1,0:T(8,128)(2,1)S(1)} %pad_maximum_fusion.1), channel_id=1, source_target_pairs={{0,2},{2,0},{1,3},{3,1},{4,6},{6,4},{5,7},{7,5},{8,10},{10,8},{9,1... | collective-permute-start | bytes 1425416 | tf_op jit(solution)/shard_map/ppermute | solution.py:31
  13.5 22.6 %collective-permute-start.2 = (bf16[640,512]{1,0:T(8,128)(2,1)S(1)}, bf16[640,512]{1,0:T(8,128)(2,1)S(1)}, u32[]{:S(2)}, u32[]{:S(2)}) collective-permute-start(bf16[640,512]{1,0:T(8,128)(2,1)S(1)} %pad_maximum_fusion), channel_id=1, source_target_pairs={{0,2},{2,0},{1,3},{3,1},{4,6},{6,4},{5,7},{7,5},{8,10},{10,8},{9,1... | collective-permute-start | bytes 1966088 | tf_op jit(solution)/shard_map/ppermute | solution.py:31
  14.0 11.0 %collective-permute-start.7 = (bf16[256,640]{1,0:T(8,128)(2,1)S(1)}, bf16[256,640]{1,0:T(8,128)(2,1)S(1)}, u32[]{:S(2)}, u32[]{:S(2)}) collective-permute-start(bf16[256,640]{1,0:T(8,128)(2,1)S(1)} %collective-permute-done.6.refs_6_), channel_id=1, source_target_pairs={{0,16},{16,0},{1,17},{17,1},{2,18},{18,2},{3,19},{19,3},{4,20},{20... | collective-permute-start | bytes 983048 | tf_op jit(solution)/shard_map/ppermute | solution.py:31
  15.5 6.1 %collective-permute-start.4 = (bf16[72,1024]{1,0:T(8,128)(2,1)S(1)}, bf16[72,1024]{1,0:T(8,128)(2,1)S(1)}, u32[]{:S(2)}, u32[]{:S(2)}) collective-permute-start(bf16[72,1024]{1,0:T(8,128)(2,1)S(1)} %split.1), channel_id=1, source_target_pairs={{0,8},{1,5},{4,12},{5,1},{8,0},{9,13},{12,4},{13,9},{2,10},{3,7},{... | collective-permute-start | bytes 442376 | tf_op jit(solution)/shard_map/ppermute | solution.py:40
  18.2 6.8 %collective-permute-start.3 = (bf16[136,1024]{1,0:T(8,128)(2,1)S(1)}, bf16[136,1024]{1,0:T(8,128)(2,1)S(1)}, u32[]{:S(2)}, u32[]{:S(2)}) collective-permute-start(bf16[136,1024]{1,0:T(8,128)(2,1)S(1)} %collective-permute-done.1.block.refs_1_), channel_id=1, source_target_pairs={{0,1},{1,0},{2,3},{3,2},{4,5},{5,4},{6,7},{7,6},{8,9},{9,8},{10,11... | collective-permute-start | bytes 835592 | tf_op jit(solution)/shard_map/ppermute | solution.py:31
  21.6 3.3 %collective-permute-start.5 = (bf16[72,1024]{1,0:T(8,128)(2,1)S(1)}, bf16[72,1024]{1,0:T(8,128)(2,1)S(1)}, u32[]{:S(2)}, u32[]{:S(2)}) collective-permute-start(bf16[72,1024]{1,0:T(8,128)(2,1)S(1)} %collective-permute-done.4.refs_3_), channel_id=1, source_target_pairs={{0,1},{1,0},{2,3},{3,2},{4,5},{5,4},{6,7},{7,6},{8,9},{9,8},{10,11... | collective-permute-start | bytes 442376 | tf_op jit(solution)/shard_map/ppermute | solution.py:31
  22.9 15.3 %collective-permute-start.8 = (bf16[464,512]{1,0:T(8,128)(2,1)S(1)}, bf16[464,512]{1,0:T(8,128)(2,1)S(1)}, u32[]{:S(2)}, u32[]{:S(2)}) collective-permute-start(bf16[464,512]{1,0:T(8,128)(2,1)S(1)} %collective-permute-done.received.refs_3_), channel_id=1, source_target_pairs={{0,16},{16,0},{1,17},{17,1},{2,18},{18,2},{3,19},{19,3},{4,20},{20... | collective-permute-start | bytes 1425416 | tf_op jit(solution)/shard_map/ppermute | solution.py:31
  26.1 10.0 %copy-start.8 = (f32[5,512]{1,0:T(8,128)S(1)}, f32[5,512]{1,0:T(8,128)}, u32[]{:S(2)}) copy-start(f32[5,512]{1,0:T(8,128)} %taps.1) | copy-start | bytes 30724
  27.2 10.4 %collective-permute-start.10 = (bf16[128,384]{1,0:T(8,128)(2,1)S(1)}, bf16[128,384]{1,0:T(8,128)(2,1)S(1)}, u32[]{:S(2)}, u32[]{:S(2)}) collective-permute-start(bf16[128,384]{1,0:T(8,128)(2,1)S(1)} %get-tuple-element.41), channel_id=1, source_target_pairs={{0,8},{4,12},{8,0},{12,4},{1,9},{5,13},{9,1},{13,5},{2,10},{6,14},... | collective-permute-start | bytes 294920 | tf_op jit(solution)/shard_map/ppermute | solution.py:31
  29.9 7.7 %collective-permute-start.11 = (bf16[128,384]{1,0:T(8,128)(2,1)S(1)}, bf16[128,384]{1,0:T(8,128)(2,1)S(1)}, u32[]{:S(2)}, u32[]{:S(2)}) collective-permute-start(bf16[128,384]{1,0:T(8,128)(2,1)S(1)} %get-tuple-element.42), channel_id=1, source_target_pairs={{0,12},{4,8},{8,4},{12,0},{1,13},{5,9},{9,5},{13,1},{2,14},{6,10},... | collective-permute-start | bytes 294920 | tf_op jit(solution)/shard_map/ppermute | solution.py:31
  32.0 6.1 %collective-permute-start.9 = (bf16[128,384]{1,0:T(8,128)(2,1)S(1)}, bf16[128,384]{1,0:T(8,128)(2,1)S(1)}, u32[]{:S(2)}, u32[]{:S(2)}) collective-permute-start(bf16[128,384]{1,0:T(8,128)(2,1)S(1)} %attend.4), channel_id=1, source_target_pairs={{0,4},{4,0},{8,12},{12,8},{1,5},{5,1},{9,13},{13,9},{2,6},{6,2},{1... | collective-permute-start | bytes 294920 | tf_op jit(solution)/shard_map/ppermute | solution.py:31
  38.8 1.4 %collective-permute-start.12 = (bf16[128,512]{1,0:T(8,128)(2,1)S(1)}, bf16[128,512]{1,0:T(8,128)(2,1)S(1)}, u32[]{:S(2)}, u32[]{:S(2)}) collective-permute-start(bf16[128,512]{1,0:T(8,128)(2,1)S(1)} %get-tuple-element.44), channel_id=1, source_target_pairs={{0,1},{1,0},{2,3},{3,2},{4,5},{5,4},{6,7},{7,6},{8,9},{9,8},{10,11... | collective-permute-start | bytes 393224 | tf_op jit(solution)/shard_map/ppermute | solution.py:31

commit v9 on v8

--- a/solution.py
+++ b/solution.py
@@ -346,7 +346,7 @@
         transcendentals=n_ctx * rows * hidden,
     )
     parts = [None] * n_ctx
-    for blocks in ((2, 3), (1,), (0,)):
+    for blocks in ((2, 3, 1), (0,)):
         done = call(
             functools.partial(attend_kernel, n_ctx, blocks),
             "attend",

time: 41.1 us -> 41.1 us (level)
  waiting for transfers between devices: 16.4 us -> 16.9 us
    ppermute x11, waiting for transfers between devices: 7.16 us -> 7.61 us  [across(): lax.ppermute(value, axis, [(source, source ^ step) for source in range(co...]
    pallas_call x11 -> x10, Pallas kernels: 7.33 us -> 6.93 us  [call(): pl.pallas_call(kernel, out_shape=[jax.ShapeDtypeStruct(shape, dtype) for...]
  transfers between devices with their start and end apart: 13 -> 13, of which waited for: 7 -> 7; matrix products, arithmetic and copies ran while one was open for 1% -> 1% of each run, Pallas kernels for 12% -> 11%
where the time goes in v9:
time: 41.1 us; the launch traced here: 41 us
  waiting for transfers between devices  16.9 us (41%)
  starting transfers between devices  16.3 us (40%)
  Pallas kernels  6.93 us (17%)
  local copies, waits for them, and re-layouts  0.57 us (1%)
    ppermute x11, starting transfers between devices, across(): lax.ppermute(value, axis, [(source, source ^ step) for source in range(co...  12.1 us
    ppermute x2, waiting for transfers between devices, two_ways(): return lax.ppermute(value, ('ctx', 'tp'), pairs)  9.25 us
    ppermute x11, waiting for transfers between devices, across(): lax.ppermute(value, axis, [(source, source ^ step) for source in range(co...  7.61 us
    pallas_call x10, Pallas kernels, call(): pl.pallas_call(kernel, out_shape=[jax.ShapeDtypeStruct(shape, dtype) for...  6.93 us
    ppermute x2, starting transfers between devices, two_ways(): return lax.ppermute(value, ('ctx', 'tp'), pairs)  4.28 us
  transfers between devices with their start and end apart: 13, of which 7 were waited for; matrix products, arithmetic and copies ran while one was open for 1% of the time, Pallas kernels for 11%

profile of v9, /device:TPU:0, one launch (start us, length us, event | category | flops | bytes accessed | tf_op | source)
XLA Modules:
  0.0 41.0 jit_solution(6938285078972634644)
XLA Ops:
  0.0 1.1 %pack.1.after = bf16[256,640]{1,0:T(8,128)(2,1)S(1)} custom-call(bf16[512,1024]{1,0:T(8,128)(2,1)} %w_up.3, bf16[512,512]{1,0:T(8,128)(2,1)} %w_query.3, bf16[512,512]{1,0:T(8,128)(2,1)} %w_key.3, bf16[512,512]{1,0:T(8,128)(2,1)} %w_value.3), custom_call_target="tpu_custom_call" | custom-call | bytes 1048576 | tf_op jit(solution)/shard_map/pack/pallas_call | solution.py:260
  1.1 3.0 %collective-permute-start.6 = (bf16[256,640]{1,0:T(8,128)(2,1)S(1)}, bf16[256,640]{1,0:T(8,128)(2,1)S(1)}, u32[]{:S(2)}, u32[]{:S(2)}) collective-permute-start(bf16[256,640]{1,0:T(8,128)(2,1)S(1)} %pack.1.after), channel_id=1, source_target_pairs={{0,2},{2,0},{1,3},{3,1},{4,6},{6,4},{5,7},{7,5},{8,10},{10,8},{9,1... | collective-permute-start | bytes 983048 | tf_op jit(solution)/shard_map/ppermute | solution.py:31
  4.3 0.6 %normalise.1 = (bf16[136,1024]{1,0:T(8,128)(2,1)S(1)}, bf16[136,1024]{1,0:T(8,128)(2,1)S(1)}, bf16[128,512]{1,0:T(8,128)(2,1)S(1)}, bf16[16,512]{1,0:T(8,128)(2,1)S(1)}) custom-call(s32[1,4]{1,0:T(1,128)S(1)} %bitcast.3, bf16[128,1024]{1,0:T(8,128)(2,1)S(1)} %reshape.6.tokens, f32[1,1024]{1,0:T(1,128)S(1)} %bitcast.2), custom_call_target="tpu_custom_call" | custom-call | bytes 1048576 | tf_op jit(solution)/shard_map/normalise/pallas_call | solution.py:260
  4.9 1.6 %collective-permute-start.1 = (bf16[136,1024]{1,0:T(8,128)(2,1)S(1)}, bf16[136,1024]{1,0:T(8,128)(2,1)S(1)}, u32[]{:S(2)}, u32[]{:S(2)}) collective-permute-start(bf16[136,1024]{1,0:T(8,128)(2,1)S(1)} %get-tuple-element.30), channel_id=1, source_target_pairs={{0,4},{1,9},{4,0},{5,13},{8,12},{9,1},{12,8},{13,5},{2,6},{3,11},{... | collective-permute-start | bytes 835592 | tf_op jit(solution)/shard_map/ppermute | solution.py:40
  6.6 0.6 %collective-permute-start = (bf16[464,512]{1,0:T(8,128)(2,1)S(1)}, bf16[464,512]{1,0:T(8,128)(2,1)S(1)}, u32[]{:S(2)}, u32[]{:S(2)}) collective-permute-start(bf16[464,512]{1,0:T(8,128)(2,1)S(1)} %pad_maximum_fusion.1), channel_id=1, source_target_pairs={{0,2},{2,0},{1,3},{3,1},{4,6},{6,4},{5,7},{7,5},{8,10},{10,8},{9,1... | collective-permute-start | bytes 1425416 | tf_op jit(solution)/shard_map/ppermute | solution.py:31
  7.7 5.8 %collective-permute-done.1.block.refs_1_ = bf16[136,1024]{1,0:T(8,128)(2,1)S(1)} collective-permute-done((bf16[136,1024]{1,0:T(8,128)(2,1)S(1)}, bf16[136,1024]{1,0:T(8,128)(2,1)S(1)}, u32[]{:S(2)}, u32[]{:S(2)}) %collective-permute-start.1) | collective-permute-done | bytes 278560 | tf_op jit(solution)/shard_map/ppermute | solution.py:40
  13.5 0.5 %collective-permute-start.2 = (bf16[640,512]{1,0:T(8,128)(2,1)S(1)}, bf16[640,512]{1,0:T(8,128)(2,1)S(1)}, u32[]{:S(2)}, u32[]{:S(2)}) collective-permute-start(bf16[640,512]{1,0:T(8,128)(2,1)S(1)} %pad_maximum_fusion), channel_id=1, source_target_pairs={{0,2},{2,0},{1,3},{3,1},{4,6},{6,4},{5,7},{7,5},{8,10},{10,8},{9,1... | collective-permute-start | bytes 1966088 | tf_op jit(solution)/shard_map/ppermute | solution.py:31
  14.0 1.5 %collective-permute-start.7 = (bf16[256,640]{1,0:T(8,128)(2,1)S(1)}, bf16[256,640]{1,0:T(8,128)(2,1)S(1)}, u32[]{:S(2)}, u32[]{:S(2)}) collective-permute-start(bf16[256,640]{1,0:T(8,128)(2,1)S(1)} %collective-permute-done.6.refs_6_), channel_id=1, source_target_pairs={{0,16},{16,0},{1,17},{17,1},{2,18},{18,2},{3,19},{19,3},{4,20},{20... | collective-permute-start | bytes 983048 | tf_op jit(solution)/shard_map/ppermute | solution.py:31
  15.5 2.6 %collective-permute-start.4 = (bf16[72,1024]{1,0:T(8,128)(2,1)S(1)}, bf16[72,1024]{1,0:T(8,128)(2,1)S(1)}, u32[]{:S(2)}, u32[]{:S(2)}) collective-permute-start(bf16[72,1024]{1,0:T(8,128)(2,1)S(1)} %split.1), channel_id=1, source_target_pairs={{0,8},{1,5},{4,12},{5,1},{8,0},{9,13},{12,4},{13,9},{2,10},{3,7},{... | collective-permute-start | bytes 442376 | tf_op jit(solution)/shard_map/ppermute | solution.py:40
  18.2 3.5 %collective-permute-done.4.refs_3_ = bf16[72,1024]{1,0:T(8,128)(2,1)S(1)} collective-permute-done((bf16[72,1024]{1,0:T(8,128)(2,1)S(1)}, bf16[72,1024]{1,0:T(8,128)(2,1)S(1)}, u32[]{:S(2)}, u32[]{:S(2)}) %collective-permute-start.4) | collective-permute-done | bytes 147488 | tf_op jit(solution)/shard_map/ppermute | solution.py:40
  21.8 1.0 %collective-permute-done.received.refs_3_ = bf16[464,512]{1,0:T(8,128)(2,1)S(1)} collective-permute-done((bf16[464,512]{1,0:T(8,128)(2,1)S(1)}, bf16[464,512]{1,0:T(8,128)(2,1)S(1)}, u32[]{:S(2)}, u32[]{:S(2)}) %collective-permute-start) | collective-permute-done | bytes 475168 | tf_op jit(solution)/shard_map/ppermute | solution.py:31
  22.9 2.1 %collective-permute-start.8 = (bf16[464,512]{1,0:T(8,128)(2,1)S(1)}, bf16[464,512]{1,0:T(8,128)(2,1)S(1)}, u32[]{:S(2)}, u32[]{:S(2)}) collective-permute-start(bf16[464,512]{1,0:T(8,128)(2,1)S(1)} %collective-permute-done.received.refs_3_), channel_id=1, source_target_pairs={{0,16},{16,0},{1,17},{17,1},{2,18},{18,2},{3,19},{19,3},{4,20},{20... | collective-permute-start | bytes 1425416 | tf_op jit(solution)/shard_map/ppermute | solution.py:31
  25.0 1.1 %project.1 = (bf16[128,256]{1,0:T(8,128)(2,1)S(1)}, bf16[128,256]{1,0:T(8,128)(2,1)S(1)}, bf16[128,256]{1,0:T(8,128)(2,1)S(1)}, bf16[128,256]{1,0:T(8,128)(2,1)S...) custom-call(bf16[136,1024]{1,0:T(8,128)(2,1)S(1)} %get-tuple-element, ...), custom_call_target="tpu_custom_call" | custom-call | flops 671088640 | bytes 4194304 | tf_op jit(solution)/shard_map/project/pallas_call | solution.py:260
  26.1 1.5 %attend.3 = (bf16[128,384]{1,0:T(8,128)(2,1)S(1)}, bf16[128,384]{1,0:T(8,128)(2,1)S(1)}, bf16[128,384]{1,0:T(8,128)(2,1)S(1)}) custom-call(bf16[128,256]{1,0:T(8,128)(2,1)S(1)} %get-tuple-element.39.refs_0_, bf16[128,256]{1,0:T(8,128)(2,1)S(1)} %get-tuple-element.40.refs_1_, bf16[128,256]{1,0:T(8,128)(2,1)S(1)} %get-tuple-element.41.refs_2_, ...), custom_call_target="tpu_custom_call" | custom-call | flops 100663296 | bytes 1048576 | tf_op jit(solution)/shard_map/attend/pallas_call | solution.py:260
  27.6 2.7 %collective-permute-start.10 = (bf16[128,384]{1,0:T(8,128)(2,1)S(1)}, bf16[128,384]{1,0:T(8,128)(2,1)S(1)}, u32[]{:S(2)}, u32[]{:S(2)}) collective-permute-start(bf16[128,384]{1,0:T(8,128)(2,1)S(1)} %get-tuple-element.43), channel_id=1, source_target_pairs={{0,8},{4,12},{8,0},{12,4},{1,9},{5,13},{9,1},{13,5},{2,10},{6,14},... | collective-permute-start | bytes 294920 | tf_op jit(solution)/shard_map/ppermute | solution.py:31
  30.2 1.4 %collective-permute-start.11 = (bf16[128,384]{1,0:T(8,128)(2,1)S(1)}, bf16[128,384]{1,0:T(8,128)(2,1)S(1)}, u32[]{:S(2)}, u32[]{:S(2)}) collective-permute-start(bf16[128,384]{1,0:T(8,128)(2,1)S(1)} %get-tuple-element.44), channel_id=1, source_target_pairs={{0,12},{4,8},{8,4},{12,0},{1,13},{5,9},{9,5},{13,1},{2,14},{6,10},... | collective-permute-start | bytes 294920 | tf_op jit(solution)/shard_map/ppermute | solution.py:31
  31.6 0.2 collective-permute-start.9
  31.8 0.8 %attend.2.last1.refs_6_ = bf16[128,384]{1,0:T(8,128)(2,1)S(1)} custom-call(bf16[128,256]{1,0:T(8,128)(2,1)S(1)} %get-tuple-element.33.refs_0_, bf16[512,128]{1,0:T(8,128)(2,1)S(1)} %get-tuple-element.34.refs_1_.refs_3_, bf16[512,128]{1,0:T(8,128)(2,1)S(1)} %get-tuple-element.35.refs_2_.refs_4_, bf16[128,512]{1,0:T(8,128)(2,1)S(1)} %get-tuple-element.36.refs_3_.refs_5_, ...), custom_call_target="tpu_custom_call" | custom-call | flops 33554432 | bytes 1048576 | tf_op jit(solution)/shard_map/attend/pallas_call | solution.py:260
  32.6 3.5 %collective-permute-done.2.last0.refs_5_ = bf16[640,512]{1,0:T(8,128)(2,1)S(1)} collective-permute-done((bf16[640,512]{1,0:T(8,128)(2,1)S(1)}, bf16[640,512]{1,0:T(8,128)(2,1)S(1)}, u32[]{:S(2)}, u32[]{:S(2)}) %collective-permute-start.2) | collective-permute-done | bytes 655392 | tf_op jit(solution)/shard_map/ppermute | solution.py:31
  36.1 0.3 convolve.1.refs_2_
  36.4 1.6 %collective-permute-done.10.refs_8_ = bf16[128,384]{1,0:T(8,128)(2,1)S(1)} collective-permute-done((bf16[128,384]{1,0:T(8,128)(2,1)S(1)}, bf16[128,384]{1,0:T(8,128)(2,1)S(1)}, u32[]{:S(2)}, u32[]{:S(2)}) %collective-permute-start.10) | collective-permute-done | bytes 98336 | tf_op jit(solution)/shard_map/ppermute | solution.py:31
  38.1 0.6 %join.1 = (f32[128,512]{1,0:T(8,128)S(1)}, bf16[128,512]{1,0:T(8,128)(2,1)S(1)}) custom-call(bf16[1024,512]{1,0:T(8,128)(2,1)S(1)} %copy-done.1, bf16[512,512]{1,0:T(8,128)(2,1)S(1)} %copy-done.5, f32[128,512]{1,0:T(8,128)S(1)} %convolve.1.refs_2_, bf16[464,512]{1,0:T(8,128)(2,1)S(1)} %collective-permute-done.received.refs_3_, ...), custom_call_target="tpu_custom_call" | custom-call | flops 402653184 | bytes 4194304 | tf_op jit(solution)/shard_map/join/pallas_call | solution.py:260
  38.8 1.3 %collective-permute-done.12.other = bf16[128,512]{1,0:T(8,128)(2,1)S(1)} collective-permute-done((bf16[128,512]{1,0:T(8,128)(2,1)S(1)}, bf16[128,512]{1,0:T(8,128)(2,1)S(1)}, u32[]{:S(2)}, u32[]{:S(2)}) %collective-permute-start.12) | collective-permute-done | bytes 131104 | tf_op jit(solution)/shard_map/ppermute | solution.py:31
  40.2 0.8 %finish.1 = bf16[64,2,512]{2,1,0:T(2,128)(2,1)} custom-call(f32[128,512]{1,0:T(8,128)S(1)} %get-tuple-element.45.keep, bf16[128,512]{1,0:T(8,128)(2,1)S(1)} %collective-permute-done.12.other), custom_call_target="tpu_custom_call" | custom-call | bytes 1048576 | tf_op jit(solution)/shard_map/finish/pallas_call | solution.py:260
  (38 shorter events, 1.0 us)
Async XLA Ops:
  0.0 4.2 %copy-start.9 = (bf16[64,2,1024]{2,1,0:T(2,128)(2,1)S(1)}, bf16[64,2,1024]{2,1,0:T(2,128)(2,1)}, u32[]{:S(2)}) copy-start(bf16[64,2,1024]{2,1,0:T(2,128)(2,1)} %param.10) | copy-start | bytes 786436
  0.0 4.3 %copy-start.7 = (s32[1,1,4]{2,1,0:T(1,128)S(1)}, s32[1,1,4]{2,1,0:T(1,128)}, u32[]{:S(2)}) copy-start(s32[1,1,4]{2,1,0:T(1,128)} %param.12) | copy-start | bytes 52
  0.0 4.3 %copy-start.6 = (f32[1024]{0:T(1024)S(1)}, f32[1024]{0:T(1024)}, u32[]{:S(2)}) copy-start(f32[1024]{0:T(1024)} %param.11) | copy-start | bytes 12292
  0.0 6.5 %copy-start.1 = (bf16[1024,512]{1,0:T(8,128)(2,1)S(1)}, bf16[1024,512]{1,0:T(8,128)(2,1)}, u32[]{:S(2)}) copy-start(bf16[1024,512]{1,0:T(8,128)(2,1)} %refs_0_.1) | copy-start | bytes 3145732
  1.1 12.9 %collective-permute-start.6 = (bf16[256,640]{1,0:T(8,128)(2,1)S(1)}, bf16[256,640]{1,0:T(8,128)(2,1)S(1)}, u32[]{:S(2)}, u32[]{:S(2)}) collective-permute-start(bf16[256,640]{1,0:T(8,128)(2,1)S(1)} %pack.1.after), channel_id=1, source_target_pairs={{0,2},{2,0},{1,3},{3,1},{4,6},{6,4},{5,7},{7,5},{8,10},{10,8},{9,1... | collective-permute-start | bytes 983048 | tf_op jit(solution)/shard_map/ppermute | solution.py:31
  4.9 8.6 %collective-permute-start.1 = (bf16[136,1024]{1,0:T(8,128)(2,1)S(1)}, bf16[136,1024]{1,0:T(8,128)(2,1)S(1)}, u32[]{:S(2)}, u32[]{:S(2)}) collective-permute-start(bf16[136,1024]{1,0:T(8,128)(2,1)S(1)} %get-tuple-element.30), channel_id=1, source_target_pairs={{0,4},{1,9},{4,0},{5,13},{8,12},{9,1},{12,8},{13,5},{2,6},{3,11},{... | collective-permute-start | bytes 835592 | tf_op jit(solution)/shard_map/ppermute | solution.py:40
  6.5 0.9 %slice-start = ((bf16[1024,512]{1,0:T(8,128)(2,1)}), bf16[128,512]{1,0:T(8,128)(2,1)S(1)}, s32[]{:S(2)}) async-start(bf16[1024,512]{1,0:T(8,128)(2,1)} %refs_0_.1), calls=%async_computation | async-start | bytes 262144 | tf_op jit(solution)/shard_map/slice | solution.py:331
  6.5 1.1 %copy-start.5 = (bf16[512,512]{1,0:T(8,128)(2,1)S(1)}, bf16[512,512]{1,0:T(8,128)(2,1)}, u32[]{:S(2)}) copy-start(bf16[512,512]{1,0:T(8,128)(2,1)} %refs_1_.1) | copy-start | bytes 1572868
  6.5 15.1 %copy-start.3 = (bf16[512,512]{1,0:T(8,128)(2,1)S(1)}, bf16[512,512]{1,0:T(8,128)(2,1)}, u32[]{:S(2)}) copy-start(bf16[512,512]{1,0:T(8,128)(2,1)} %w_key.3) | copy-start | bytes 1572868
  6.6 15.1 %copy-start.4 = (bf16[512,512]{1,0:T(8,128)(2,1)S(1)}, bf16[512,512]{1,0:T(8,128)(2,1)}, u32[]{:S(2)}) copy-start(bf16[512,512]{1,0:T(8,128)(2,1)} %w_value.3) | copy-start | bytes 1572868
  6.6 15.0 %copy-start = (bf16[512,1024]{1,0:T(8,128)(2,1)S(1)}, bf16[512,1024]{1,0:T(8,128)(2,1)}, u32[]{:S(2)}) copy-start(bf16[512,1024]{1,0:T(8,128)(2,1)} %w_up.3) | copy-start | bytes 3145732
  6.6 15.0 %copy-start.2 = (bf16[512,512]{1,0:T(8,128)(2,1)S(1)}, bf16[512,512]{1,0:T(8,128)(2,1)}, u32[]{:S(2)}) copy-start(bf16[512,512]{1,0:T(8,128)(2,1)} %w_query.3) | copy-start | bytes 1572868
  6.6 16.2 %collective-permute-start = (bf16[464,512]{1,0:T(8,128)(2,1)S(1)}, bf16[464,512]{1,0:T(8,128)(2,1)S(1)}, u32[]{:S(2)}, u32[]{:S(2)}) collective-permute-start(bf16[464,512]{1,0:T(8,128)(2,1)S(1)} %pad_maximum_fusion.1), channel_id=1, source_target_pairs={{0,2},{2,0},{1,3},{3,1},{4,6},{6,4},{5,7},{7,5},{8,10},{10,8},{9,1... | collective-permute-start | bytes 1425416 | tf_op jit(solution)/shard_map/ppermute | solution.py:31
  13.5 22.6 %collective-permute-start.2 = (bf16[640,512]{1,0:T(8,128)(2,1)S(1)}, bf16[640,512]{1,0:T(8,128)(2,1)S(1)}, u32[]{:S(2)}, u32[]{:S(2)}) collective-permute-start(bf16[640,512]{1,0:T(8,128)(2,1)S(1)} %pad_maximum_fusion), channel_id=1, source_target_pairs={{0,2},{2,0},{1,3},{3,1},{4,6},{6,4},{5,7},{7,5},{8,10},{10,8},{9,1... | collective-permute-start | bytes 1966088 | tf_op jit(solution)/shard_map/ppermute | solution.py:31
  14.0 11.0 %collective-permute-start.7 = (bf16[256,640]{1,0:T(8,128)(2,1)S(1)}, bf16[256,640]{1,0:T(8,128)(2,1)S(1)}, u32[]{:S(2)}, u32[]{:S(2)}) collective-permute-start(bf16[256,640]{1,0:T(8,128)(2,1)S(1)} %collective-permute-done.6.refs_6_), channel_id=1, source_target_pairs={{0,16},{16,0},{1,17},{17,1},{2,18},{18,2},{3,19},{19,3},{4,20},{20... | collective-permute-start | bytes 983048 | tf_op jit(solution)/shard_map/ppermute | solution.py:31
  15.5 6.1 %collective-permute-start.4 = (bf16[72,1024]{1,0:T(8,128)(2,1)S(1)}, bf16[72,1024]{1,0:T(8,128)(2,1)S(1)}, u32[]{:S(2)}, u32[]{:S(2)}) collective-permute-start(bf16[72,1024]{1,0:T(8,128)(2,1)S(1)} %split.1), channel_id=1, source_target_pairs={{0,8},{1,5},{4,12},{5,1},{8,0},{9,13},{12,4},{13,9},{2,10},{3,7},{... | collective-permute-start | bytes 442376 | tf_op jit(solution)/shard_map/ppermute | solution.py:40
  18.2 6.8 %collective-permute-start.3 = (bf16[136,1024]{1,0:T(8,128)(2,1)S(1)}, bf16[136,1024]{1,0:T(8,128)(2,1)S(1)}, u32[]{:S(2)}, u32[]{:S(2)}) collective-permute-start(bf16[136,1024]{1,0:T(8,128)(2,1)S(1)} %collective-permute-done.1.block.refs_1_), channel_id=1, source_target_pairs={{0,1},{1,0},{2,3},{3,2},{4,5},{5,4},{6,7},{7,6},{8,9},{9,8},{10,11... | collective-permute-start | bytes 835592 | tf_op jit(solution)/shard_map/ppermute | solution.py:31
  21.6 3.3 %collective-permute-start.5 = (bf16[72,1024]{1,0:T(8,128)(2,1)S(1)}, bf16[72,1024]{1,0:T(8,128)(2,1)S(1)}, u32[]{:S(2)}, u32[]{:S(2)}) collective-permute-start(bf16[72,1024]{1,0:T(8,128)(2,1)S(1)} %collective-permute-done.4.refs_3_), channel_id=1, source_target_pairs={{0,1},{1,0},{2,3},{3,2},{4,5},{5,4},{6,7},{7,6},{8,9},{9,8},{10,11... | collective-permute-start | bytes 442376 | tf_op jit(solution)/shard_map/ppermute | solution.py:31
  22.9 15.2 %collective-permute-start.8 = (bf16[464,512]{1,0:T(8,128)(2,1)S(1)}, bf16[464,512]{1,0:T(8,128)(2,1)S(1)}, u32[]{:S(2)}, u32[]{:S(2)}) collective-permute-start(bf16[464,512]{1,0:T(8,128)(2,1)S(1)} %collective-permute-done.received.refs_3_), channel_id=1, source_target_pairs={{0,16},{16,0},{1,17},{17,1},{2,18},{18,2},{3,19},{19,3},{4,20},{20... | collective-permute-start | bytes 1425416 | tf_op jit(solution)/shard_map/ppermute | solution.py:31
  26.1 10.0 %copy-start.8 = (f32[5,512]{1,0:T(8,128)S(1)}, f32[5,512]{1,0:T(8,128)}, u32[]{:S(2)}) copy-start(f32[5,512]{1,0:T(8,128)} %taps.1) | copy-start | bytes 30724
  27.6 10.4 %collective-permute-start.10 = (bf16[128,384]{1,0:T(8,128)(2,1)S(1)}, bf16[128,384]{1,0:T(8,128)(2,1)S(1)}, u32[]{:S(2)}, u32[]{:S(2)}) collective-permute-start(bf16[128,384]{1,0:T(8,128)(2,1)S(1)} %get-tuple-element.43), channel_id=1, source_target_pairs={{0,8},{4,12},{8,0},{12,4},{1,9},{5,13},{9,1},{13,5},{2,10},{6,14},... | collective-permute-start | bytes 294920 | tf_op jit(solution)/shard_map/ppermute | solution.py:31
  30.2 7.7 %collective-permute-start.11 = (bf16[128,384]{1,0:T(8,128)(2,1)S(1)}, bf16[128,384]{1,0:T(8,128)(2,1)S(1)}, u32[]{:S(2)}, u32[]{:S(2)}) collective-permute-start(bf16[128,384]{1,0:T(8,128)(2,1)S(1)} %get-tuple-element.44), channel_id=1, source_target_pairs={{0,12},{4,8},{8,4},{12,0},{1,13},{5,9},{9,5},{13,1},{2,14},{6,10},... | collective-permute-start | bytes 294920 | tf_op jit(solution)/shard_map/ppermute | solution.py:31
  31.6 6.5 %collective-permute-start.9 = (bf16[128,384]{1,0:T(8,128)(2,1)S(1)}, bf16[128,384]{1,0:T(8,128)(2,1)S(1)}, u32[]{:S(2)}, u32[]{:S(2)}) collective-permute-start(bf16[128,384]{1,0:T(8,128)(2,1)S(1)} %get-tuple-element.42), channel_id=1, source_target_pairs={{0,4},{4,0},{8,12},{12,8},{1,5},{5,1},{9,13},{13,9},{2,6},{6,2},{1... | collective-permute-start | bytes 294920 | tf_op jit(solution)/shard_map/ppermute | solution.py:31
  38.8 1.4 %collective-permute-start.12 = (bf16[128,512]{1,0:T(8,128)(2,1)S(1)}, bf16[128,512]{1,0:T(8,128)(2,1)S(1)}, u32[]{:S(2)}, u32[]{:S(2)}) collective-permute-start(bf16[128,512]{1,0:T(8,128)(2,1)S(1)} %get-tuple-element.46), channel_id=1, source_target_pairs={{0,1},{1,0},{2,3},{3,2},{4,5},{5,4},{6,7},{7,6},{8,9},{9,8},{10,11... | collective-permute-start | bytes 393224 | tf_op jit(solution)/shard_map/ppermute | solution.py:31
